TPU v7x, 128 devices: a whole 4x4x4 slice. The times are simulated.
128 devices in a mesh: row: 16 (over x_lo, y, core), col: 8 (over z, x_hi).
Axes of the slice: x: 4 (x_hi: 2, x_lo: 2; x = x_hi * 2 + x_lo), y: 4, z: 4, core: 2. Of those that a mesh axis runs over, the one named last changes fastest.
Arguments:
- pair: bfloat16 [512, 512, 128], P('row', 'col'), may hold values from -6 to 6
- mask: int32 [512], replicated, may hold values 0 or 1
- tri_in: bfloat16 [128, 640], replicated, may hold values from -0.5 to 0.5
- tri_out: bfloat16 [128, 128], replicated, may hold values from -0.5 to 0.5
- start_in: bfloat16 [128, 512], replicated, may hold values from -0.5 to 0.5
- start_bias: bfloat16 [128, 4], replicated, may hold values from -30 to 30
- start_out: bfloat16 [128, 128], replicated, may hold values from -0.5 to 0.5
- end_in: bfloat16 [128, 512], replicated, may hold values from -0.5 to 0.5
- end_bias: bfloat16 [128, 4], replicated, may hold values from -30 to 30
- end_out: bfloat16 [128, 128], replicated, may hold values from -0.5 to 0.5
Outputs:
- pair_out: bfloat16 [512, 512, 128], P('row', 'col')
All inputs are finite; a program needn't handle non-finite values.
Results may differ from a plain program's by a relative error of at most 0.035.
The roundings to bfloat16 on the way count: a program that leaves them out, or rounds other values in their place, can miss the bound.
Values may be sent and summed in bfloat16 or wider, within the bound.
No kernel may reach another device: no remote copies, remote signals or barrier semaphores. Data moves between devices by JAX's collectives and lax.ppermute only.
A program may use at most 128 MiB of HBM per device.

v0:
```python
import jax
import jax.numpy as jnp
from jax import lax
from jax.sharding import PartitionSpec as P

epsilon = 1e-05


def layer_norm(values_in):
    average = jnp.mean(values_in, axis=-1, keepdims=True)
    centred = values_in - average
    variance = jnp.mean(centred * centred, axis=-1, keepdims=True)
    return centred * lax.rsqrt(variance + epsilon)


def softmax_attend(query_blocks, key_blocks, value_blocks, bias_block, mask_bias):
    scores = jnp.einsum(
        "bhqd,bhkd->bhqk", query_blocks, key_blocks, preferred_element_type=jnp.float32
    )
    scores = scores + bias_block[None] + mask_bias
    largest = jnp.max(scores, axis=-1, keepdims=True)
    exponent = jnp.exp(scores - largest)
    weights = (exponent / jnp.sum(exponent, axis=-1, keepdims=True)).astype(jnp.bfloat16)
    return jnp.einsum("bhqk,bhkd->bhqd", weights, value_blocks, preferred_element_type=jnp.float32)


def project_heads(pair_now, weights_in, weights_bias):
    row_count, col_count, channels = pair_now.shape
    head_width = channels // weights_bias.shape[1]
    pair_float = pair_now.astype(jnp.float32)
    normed = layer_norm(pair_float).astype(jnp.bfloat16)
    flat_rows = normed.reshape(row_count * col_count, channels)
    projected = jnp.dot(flat_rows, weights_in, preferred_element_type=jnp.float32).reshape(
        row_count, col_count, 4 * channels
    )
    query_heads = (projected[..., :channels] * head_width ** (-0.5)).astype(jnp.bfloat16)
    key_heads = projected[..., channels : 2 * channels].astype(jnp.bfloat16)
    value_heads = projected[..., 2 * channels : 3 * channels].astype(jnp.bfloat16)
    gating = jax.nn.sigmoid(projected[..., 3 * channels :])
    bias_terms = jnp.dot(flat_rows, weights_bias, preferred_element_type=jnp.float32)
    bias_terms = bias_terms.reshape(row_count, col_count, -1).transpose(2, 0, 1)
    return (pair_float, query_heads, key_heads, value_heads, gating, bias_terms)


def finish(pair_float, attended, gating, weights_out):
    channels = pair_float.shape[2]
    gated_out = (attended * gating).astype(jnp.bfloat16)
    update = jnp.dot(
        gated_out.reshape(-1, channels), weights_out, preferred_element_type=jnp.float32
    )
    return (pair_float + update.reshape(pair_float.shape)).astype(jnp.bfloat16)


def body(pair, mask, tri_in, tri_out, start_in, start_bias, start_out, end_in, end_bias, end_out):
    row_count, col_count, channels = pair.shape
    head_count = start_bias.shape[1]
    head_width = channels // head_count
    total_len = mask.shape[0]
    row_place = lax.axis_index("row")
    col_place = lax.axis_index("col")
    mask_float = mask.astype(jnp.float32)
    row_mask = lax.dynamic_slice_in_dim(mask_float, row_place * row_count, row_count)
    col_mask = lax.dynamic_slice_in_dim(mask_float, col_place * col_count, col_count)
    mask_bias = (mask_float - 1.0) * 1000000000.0
    pair_float = pair.astype(jnp.float32)
    normed = layer_norm(pair_float).astype(jnp.bfloat16)
    projected = jnp.dot(normed.reshape(-1, channels), tri_in, preferred_element_type=jnp.float32)
    projected = projected.reshape(row_count, col_count, 5 * channels)
    pair_mask = row_mask[:, None, None] * col_mask[None, :, None]
    left_terms = (
        jax.nn.sigmoid(projected[..., :channels])
        * projected[..., channels : 2 * channels]
        * pair_mask
    ).astype(jnp.bfloat16)
    right_terms = (
        jax.nn.sigmoid(projected[..., 2 * channels : 3 * channels])
        * projected[..., 3 * channels : 4 * channels]
        * pair_mask
    ).astype(jnp.bfloat16)
    gating = jax.nn.sigmoid(projected[..., 4 * channels :])
    right_cols = lax.all_gather(right_terms, "row", axis=0, tiled=True)
    combined = lax.psum_scatter(
        jnp.einsum("ikc,jkc->jic", left_terms, right_cols, preferred_element_type=jnp.float32),
        "col",
        scatter_dimension=0,
        tiled=True,
    ).transpose(1, 0, 2)
    mixed_norm = layer_norm(combined).astype(jnp.bfloat16)
    update = jnp.dot(mixed_norm.reshape(-1, channels), tri_out, preferred_element_type=jnp.float32)
    pair_one = (pair_float + gating * update.reshape(row_count, col_count, channels)).astype(
        jnp.bfloat16
    )
    pair_float, query_heads, key_heads, value_heads, gating, bias_terms = project_heads(
        pair_one, start_in, start_bias
    )
    bias_strip = lax.all_gather(bias_terms, "col", axis=2, tiled=True)
    bias_all = lax.all_gather(bias_strip, "row", axis=1, tiled=True)
    bias_block = lax.dynamic_slice_in_dim(bias_all, col_place * col_count, col_count, 1)
    keys_rows, values_rows = (
        lax.all_gather(key_heads, "col", axis=1, tiled=True),
        lax.all_gather(value_heads, "col", axis=1, tiled=True),
    )
    query_blocks = query_heads.reshape(row_count, col_count, head_count, head_width).transpose(
        0, 2, 1, 3
    )
    key_blocks = keys_rows.reshape(row_count, total_len, head_count, head_width).transpose(
        0, 2, 1, 3
    )
    value_blocks = values_rows.reshape(row_count, total_len, head_count, head_width).transpose(
        0, 2, 1, 3
    )
    attended = softmax_attend(query_blocks, key_blocks, value_blocks, bias_block, mask_bias)
    attended = attended.transpose(0, 2, 1, 3).reshape(row_count, col_count, channels)
    pair_two = finish(pair_float, attended, gating, start_out)
    pair_float, query_heads, key_heads, value_heads, gating, bias_terms = project_heads(
        pair_two, end_in, end_bias
    )
    bias_cols = lax.all_gather(bias_terms, "row", axis=1, tiled=True)
    bias_all = lax.all_gather(bias_cols, "col", axis=2, tiled=True)
    bias_block = lax.dynamic_slice_in_dim(bias_all, row_place * row_count, row_count, 2)
    bias_block = bias_block.transpose(0, 2, 1)
    keys_cols, values_cols = (
        lax.all_gather(key_heads, "row", axis=0, tiled=True),
        lax.all_gather(value_heads, "row", axis=0, tiled=True),
    )
    query_blocks = query_heads.reshape(row_count, col_count, head_count, head_width).transpose(
        1, 2, 0, 3
    )
    key_blocks = keys_cols.reshape(total_len, col_count, head_count, head_width).transpose(
        1, 2, 0, 3
    )
    value_blocks = values_cols.reshape(total_len, col_count, head_count, head_width).transpose(
        1, 2, 0, 3
    )
    attended = softmax_attend(query_blocks, key_blocks, value_blocks, bias_block, mask_bias)
    attended = attended.transpose(2, 0, 1, 3).reshape(row_count, col_count, channels)
    return finish(pair_float, attended, gating, end_out)


def solution(mesh):
    in_specs = (P("row", "col", None), P(), P(), P(), P(), P(), P(), P(), P(), P())
    out_specs = P("row", "col", None)
    return jax.shard_map(body, mesh=mesh, in_specs=in_specs, out_specs=out_specs, check_vma=False)
```

profile of v0, /device:TPU:1, one launch (start us, length us, event | category | flops | bytes accessed | tf_op | source)
XLA Modules:
  0.0 693.7 jit_solution(18055839130366698160)
XLA Ops:
  7.4 1.4 convert_reduce_fusion.2
  8.8 1.7 fusion.28
  10.6 2.2 fusion.55
  12.8 2.4 copy-done.2
  15.2 1.4 fusion.41
  16.7 1.6 copy.86
  18.3 54.2 %all-gather.8.cloned.1.call-done = bf16[512,64,128]{2,1,0:T(8,128)(2,1)} async-done(((bf16[32,64,128]{2,1,0:T(8,128)(2,1)}), bf16[512,64,128]{2,1,0:T(8,128)(2,1)}) %all-gather.8.cloned.1.call-update) | async-done | bytes 8388624 | tf_op jit(solution)/shard_map/all_gather | solution.py:81
  72.5 23.8 %copy.85 = bf16[512,64,128]{1,0,2:T(8,128)(2,1)} copy(bf16[512,64,128]{2,1,0:T(8,128)(2,1)} %all-gather.8.cloned.1.call-done) | data formatting | bytes 16777216 | tf_op jit(solution)/shard_map/all_gather | solution.py:81
  96.3 11.3 %convolution_bitcast_fusion = f32[512,32,128]{0,1,2:T(8,128)} fusion(bf16[512,64,128]{1,0,2:T(8,128)(2,1)} %copy.85, bf16[32,64,128]{1,0,2:T(8,128)(2,1)S(1)} %copy.86), kind=kOutput, calls=%fused_computation.16 | convolution fusion | flops 268435456 | bytes 17301504 | tf_op jit(solution)/shard_map/ikc,jkc->jic/dot_general | solution.py:83
  107.6 11.0 %copy.87 = f32[512,32,128]{2,1,0:T(8,128)} copy(f32[512,32,128]{0,1,2:T(8,128)} %convolution_bitcast_fusion) | data formatting | bytes 16777216 | tf_op jit(solution)/shard_map/ikc,jkc->jic/transpose | solution.py:83
  118.6 114.3 %reduce-scatter.2.cloned.1.call-done = f32[64,32,128]{2,1,0:T(8,128)} async-done(((f32[512,32,128]{2,1,0:T(8,128)}), f32[64,32,128]{2,1,0:T(8,128)}) %reduce-scatter.2.cloned.1.call-update) | async-done | bytes 1048592 | tf_op jit(solution)/shard_map/reduce_scatter | solution.py:82
  232.9 1.6 bitcast_reduce_fusion
  234.6 1.9 multiply_reduce_fusion
  236.7 1.8 multiply_convert_fusion
  238.6 1.8 convert_reduce_fusion.1
  241.1 2.5 fusion.80
  243.5 1.3 fusion.79
  246.3 35.0 %all_gather.29 = f32[4,32,512]{1,0,2:T(4,128)S(1)} all-gather(f32[4,32,64]{1,0,2:T(4,128)S(1)} %copy.95), channel_id=1, replica_groups=mesh['row'=16,'col'=8] {'col'}, dimensions={2}, use_global_device_ids=true | all-gather | bytes 294912 | tf_op jit(solution)/shard_map/all_gather | solution.py:96
  281.4 1.1 copy.96
  282.7 1.4 fusion.39
  284.6 34.8 %all-gather.10.cloned.1.call-done = bf16[32,512,128]{2,1,0:T(8,128)(2,1)} async-done(((bf16[32,64,128]{2,1,0:T(8,128)(2,1)}), bf16[32,512,128]{2,1,0:T(8,128)(2,1)}) %all-gather.10.cloned.1.call-update) | async-done | bytes 4194320 | tf_op jit(solution)/shard_map/all_gather | solution.py:100
  319.4 6.5 copy.94
  325.9 65.3 %all-gather.14.cloned.1.call-done = bf16[32,512,128]{2,1,0:T(8,128)(2,1)} async-done(((bf16[32,64,128]{2,1,0:T(8,128)(2,1)}), bf16[32,512,128]{2,1,0:T(8,128)(2,1)}) %all-gather.14.cloned.1.call-update) | async-done | bytes 4194320 | tf_op jit(solution)/shard_map/all_gather | solution.py:101
  391.2 6.5 copy.98
  397.7 31.1 %all-gather.12.cloned.1.call-done = f32[4,512,512]{2,0,1:T(4,128)} async-done(((f32[4,32,512]{2,0,1:T(4,128)}), f32[4,512,512]{2,0,1:T(4,128)}) %all-gather.12.cloned.1.call-update) | async-done | bytes 4194320 | tf_op jit(solution)/shard_map/all_gather | solution.py:97
  428.8 1.1 constant_dynamic-slice_fusion
  430.1 11.2 %fusion.81 = (f32[32,4,64]{2,1,0:T(4,128)S(1)}, f32[32,4,64,512]{3,2,1,0:T(8,128)}) fusion(f32[512]{0:T(512)S(1)} %add_multiply_fusion, f32[4,64,512]{2,1,0:T(8,128)S(1)} %copy.97, bf16[32,4,64,32]{2,3,1,0:T(8,128)(2,1)S(1)} %bitcast.85, bf16[32,4,512,32]{2,3,1,0:T(8,128)(2,1)} %bitcast.82), kind=kOutput, calls=%fused_computation.117 | convolution fusion | flops 285213184 | bytes 22054912 | tf_op jit(solution)/shard_map/sub | solution.py:22
  441.3 8.3 %fusion.9 = f32[32,4,64,32]{2,3,1,0:T(8,128)S(1)} fusion(bf16[32,4,512,32]{2,3,1,0:T(8,128)(2,1)} %bitcast.87, f32[32,4,64,512]{3,2,1,0:T(8,128)} %get-tuple-element.16, f32[32,4,64]{2,1,0:T(4,128)S(1)} %get-tuple-element.15), kind=kOutput, calls=%fused_computation.15 | convolution fusion | flops 276824064 | bytes 22052864 | tf_op jit(solution)/shard_map/bhqk,bhkd->bhqd/dot_general | solution.py:24
  449.6 1.6 copy.99
  451.1 2.1 convert_reduce_fusion
  454.6 21.1 %all_gather.33 = f32[4,512,64]{2,0,1:T(4,128)S(1)} all-gather(f32[4,32,64]{2,0,1:T(4,128)S(1)} %convolution_bitcast_fusion.1), channel_id=1, replica_groups=mesh['row'=16,'col'=8] {'row'}, dimensions={1}, use_global_device_ids=true | all-gather | bytes 557056 | tf_op jit(solution)/shard_map/all_gather | solution.py:118
  475.7 1.2 copy.103
  477.0 2.5 fusion.82
  479.5 1.3 fusion.78
  481.5 1.4 fusion.34
  483.4 3.5 copy.101
  486.9 59.4 %all-gather.18.cloned.1.call-done = f32[4,512,512]{1,0,2:T(4,128)} async-done(((f32[4,512,64]{1,0,2:T(4,128)}), f32[4,512,512]{1,0,2:T(4,128)}) %all-gather.18.cloned.1.call-update) | async-done | bytes 4194320 | tf_op jit(solution)/shard_map/all_gather | solution.py:119
  546.3 1.0 dynamic-slice_bitcast_fusion
  547.3 51.5 %all-gather.16.cloned.1.call-done = bf16[512,64,128]{2,1,0:T(8,128)(2,1)} async-done(((bf16[32,64,128]{2,1,0:T(8,128)(2,1)}), bf16[512,64,128]{2,1,0:T(8,128)(2,1)}) %all-gather.16.cloned.1.call-update) | async-done | bytes 8388624 | tf_op jit(solution)/shard_map/all_gather | solution.py:123
  598.8 12.7 %copy.102 = bf16[512,64,128]{0,2,1:T(8,128)(2,1)} copy(bf16[512,64,128]{2,1,0:T(8,128)(2,1)} %all-gather.16.cloned.1.call-done) | data formatting | bytes 16777216 | tf_op jit(solution)/shard_map/all_gather | solution.py:123
  611.5 11.6 %fusion.13 = f32[64,4,32,512]{3,2,1,0:T(8,128)} fusion(bf16[64,4,512,32]{2,3,1,0:T(8,128)(2,1)} %bitcast.81, bf16[32,64,4,32]{3,0,2,1:T(8,128)(2,1)S(1)} %copy.101), kind=kOutput, calls=%fused_computation.19 | convolution fusion | flops 268435456 | bytes 25690112 | tf_op jit(solution)/shard_map/bhqd,bhkd->bhqk/dot_general | solution.py:17
  623.1 20.0 %fusion.83 = (f32[64,4,32]{2,1,0:T(4,128)S(1)}, f32[64,4,32,512]{3,2,1,0:T(8,128)}) fusion(f32[64,4,32,512]{3,2,1,0:T(8,128)} %fusion.13, f32[512]{0:T(512)S(1)} %add_multiply_fusion, f32[4,32,512]{2,1,0:T(8,128)S(1)} %copy.104), kind=kOutput, calls=%fused_computation.119 | output fusion | flops 25166336 | bytes 33851392 | tf_op jit(solution)/shard_map/sub | solution.py:22
  643.2 10.6 %all-gather.20.cloned.1.call-done = bf16[512,64,128]{2,1,0:T(8,128)(2,1)} async-done(((bf16[32,64,128]{2,1,0:T(8,128)(2,1)}), bf16[512,64,128]{2,1,0:T(8,128)(2,1)}) %all-gather.20.cloned.1.call-update) | async-done | bytes 8388624 | tf_op jit(solution)/shard_map/all_gather | solution.py:124
  653.7 13.0 %copy.105 = bf16[512,64,128]{0,2,1:T(8,128)(2,1)} copy(bf16[512,64,128]{2,1,0:T(8,128)(2,1)} %all-gather.20.cloned.1.call-done) | data formatting | bytes 16777216 | tf_op jit(solution)/shard_map/all_gather | solution.py:124
  666.7 12.0 %fusion.12 = f32[32,64,4,32]{3,0,2,1:T(8,128)} fusion(bf16[64,4,512,32]{2,3,1,0:T(8,128)(2,1)} %bitcast.84, f32[64,4,32,512]{3,2,1,0:T(8,128)} %get-tuple-element.22, f32[64,4,32]{2,1,0:T(4,128)S(1)} %get-tuple-element.21), kind=kOutput, calls=%fused_computation.18 | convolution fusion | flops 276824064 | bytes 26247168 | tf_op jit(solution)/shard_map/bhqk,bhkd->bhqd/dot_general | solution.py:24
  678.7 3.9 copy.106
  682.5 1.6 copy.107
  684.1 2.8 fusion.16
  (69 shorter events, 7.2 us)
Async XLA Ops:
  6.5 4.1 copy-start
  6.5 65.9 %all-gather.8.cloned.1.call-start = ((), (), s32[]{:S(2)}) async-start(), calls=%async_computation.1 | async-start | bytes 8912896 | tf_op jit(solution)/shard_map/all_gather | solution.py:81
  12.8 2.4 copy-start.2
  16.6 216.3 %reduce-scatter.2.cloned.1.call-start = ((), (), s32[]{:S(2)}) async-start(), calls=%async_computation.2 | async-start | bytes 9437184 | tf_op jit(solution)/shard_map/reduce_scatter | solution.py:82
  118.6 120.0 %copy-start.3 = (bf16[32,64,128]{2,1,0:T(8,128)(2,1)S(1)}, bf16[32,64,128]{2,1,0:T(8,128)(2,1)}, u32[]{:S(2)}) copy-start(bf16[32,64,128]{2,1,0:T(8,128)(2,1)} %param.10) | copy-start | bytes 1572868
  118.6 120.0 %copy-start.9 = (bf16[128,128]{1,0:T(8,128)(2,1)S(1)}, bf16[128,128]{1,0:T(8,128)(2,1)}, u32[]{:S(2)}) copy-start(bf16[128,128]{1,0:T(8,128)(2,1)} %param.13) | copy-start | bytes 98308
  118.6 122.5 %copy-start.6 = (bf16[128,512]{1,0:T(8,128)(2,1)S(1)}, bf16[128,512]{1,0:T(8,128)(2,1)}, u32[]{:S(2)}) copy-start(bf16[128,512]{1,0:T(8,128)(2,1)} %param.14) | copy-start | bytes 393220
  118.6 200.8 %all-gather.10.cloned.1.call-start = ((), (), s32[]{:S(2)}) async-start(), calls=%async_computation.3 | async-start | bytes 4718592 | tf_op jit(solution)/shard_map/all_gather | solution.py:100
  238.5 7.0 %copy-start.12 = (bf16[128,4]{0,1:T(4,128)(2,1)S(1)}, bf16[128,4]{0,1:T(4,128)(2,1)}, u32[]{:S(2)}) copy-start(bf16[128,4]{0,1:T(4,128)(2,1)} %param.15) | copy-start | bytes 3076
  240.4 42.3 %copy-start.8 = (s32[512]{0:T(512)S(1)}, s32[512]{0:T(512)}, u32[]{:S(2)}) copy-start(s32[512]{0:T(512)} %param.11) | copy-start | bytes 6148
  244.9 146.3 %all-gather.14.cloned.1.call-start = ((), (), s32[]{:S(2)}) async-start(), calls=%async_computation.5 | async-start | bytes 4718592 | tf_op jit(solution)/shard_map/all_gather | solution.py:101
  245.4 183.4 %all-gather.12.cloned.1.call-start = ((), (), s32[]{:S(2)}) async-start(), calls=%async_computation.4 | async-start | bytes 4456448 | tf_op jit(solution)/shard_map/all_gather | solution.py:97
  282.4 263.8 %all-gather.18.cloned.1.call-start = ((), (), s32[]{:S(2)}) async-start(), calls=%async_computation.7 | async-start | bytes 4718592 | tf_op jit(solution)/shard_map/all_gather | solution.py:119
  441.3 9.9 %copy-start.10 = (bf16[128,128]{1,0:T(8,128)(2,1)S(1)}, bf16[128,128]{1,0:T(8,128)(2,1)}, u32[]{:S(2)}) copy-start(bf16[128,128]{1,0:T(8,128)(2,1)} %param.16) | copy-start | bytes 98308
  449.6 4.3 copy-start.13
  449.6 27.4 %copy-start.7 = (bf16[128,512]{1,0:T(8,128)(2,1)S(1)}, bf16[128,512]{1,0:T(8,128)(2,1)}, u32[]{:S(2)}) copy-start(bf16[128,512]{1,0:T(8,128)(2,1)} %param.17) | copy-start | bytes 393220
  453.2 30.2 %copy-start.4 = (bf16[32,64,128]{2,1,0:T(8,128)(2,1)}, bf16[32,64,128]{2,1,0:T(8,128)(2,1)S(1)}, u32[]{:S(2)}) copy-start(bf16[32,64,128]{2,1,0:T(8,128)(2,1)S(1)} %get-tuple-element.18) | copy-start | bytes 1572868
  476.9 121.9 %all-gather.16.cloned.1.call-start = ((), (), s32[]{:S(2)}) async-start(), calls=%async_computation.6 | async-start | bytes 8912896 | tf_op jit(solution)/shard_map/all_gather | solution.py:123
  480.8 173.0 %all-gather.20.cloned.1.call-start = ((), (), s32[]{:S(2)}) async-start(), calls=%async_computation.8 | async-start | bytes 8912896 | tf_op jit(solution)/shard_map/all_gather | solution.py:124
  666.7 20.2 %copy-start.1 = (bf16[128,640]{1,0:T(8,128)(2,1)S(1)}, bf16[128,640]{1,0:T(8,128)(2,1)}, u32[]{:S(2)}) copy-start(bf16[128,640]{1,0:T(8,128)(2,1)} %param.12) | copy-start | bytes 491524
  678.7 5.4 copy-start.5
  678.7 5.4 copy-start.11
Sparse Core Ops, SparseCore 0:
  16.7 55.7 all-gather.7
  118.7 114.1 reduce-scatter.1
  245.0 74.3 all-gather.9
  321.8 69.3 all-gather.13
  392.9 35.9 all-gather.11
  477.0 69.1 all-gather.17
  548.1 50.6 all-gather.15
  600.6 53.0 all-gather.19
where the time goes:
time: 696 us; the launch traced here: 694 us
  waiting for transfers between devices  422 us (61%)
  local copies, waits for them, and re-layouts  96.6 us (14%)
  matrix products  69.6 us (10%)
  blocking collectives  56.1 us (8%)
  other arithmetic  34.6 us (5%)
  between operations  13.8 us (2%)
    reduce_scatter x1, waiting for transfers between devices, body(): lax.psum_scatter(jnp.einsum('ikc,jkc->jic', left_terms, right_cols, prefe...  114 us
    all_gather x1, waiting for transfers between devices, body(): lax.all_gather(value_heads, 'col', axis=1, tiled=True)  65.3 us
    all_gather x1, waiting for transfers between devices, body(): bias_all = lax.all_gather(bias_cols, 'col', axis=2, tiled=True)  59.4 us
    all_gather x1, waiting for transfers between devices, body(): right_cols = lax.all_gather(right_terms, 'row', axis=0, tiled=True)  54.2 us
    all_gather x1, waiting for transfers between devices, body(): lax.all_gather(key_heads, 'row', axis=0, tiled=True)  51.5 us
    all_gather x1, blocking collectives, body(): bias_strip = lax.all_gather(bias_terms, 'col', axis=2, tiled=True)  35 us
    all_gather x1, waiting for transfers between devices, body(): lax.all_gather(key_heads, 'col', axis=1, tiled=True)  34.8 us
    all_gather x1, waiting for transfers between devices, body(): bias_all = lax.all_gather(bias_strip, 'row', axis=1, tiled=True)  31.1 us
  transfers between devices with their start and end apart: 8, of which 8 were waited for; matrix products, arithmetic and copies ran while one was open for 11% of the time, Pallas kernels for 0%

commit v1 on v0

v1 whole, which is shorter than its diff:
```python
import jax
import jax.numpy as jnp
from jax import lax
from jax.sharding import Mesh, PartitionSpec as P

everyone = ("xl", "y", "core", "z", "xh")
same_q = ("core", "z", "xh")
same_c = ("xl", "y", "core")
epsilon = 1e-05
bf16, f32 = jnp.bfloat16, jnp.float32


def swap(pieces, axes):
    return lax.all_to_all(pieces, axes, 0, 0, tiled=True)


def layer_norm(values_in, axis=-1):
    average = jnp.mean(values_in, axis=axis, keepdims=True)
    centred = values_in - average
    variance = jnp.mean(centred * centred, axis=axis, keepdims=True)
    return centred * lax.rsqrt(variance + epsilon)


def dot(a, b, dims):
    return lax.dot_general(a, b, (dims, ((), ())), preferred_element_type=f32)


def split_bias(bias, kept, axis):
    masked = jnp.where(kept, bias, -3e38)
    top = jnp.max(masked, axis=axis, keepdims=True)
    top = jnp.where(top > -1e38, top, jnp.max(bias, axis=axis, keepdims=True)).astype(bf16)
    rest = (bias - top.astype(f32)).astype(bf16)
    return top, rest


def attend(query, keys, values, bias, scores_spec):
    scores = jnp.einsum(scores_spec, query, keys, preferred_element_type=f32)
    return scores


def body(pair, mask, tri_in, tri_out, start_in, start_bias, start_out, end_in, end_bias, end_out):
    q = lax.axis_index(("xl", "y"))
    core = lax.axis_index("core")
    c = lax.axis_index(("z", "xh"))
    maskf = mask.astype(f32)
    mask_bias = (maskf - 1.0) * 1000000000.0

    pieces = pair.reshape(4, 8, 2, 32, 128).transpose(2, 1, 0, 3, 4).reshape(16, 128, 128)
    pair_rows = swap(pieces, same_q).reshape(2, 8, 4, 32, 128).transpose(0, 2, 1, 3, 4).reshape(2048, 128)

    normed = layer_norm(pair.astype(f32)).astype(bf16).reshape(2048, 128)
    terms = dot(tri_in[:, :512], normed, ((0,), (1,)))
    row_mask = lax.dynamic_slice_in_dim(maskf, (2 * q + core) * 32, 32)
    col_mask = lax.dynamic_slice_in_dim(maskf, c * 64, 64)
    pair_mask = (row_mask[:, None] * col_mask[None, :]).reshape(1, 2048)
    left = (jax.nn.sigmoid(terms[:128]) * terms[128:256] * pair_mask).astype(bf16)
    right = (jax.nn.sigmoid(terms[256:384]) * terms[384:512] * pair_mask).astype(bf16)
    both = jnp.concatenate([left.reshape(128, 16, 128), right.reshape(128, 16, 128)], axis=1)
    both = swap(both, everyone).reshape(16, 8, 2, 32, 64).transpose(2, 0, 3, 1, 4).reshape(2, 512, 512)
    combined = dot(both[0], both[1], ((1,), (1,))).astype(bf16)
    pieces = combined.reshape(8, 2, 4, 8, 8, 2, 32).transpose(0, 5, 3, 1, 2, 4, 6).reshape(128, 16, 128)
    combined = swap(pieces, everyone).reshape(128, 2048).astype(f32)

    mixed = layer_norm(combined, 0).astype(bf16)
    update = dot(mixed, tri_out, ((0,), (0,)))
    normed_rows = layer_norm(pair_rows.astype(f32)).astype(bf16)
    gate = jax.nn.sigmoid(dot(normed_rows, tri_in[:, 512:], ((1,), (0,))))
    pair_one = (pair_rows.astype(f32) + gate * update).astype(bf16)

    normed = layer_norm(pair_one.astype(f32)).astype(bf16)
    other = swap(jnp.broadcast_to(normed[None], (2, 2048, 128)), "core")
    normed_full = other.reshape(2, 8, 8, 32, 128).transpose(1, 2, 0, 3, 4).reshape(4096, 128)
    kept = lax.dynamic_index_in_dim(mask.reshape(8, 2, 32), core, 1, False).reshape(256) > 0
    bias = dot(start_bias, normed, ((0,), (1,))).reshape(4, 8, 256)
    top, rest = split_bias(bias, kept, 2)
    rest = rest.reshape(4, 2, 4, 256).transpose(1, 0, 2, 3).reshape(2, 32, 128)
    top = top.reshape(4, 2, 4).transpose(1, 0, 2).reshape(2, 1, 16)
    top = jnp.pad(top, ((0, 0), (0, 7), (0, 112)))
    pieces = jnp.concatenate([rest, top], axis=1)
    pieces = jnp.broadcast_to(pieces[None, :, None], (8, 2, 8, 40, 128)).reshape(128, 40, 128)
    pieces = swap(pieces, everyone)
    rest = pieces[:, :32].reshape(8, 2, 8, 4, 4, 8, 32).astype(f32)
    top = pieces[:, 32, :16].reshape(8, 2, 8, 4, 4, 1, 1).astype(f32)
    bias = (rest + top).transpose(3, 0, 4, 2, 5, 1, 6).reshape(4, 256, 512) + mask_bias
    scale = 32 ** (-0.5)
    query = (dot(normed, start_in[:, :128], ((1,), (0,))) * scale).astype(bf16).reshape(8, 256, 4, 32)
    keys = dot(normed_full, start_in[:, 128:256], ((1,), (0,))).astype(bf16).reshape(8, 512, 4, 32)
    values = dot(normed_full, start_in[:, 256:384], ((1,), (0,))).astype(bf16).reshape(8, 512, 4, 32)
    gate = jax.nn.sigmoid(dot(normed, start_in[:, 384:], ((1,), (0,))))
    scores = jnp.einsum("iqhd,ikhd->ihqk", query, keys, preferred_element_type=f32) + bias[None]
    weights = jax.nn.softmax(scores, axis=-1).astype(bf16)
    attended = jnp.einsum("ihqk,ikhd->iqhd", weights, values, preferred_element_type=f32)
    attended = (attended.reshape(2048, 128) * gate).astype(bf16)
    pair_two = (pair_one.astype(f32) + dot(attended, start_out, ((1,), (0,)))).astype(bf16)

    normed = layer_norm(pair_two.astype(f32)).astype(bf16)
    bias = dot(end_bias, normed, ((0,), (1,))).reshape(4, 8, 256)
    own = lax.dynamic_index_in_dim(mask.reshape(8, 2, 4, 8), c, 3, False)
    kept = lax.dynamic_index_in_dim(own, q, 0, False).reshape(8, 1) > 0
    top, rest = split_bias(bias, kept, 1)
    rest = rest.reshape(4, 8, 8, 2, 16).transpose(3, 0, 1, 2, 4).reshape(2, 32, 128)
    top = top.reshape(4, 8, 2, 16).transpose(2, 0, 1, 3).reshape(2, 4, 128)
    extra = jnp.concatenate([rest, jnp.pad(top, ((0, 0), (0, 4), (0, 0)))], axis=1)
    extra = jnp.broadcast_to(extra[None, :, None], (8, 2, 8, 40, 128)).reshape(128, 40, 128)
    pieces = pair_two.reshape(2, 2, 2, 8, 4, 8, 128).transpose(5, 1, 3, 4, 0, 2, 6).reshape(128, 16, 128)
    pieces = swap(jnp.concatenate([pieces, extra], axis=1), everyone)
    pair_two = pieces[:, :16].reshape(8, 2, 8, 4, 2, 2, 128).transpose(1, 3, 0, 4, 5, 2, 6).reshape(2048, 128)
    rest = pieces[:, 16:48].reshape(8, 2, 8, 4, 2, 4, 8, 16).astype(f32)
    top = pieces[:, 48:52].reshape(8, 2, 8, 4, 1, 1, 8, 16).astype(f32)
    bias = (rest + top).transpose(3, 0, 4, 5, 2, 6, 1, 7).reshape(4, 512, 256) + mask_bias[:, None]

    normed = layer_norm(pair_two.astype(f32)).astype(bf16)
    other = swap(jnp.broadcast_to(normed[None], (2, 2048, 128)), "core")
    normed_full = other.reshape(2, 8, 16, 16, 128).transpose(1, 2, 0, 3, 4).reshape(4096, 128)
    query = (dot(normed, end_in[:, :128], ((1,), (0,))) * scale).astype(bf16).reshape(8, 256, 4, 32)
    keys = dot(normed_full, end_in[:, 128:256], ((1,), (0,))).astype(bf16).reshape(8, 512, 4, 32)
    values = dot(normed_full, end_in[:, 256:384], ((1,), (0,))).astype(bf16).reshape(8, 512, 4, 32)
    gate = jax.nn.sigmoid(dot(normed, end_in[:, 384:], ((1,), (0,))))
    scores = jnp.einsum("ikhd,iqhd->ihkq", keys, query, preferred_element_type=f32) + bias[None]
    weights = jax.nn.softmax(scores, axis=2).astype(bf16)
    attended = jnp.einsum("ihkq,ikhd->iqhd", weights, values, preferred_element_type=f32)
    attended = (attended.reshape(2048, 128) * gate).astype(bf16)
    result = (pair_two.astype(f32) + dot(attended, end_out, ((1,), (0,)))).astype(bf16)

    pieces = result.reshape(8, 16, 16, 128).transpose(1, 2, 0, 3).reshape(16, 128, 128)
    pieces = swap(pieces, same_c).reshape(8, 2, 16, 8, 128).transpose(1, 2, 3, 0, 4)
    return pieces.reshape(32, 64, 128)


def solution(mesh):
    parts = Mesh(mesh.devices.reshape(2, 4, 2, 4, 2), everyone)
    placed = P(("xl", "y", "core"), ("z", "xh"), None)
    in_specs = (placed,) + (P(),) * 9
    return jax.shard_map(body, mesh=parts, in_specs=in_specs, out_specs=placed, check_vma=False)
```

time: 696 us -> 337 us (0.48)
  waiting for transfers between devices: 422 us -> 36.6 us
  starting transfers between devices: 0.47 us -> 33.3 us
  local copies, waits for them, and re-layouts: 96.6 us -> 126 us
  matrix products: 69.6 us -> 50.9 us
  between operations: 13.8 us -> 1.02 us
    all_gather x7 -> x0, waiting for transfers between devices: 307 us -> none  [the longest x1 65.3 us: body(): lax.all_gather(value_heads, 'col', axis=1, tiled=True)]
    reduce_scatter x1 -> x0, waiting for transfers between devices: 114 us -> none  [body(): lax.psum_scatter(jnp.einsum('ikc,jkc->jic', left_terms, right_cols, prefe...]
    all_gather x7 -> x0, local copies, waits for them, and re-layouts: 64.7 us -> none  [the longest x1 23.8 us: body(): right_cols = lax.all_gather(right_terms, 'row', axis=0, tiled=True)]
    all_gather x2 -> x0, blocking collectives: 56.1 us -> none  [the longest x1 35 us: body(): bias_strip = lax.all_gather(bias_terms, 'col', axis=2, tiled=True)]
    all_to_all x0 -> x3, blocking collectives: none -> 51.3 us  [swap(): return lax.all_to_all(pieces, axes, 0, 0, tiled=True)]
    reshape x3 -> x21, local copies, waits for them, and re-layouts: 6.58 us -> 54.4 us  [the longest x1 23.5 us: body(): (rest + top).transpose(3, 0, 4, 5, 2, 6, 1, 7).reshape(4, 512, 256)]
    all_to_all x0 -> x5, waiting for transfers between devices: none -> 36.6 us  [swap(): return lax.all_to_all(pieces, axes, 0, 0, tiled=True)]
    all_to_all x0 -> x5, starting transfers between devices: none -> 33.3 us  [swap(): return lax.all_to_all(pieces, axes, 0, 0, tiled=True)]
  transfers between devices with their start and end apart: 8 -> 5, of which waited for: 8 -> 5; matrix products, arithmetic and copies ran while one was open for 11% -> 8% of each run, Pallas kernels for 0% -> 0%
where the time goes in v1:
time: 337 us; the launch traced here: 332 us
  local copies, waits for them, and re-layouts  126 us (37%)
  blocking collectives  51.3 us (15%)
  matrix products  50.9 us (15%)
  waiting for transfers between devices  36.6 us (11%)
  starting transfers between devices  33.3 us (10%)
  other arithmetic  33 us (10%)
    all_to_all x3, blocking collectives, swap(): return lax.all_to_all(pieces, axes, 0, 0, tiled=True)  51.3 us
    all_to_all x5, waiting for transfers between devices, swap(): return lax.all_to_all(pieces, axes, 0, 0, tiled=True)  36.6 us
    all_to_all x5, starting transfers between devices, swap(): return lax.all_to_all(pieces, axes, 0, 0, tiled=True)  33.3 us
    reshape x1, local copies, waits for them, and re-layouts, body(): (rest + top).transpose(3, 0, 4, 5, 2, 6, 1, 7).reshape(4, 512, 256)  23.5 us
    dot_general x14, matrix products, dot(): return lax.dot_general(a, b, (dims, ((), ())), preferred_element_type=f32)  15.2 us
    transpose x1, local copies, waits for them, and re-layouts, body(): (rest + top).transpose(3, 0, 4, 5, 2, 6, 1, 7).reshape(4, 512, 256)  13.4 us
    reshape x1, local copies, waits for them, and re-layouts, body(): (rest + top).transpose(3, 0, 4, 2, 5, 1, 6).reshape(4, 256, 512) + mask_bias  11.9 us
    reshape x3, local copies, waits for them, and re-layouts, body(): combined.reshape(8, 2, 4, 8, 8, 2, 32).transpose(0, 5, 3, 1, 2, 4, 6)  10.7 us
  transfers between devices with their start and end apart: 5, of which 5 were waited for; matrix products, arithmetic and copies ran while one was open for 8% of the time, Pallas kernels for 0%

profile of v1, /device:TPU:1, one launch (start us, length us, event | category | flops | bytes accessed | tf_op | source)
XLA Modules:
  0.0 331.9 jit_solution(12641391613746069446)
XLA Ops:
  0.0 2.0 copy.203
  2.0 9.3 %all-to-all-start = ((bf16[16,128,128]{2,1,0:T(8,128)(2,1)}), bf16[16,128,128]{2,1,0:T(8,128)(2,1)S(1)}, u32[]{:S(2)}, u32[]{:S(2)}) async-start(bf16[16,128,128]{2,1,0:T(8,128)(2,1)} %bitcast.2), calls=%async_computation | async-start | bytes 1048576 | tf_op jit(solution)/shard_map/all_to_all | solution.py:14
  12.7 1.7 fusion.44
  18.6 2.8 all-to-all-done
  21.5 8.4 %all-to-all-start.1 = ((bf16[128,32,128]{2,1,0:T(8,128)(2,1)}), bf16[128,32,128]{2,1,0:T(8,128)(2,1)}, u32[]{:S(2)}, u32[]{:S(2)}) async-start(bf16[128,32,128]{2,1,0:T(8,128)(2,1)} %pad_maximum_fusion.1), calls=%async_computation.1 | async-start | bytes 2097152 | tf_op jit(solution)/shard_map/all_to_all | solution.py:14
  31.6 15.6 %all-to-all-done.1 = bf16[128,32,128]{2,1,0:T(8,128)(2,1)} async-done(((bf16[128,32,128]{2,1,0:T(8,128)(2,1)}), bf16[128,32,128]{2,1,0:T(8,128)(2,1)}, u32[]{:S(2)}, u32[]{:S(2)}) %all-to-all-start.1) | async-done | bytes 1048608 | tf_op jit(solution)/shard_map/all_to_all | solution.py:14
  47.1 2.7 reshape.433
  49.9 1.4 fusion.129
  51.7 1.4 squeeze.12
  54.2 2.3 convolution_convert_fusion.4
  56.5 5.0 %reshape.434 = bf16[8,2,4,8,8,2,32]{6,5,4,3,2,1,0:T(2,128)(2,1)S(1)} reshape(bf16[512,512]{1,0:T(8,128)(2,1)} %convolution_convert_fusion.4) | data formatting | bytes 1048576 | tf_op jit(solution)/shard_map/reshape | solution.py:61
  61.5 1.9 copy.352
  63.4 3.7 %reshape.435 = bf16[128,16,128]{2,1,0:T(8,128)(2,1)} reshape(bf16[8,2,8,2,4,8,32]{6,5,4,3,2,1,0:T(8,128)(2,1)} %bitcast.193) | data formatting | bytes 1048576 | tf_op jit(solution)/shard_map/reshape | solution.py:61
  67.2 5.4 %all-to-all-start.2 = ((bf16[128,16,128]{2,1,0:T(8,128)(2,1)}), bf16[128,16,128]{2,1,0:T(8,128)(2,1)S(1)}, u32[]{:S(2)}, u32[]{:S(2)}) async-start(bf16[128,16,128]{2,1,0:T(8,128)(2,1)} %reshape.435), calls=%async_computation.2 | async-start | bytes 1048576 | tf_op jit(solution)/shard_map/all_to_all | solution.py:14
  73.7 11.9 %all-to-all-done.2 = bf16[128,16,128]{2,1,0:T(8,128)(2,1)S(1)} async-done(((bf16[128,16,128]{2,1,0:T(8,128)(2,1)}), bf16[128,16,128]{2,1,0:T(8,128)(2,1)S(1)}, u32[]{:S(2)}, u32[]{:S(2)}) %all-to-all-start.2) | async-done | bytes 524320 | tf_op jit(solution)/shard_map/all_to_all | solution.py:14
  89.8 5.2 %all-to-all-start.3 = ((bf16[2,2048,128]{2,1,0:T(8,128)(2,1)}), bf16[2,2048,128]{2,1,0:T(8,128)(2,1)S(1)}, u32[]{:S(2)}, u32[]{:S(2)}) async-start(bf16[2,2048,128]{2,1,0:T(8,128)(2,1)} %broadcast_in_dim.22), calls=%async_computation.3 | async-start | bytes 2097152 | tf_op jit(solution)/shard_map/all_to_all | solution.py:14
  95.1 1.7 all-to-all-done.3
  96.8 1.4 broadcast_in_dim.25
  98.2 5.0 %all-to-all-start.4 = ((bf16[128,40,128]{2,1,0:T(8,128)(2,1)}), bf16[128,40,128]{2,1,0:T(8,128)(2,1)}, u32[]{:S(2)}, u32[]{:S(2)}) async-start(bf16[128,40,128]{2,1,0:T(8,128)(2,1)} %bitcast.199), calls=%async_computation.4 | async-start | bytes 2621440 | tf_op jit(solution)/shard_map/all_to_all | solution.py:14
  106.4 2.3 copy.216
  108.7 2.6 copy.262
  114.5 1.4 convolution_convert_fusion.3
  115.9 1.5 copy.214
  118.8 4.6 %all-to-all-done.4 = bf16[128,40,128]{2,1,0:T(8,128)(2,1)} async-done(((bf16[128,40,128]{2,1,0:T(8,128)(2,1)}), bf16[128,40,128]{2,1,0:T(8,128)(2,1)}, u32[]{:S(2)}, u32[]{:S(2)}) %all-to-all-start.4) | async-done | bytes 1310752 | tf_op jit(solution)/shard_map/all_to_all | solution.py:14
  123.4 2.9 slice_convert_fusion.1
  126.3 6.0 %reshape.470 = f32[8,2,8,4,4,8,32]{6,5,4,3,2,1,0:T(8,128)} reshape(f32[128,32,128]{2,1,0:T(8,128)} %slice_convert_fusion.1) | data formatting | bytes 4194304 | tf_op jit(solution)/shard_map/convert_element_type | solution.py:82
  134.1 5.2 %add_bitcast_fusion.1 = f32[4,8,4,8,8,2,32]{6,4,2,0,3,5,1:T(8,128)S(1)} fusion(f32[8,2,8,4,4,8,32]{6,5,4,3,2,1,0:T(8,128)} %reshape.470, f32[8,2,8,4,4]{4,3,2,1,0:T(4,128)S(1)} %copy.224), kind=kLoop, calls=%fused_computation.13 | loop fusion | flops 524288 | bytes 4202496 | tf_op jit(solution)/shard_map/transpose | solution.py:84
  139.3 7.8 %copy.225 = f32[4,8,4,8,8,2,32]{6,5,4,3,2,1,0:T(2,128)} copy(f32[4,8,4,8,8,2,32]{6,4,2,0,3,5,1:T(8,128)S(1)} %add_bitcast_fusion.1) | data formatting | bytes 4194304 | tf_op jit(solution)/shard_map/transpose | solution.py:84
  147.1 11.9 %reshape.447 = f32[4,256,512]{2,1,0:T(8,128)} reshape(f32[4,8,4,8,8,2,32]{6,5,4,3,2,1,0:T(2,128)} %copy.225) | data formatting | bytes 4194304 | tf_op jit(solution)/shard_map/reshape | solution.py:84
  159.0 3.3 broadcast_add_fusion.1
  162.3 10.5 %fusion.131 = (f32[8,4,256]{2,1,0:T(4,128)S(1)}, f32[8,4,256,512]{3,2,1,0:T(8,128)}) fusion(f32[4,256,512]{2,1,0:T(8,128)} %broadcast_add_fusion.1, bf16[8,512,4,32]{1,0,3,2:T(8,128)(2,1)S(1)} %bitcast.221, bf16[8,256,4,32]{1,0,3,2:T(8,128)(2,1)S(1)} %bitcast.225), kind=kOutput, calls=%fused_computation.184 | convolution fusion | flops 281018880 | bytes 20480000 | tf_op jit(solution)/shard_map/sub | solution.py:91
  172.8 8.0 %fusion.37 = f32[8,256,4,32]{1,3,2,0:T(8,128)S(1)} fusion(f32[8,4,256,512]{3,2,1,0:T(8,128)} %get-tuple-element.18, f32[8,4,256]{2,1,0:T(4,128)S(1)} %get-tuple-element.17, bf16[8,512,4,32]{1,0,3,2:T(8,128)(2,1)} %bitcast.222), kind=kOutput, calls=%fused_computation.54 | convolution fusion | flops 276824064 | bytes 18907136 | tf_op jit(solution)/shard_map/ihqk,ikhd->iqhd/dot_general | solution.py:92
  183.1 1.9 convert_reduce_fusion
  188.4 31.4 %all_to_all.40 = bf16[128,56,128]{2,1,0:T(8,128)(2,1)S(1)} all-to-all(bf16[128,56,128]{2,1,0:T(8,128)(2,1)S(1)} %pad_maximum_fusion), channel_id=1, replica_groups=mesh['xl'=2,'y'=4,'core'=2,'z'=4,'xh'=2] {'xl','y','core','z','xh'}, dimensions={0} | all-to-all | bytes 3670016 | tf_op jit(solution)/shard_map/all_to_all | solution.py:14
  224.2 6.4 %all_to_all.41 = bf16[2,2048,128]{2,1,0:T(8,128)(2,1)S(1)} all-to-all(bf16[2,2048,128]{2,1,0:T(8,128)(2,1)S(1)} %broadcast_in_dim.28), channel_id=1, replica_groups=mesh['xl'=2,'y'=4,'core'=2,'z'=4,'xh'=2] {'core'}, dimensions={0} | all-to-all | bytes 2097152 | tf_op jit(solution)/shard_map/all_to_all | solution.py:14
  231.1 1.4 convolution_convert_fusion
  232.5 1.4 convolution_convert_fusion.1
  234.1 8.4 %reshape.473 = f32[8,2,8,4,2,4,8,16]{7,6,5,4,3,2,1,0:T(8,128)} reshape(f32[128,32,128]{2,1,0:T(8,128)S(1)} %slice_convert_fusion) | data formatting | bytes 4194304 | tf_op jit(solution)/shard_map/convert_element_type | solution.py:108
  244.2 7.4 %add_bitcast_fusion = f32[4,8,2,4,8,8,2,16]{7,5,3,2,0,4,6,1:T(8,128)S(1)} fusion(f32[8,2,8,4,2,4,8,16]{7,6,5,4,3,2,1,0:T(8,128)} %reshape.473, f32[8,2,8,4,8,16]{5,4,2,1,0,3:T(8,128)S(1)} %reshape.474), kind=kLoop, calls=%fused_computation.4 | loop fusion | flops 524288 | bytes 4456448 | tf_op jit(solution)/shard_map/transpose | solution.py:110
  251.6 13.4 %copy.249 = f32[4,8,2,4,8,8,2,16]{7,6,5,4,3,2,1,0:T(2,128)} copy(f32[4,8,2,4,8,8,2,16]{7,5,3,2,0,4,6,1:T(8,128)S(1)} %add_bitcast_fusion) | data formatting | bytes 4194304 | tf_op jit(solution)/shard_map/transpose | solution.py:110
  265.0 23.5 %reshape.462 = f32[4,512,256]{2,1,0:T(8,128)S(1)} reshape(f32[4,8,2,4,8,8,2,16]{7,6,5,4,3,2,1,0:T(2,128)} %copy.249) | data formatting | bytes 4194304 | tf_op jit(solution)/shard_map/reshape | solution.py:110
  288.5 1.6 broadcast_add_fusion
  290.1 1.6 copy.243
  294.3 10.6 %fusion.142 = (f32[8,4,256]{2,1,0:T(4,128)S(1)}, f32[8,4,512,256]{3,2,1,0:T(8,128)}) fusion(f32[4,512,256]{2,1,0:T(8,128)} %broadcast_add_fusion, bf16[8,512,4,32]{1,0,3,2:T(8,128)(2,1)} %bitcast.223, bf16[8,256,4,32]{1,0,3,2:T(8,128)(2,1)S(1)} %bitcast.226), kind=kOutput, calls=%fused_computation.185 | convolution fusion | flops 281018880 | bytes 20480000 | tf_op jit(solution)/shard_map/sub | solution.py:120
  305.0 6.6 %fusion.36 = f32[8,256,4,32]{1,3,2,0:T(8,128)S(1)} fusion(f32[8,4,512,256]{3,2,1,0:T(8,128)} %get-tuple-element.22, f32[8,4,256]{2,1,0:T(4,128)S(1)} %get-tuple-element.21, bf16[8,512,4,32]{1,0,3,2:T(8,128)(2,1)S(1)} %bitcast.224), kind=kOutput, calls=%fused_computation.53 | convolution fusion | flops 276824064 | bytes 18907136 | tf_op jit(solution)/shard_map/ihkq,ikhd->iqhd/dot_general | solution.py:121
  313.6 1.5 copy.252
  316.8 13.4 %all_to_all.42 = bf16[16,128,128]{2,1,0:T(8,128)(2,1)S(1)} all-to-all(bf16[16,128,128]{2,1,0:T(8,128)(2,1)S(1)} %bitcast.219), channel_id=1, replica_groups=mesh['xl'=2,'y'=4,'core'=2,'z'=4,'xh'=2] {'xl','y','core'}, dimensions={0} | all-to-all | bytes 1048576 | tf_op jit(solution)/shard_map/all_to_all | solution.py:14
  330.3 1.4 copy.254
  (160 shorter events, 41.8 us)
Async XLA Ops:
  0.0 86.0 %copy-start = (bf16[128,128]{1,0:T(8,128)(2,1)S(1)}, bf16[128,128]{1,0:T(8,128)(2,1)}, u32[]{:S(2)}) copy-start(bf16[128,128]{1,0:T(8,128)(2,1)} %param.13) | copy-start | bytes 98308
  0.0 14.4 %copy-start.2 = (bf16[32,64,128]{2,1,0:T(8,128)(2,1)S(1)}, bf16[32,64,128]{2,1,0:T(8,128)(2,1)}, u32[]{:S(2)}) copy-start(bf16[32,64,128]{2,1,0:T(8,128)(2,1)} %param.10) | copy-start | bytes 1572868
  0.0 15.0 %copy-start.15 = (s32[512]{0:T(512)S(1)}, s32[512]{0:T(512)}, u32[]{:S(2)}) copy-start(s32[512]{0:T(512)} %param.11) | copy-start | bytes 6148
  0.0 15.3 %copy-start.12 = (bf16[128,640]{1,0:T(8,128)(2,1)S(1)}, bf16[128,640]{1,0:T(8,128)(2,1)}, u32[]{:S(2)}) copy-start(bf16[128,640]{1,0:T(8,128)(2,1)} %param.12) | copy-start | bytes 491524
  2.0 19.5 %all-to-all-start = ((bf16[16,128,128]{2,1,0:T(8,128)(2,1)}), bf16[16,128,128]{2,1,0:T(8,128)(2,1)S(1)}, u32[]{:S(2)}, u32[]{:S(2)}) async-start(bf16[16,128,128]{2,1,0:T(8,128)(2,1)} %bitcast.2), calls=%async_computation | async-start | bytes 1048576 | tf_op jit(solution)/shard_map/all_to_all | solution.py:14
  21.5 25.7 %all-to-all-start.1 = ((bf16[128,32,128]{2,1,0:T(8,128)(2,1)}), bf16[128,32,128]{2,1,0:T(8,128)(2,1)}, u32[]{:S(2)}, u32[]{:S(2)}) async-start(bf16[128,32,128]{2,1,0:T(8,128)(2,1)} %pad_maximum_fusion.1), calls=%async_computation.1 | async-start | bytes 2097152 | tf_op jit(solution)/shard_map/all_to_all | solution.py:14
  51.3 1.9 copy-start.9
  67.2 18.3 %all-to-all-start.2 = ((bf16[128,16,128]{2,1,0:T(8,128)(2,1)}), bf16[128,16,128]{2,1,0:T(8,128)(2,1)S(1)}, u32[]{:S(2)}, u32[]{:S(2)}) async-start(bf16[128,16,128]{2,1,0:T(8,128)(2,1)} %reshape.435), calls=%async_computation.2 | async-start | bytes 1048576 | tf_op jit(solution)/shard_map/all_to_all | solution.py:14
  86.0 2.0 copy-start.16
  89.8 15.2 %copy-start.13 = (bf16[128,512]{1,0:T(8,128)(2,1)S(1)}, bf16[128,512]{1,0:T(8,128)(2,1)}, u32[]{:S(2)}) copy-start(bf16[128,512]{1,0:T(8,128)(2,1)} %param.14) | copy-start | bytes 393220
  89.8 7.0 %all-to-all-start.3 = ((bf16[2,2048,128]{2,1,0:T(8,128)(2,1)}), bf16[2,2048,128]{2,1,0:T(8,128)(2,1)S(1)}, u32[]{:S(2)}, u32[]{:S(2)}) async-start(bf16[2,2048,128]{2,1,0:T(8,128)(2,1)} %broadcast_in_dim.22), calls=%async_computation.3 | async-start | bytes 2097152 | tf_op jit(solution)/shard_map/all_to_all | solution.py:14
  96.8 6.8 %copy-start.7 = (bf16[2,2048,128]{2,1,0:T(8,128)(2,1)}, bf16[2,2048,128]{2,1,0:T(8,128)(2,1)S(1)}, u32[]{:S(2)}) copy-start(bf16[2,2048,128]{2,1,0:T(8,128)(2,1)S(1)} %all-to-all-done.3) | copy-start | bytes 3145732
  98.2 25.1 %all-to-all-start.4 = ((bf16[128,40,128]{2,1,0:T(8,128)(2,1)}), bf16[128,40,128]{2,1,0:T(8,128)(2,1)}, u32[]{:S(2)}, u32[]{:S(2)}) async-start(bf16[128,40,128]{2,1,0:T(8,128)(2,1)} %bitcast.199), calls=%async_computation.4 | async-start | bytes 2621440 | tf_op jit(solution)/shard_map/all_to_all | solution.py:14
  159.0 3.3 copy-start.10
  159.0 3.3 copy-start.11
  180.8 2.3 copy-start.17
  181.8 3.9 %copy-start.19 = (bf16[128,4]{0,1:T(4,128)(2,1)S(1)}, bf16[128,4]{0,1:T(4,128)(2,1)}, u32[]{:S(2)}) copy-start(bf16[128,4]{0,1:T(4,128)(2,1)} %param.18) | copy-start | bytes 3076
  219.8 1.3 copy-start.3
  222.2 8.6 %copy-start.5 = (f32[2,4,8,2,2,8,128]{6,5,4,3,2,1,0:T(8,128)}, f32[2,4,8,2,2,8,128]{6,5,4,3,2,1,0:T(8,128)S(1)}, u32[]{:S(2)}) copy-start(f32[2,4,8,2,2,8,128]{6,5,4,3,2,1,0:T(8,128)S(1)} %copy.235) | copy-start | bytes 3145732
  223.5 7.3 %copy-start.14 = (bf16[128,512]{1,0:T(8,128)(2,1)S(1)}, bf16[128,512]{1,0:T(8,128)(2,1)}, u32[]{:S(2)}) copy-start(bf16[128,512]{1,0:T(8,128)(2,1)} %param.17) | copy-start | bytes 393220
  230.6 3.3 copy-start.4
  290.1 3.3 copy-start.8
  311.6 3.5 %copy-start.6 = (f32[2,4,8,2,2,8,128]{6,5,4,3,2,1,0:T(8,128)S(1)}, f32[2,4,8,2,2,8,128]{6,5,4,3,2,1,0:T(8,128)}, u32[]{:S(2)}) copy-start(f32[2,4,8,2,2,8,128]{6,5,4,3,2,1,0:T(8,128)} %copy-done.5) | copy-start | bytes 3145732
  311.6 3.5 %copy-start.18 = (bf16[128,128]{1,0:T(8,128)(2,1)S(1)}, bf16[128,128]{1,0:T(8,128)(2,1)}, u32[]{:S(2)}) copy-start(bf16[128,128]{1,0:T(8,128)(2,1)} %param.19) | copy-start | bytes 98308
  315.1 16.5 %copy-start.1 = (bf16[128,128]{1,0:T(8,128)(2,1)S(1)}, bf16[128,128]{1,0:T(8,128)(2,1)}, u32[]{:S(2)}) copy-start(bf16[128,128]{1,0:T(8,128)(2,1)} %param.13) | copy-start | bytes 98308

commit v2 on v1

v2 whole, which is shorter than its diff:
```python
import jax
import jax.numpy as jnp
from jax import lax
from jax.experimental import pallas as pl
from jax.experimental.pallas import tpu as pltpu
from jax.sharding import Mesh, PartitionSpec as P

everyone = ("xl", "y", "core", "z", "xh")
same_q = ("core", "z", "xh")
same_c = ("xl", "y", "core")
epsilon = 1e-05
bf16, f32 = jnp.bfloat16, jnp.float32
log2e = 1.4426950408889634
lowest = -3e38


def swap(pieces, axes):
    return lax.all_to_all(pieces, axes, 0, 0, tiled=True)


def layer_norm(values_in, axis=-1):
    average = jnp.mean(values_in, axis=axis, keepdims=True)
    centred = values_in - average
    variance = jnp.mean(centred * centred, axis=axis, keepdims=True)
    return centred * lax.rsqrt(variance + epsilon)


def dot(a, b, dims):
    return lax.dot_general(a, b, (dims, ((), ())), preferred_element_type=f32)


def nn(a, b):
    return dot(a, b, ((1,), (0,)))


def nt(a, b):
    return dot(a, b, ((1,), (1,)))


def head_lanes(rows):
    lanes = lax.broadcasted_iota(jnp.int32, (rows, 128), 1)
    return [(lanes >= 32 * head) & (lanes < 32 * head + 32) for head in range(4)]


def start_kernel(core_ref, kept_ref, own_ref, other_ref, rest_ref, mask_ref, w_in_ref, w_out_ref, pair_ref, next_ref,
                 out_ref, extra_ref, bias_ref, after_ref):
    core = core_ref[0]
    to = lax.broadcasted_iota(jnp.int32, (256, 256), 0)
    place = (to // 16 % 2 * 8 + to % 8) * 16 + (to // 32 % 2 * 2 + to // 8 % 2) * 4 + to // 64
    order = (lax.broadcasted_iota(jnp.int32, (256, 256), 1) == place).astype(f32).astype(bf16)
    for half in range(2):
        source = core if half == 0 else 1 - core
        mask_bias = mask_ref[:, half * 256 : half * 256 + 256]
        for block in range(4):
            taken = [
                rest_ref[block * 2 : block * 2 + 2, source, :, part * 16 : part * 16 + 16, :].reshape(256, 128)
                for part in range(2)
            ]
            placed = nn(order, jnp.concatenate(taken, axis=1)) * log2e + mask_bias
            for head in range(4):
                for ah in range(2):
                    at = head * 64 + ah * 32
                    bias_ref[head, ah * 128 + block * 32 : ah * 128 + block * 32 + 32, half * 256 : half * 256 + 256] = (
                        placed[at : at + 32]
                    )
    heads = head_lanes(256)
    ones = jnp.ones((512, 128), bf16)

    def one_row(row, carry):
        own, other = own_ref[row], other_ref[row]
        projected = nn(own, w_in_ref[...])
        projected_other = nn(other, w_in_ref[:, 128:384])
        query = (projected[:, :128] * (32 ** (-0.5) * log2e)).astype(bf16)
        keys = jnp.concatenate([projected[:, 128:256].astype(bf16), projected_other[:, :128].astype(bf16)], axis=0)
        values = jnp.concatenate([projected[:, 256:384].astype(bf16), projected_other[:, 128:].astype(bf16)], axis=0)
        values = jnp.concatenate([values, ones], axis=1)
        gate = jax.nn.sigmoid(projected[:, 384:])
        attended = jnp.zeros((256, 128), f32)
        for head in range(4):
            scores = nt(jnp.where(heads[head], query, jnp.zeros_like(query)), keys) + bias_ref[head]
            weights = jnp.exp2(scores - jnp.max(scores, axis=1, keepdims=True)).astype(bf16)
            summed = nn(weights, values)
            attended = jnp.where(heads[head], summed[:, :128] / summed[:, 128:], attended)
        update = nn((attended * gate).astype(bf16), w_out_ref[...])
        result = (pair_ref[row].astype(f32) + update).astype(bf16)
        out_ref[row] = result
        normed = layer_norm(result.astype(f32)).astype(bf16)
        after_ref[row] = nt(next_ref[...], normed)
        return carry

    lax.fori_loop(0, 8, one_row, 0)
    largest, top = after_ref[0], jnp.full((8, 256), lowest, f32)
    for row in range(8):
        largest = jnp.maximum(largest, after_ref[row])
        top = jnp.maximum(top, jnp.where(kept_ref[row] > 0, after_ref[row], lowest))
    top = jnp.where(top > -1e38, top, largest).astype(bf16).astype(f32)
    for ah in range(2):
        extra_ref[ah, 32:40, :] = top[:, ah * 128 : ah * 128 + 128]
        for row in range(8):
            remains = after_ref[row] - top
            extra_ref[ah, row * 4 : row * 4 + 4, :] = remains[0:4, ah * 128 : ah * 128 + 128]


def end_kernel(core_ref, own_ref, other_ref, rest_ref, top_ref, mask_ref, w_in_ref, w_turned_ref, w_out_ref, pair_ref,
               out_ref, bias_ref):
    core = core_ref[0]
    to = lax.broadcasted_iota(jnp.int32, (256, 256), 0)
    key = to // 16 % 2 * 4 + to // 32 % 2 * 2 + to // 8 % 2
    place = to % 8 * 32 + key * 4 + to // 64
    order = (lax.broadcasted_iota(jnp.int32, (256, 256), 1) == place).astype(f32).astype(bf16)
    to = lax.broadcasted_iota(jnp.int32, (256, 64), 0)
    order_top = (lax.broadcasted_iota(jnp.int32, (256, 64), 1) == to % 8 * 8 + to // 64).astype(f32).astype(bf16)
    for block in range(8):
        rest = jnp.concatenate([rest_ref[block, t].reshape(256, 128) for t in range(2)], axis=1)
        top = jnp.concatenate([top_ref[block, t].reshape(64, 128).astype(bf16) for t in range(2)], axis=1)
        placed = (nn(order, rest) + nn(order_top, top)) * log2e
        for ah in range(2):
            half = core if ah == 0 else 1 - core
            for n5 in range(2):
                rows = pl.ds(pl.multiple_of(half * 256 + n5 * 128 + block * 16, 16), 16)
                mask_bias = mask_ref[rows, :]
                for head in range(4):
                    at = head * 64 + ah * 32 + n5 * 16
                    bias_ref[head, rows, :] = placed[at : at + 16] + mask_bias
    heads = head_lanes(512)
    ones = jnp.ones((16, 512), bf16)

    def one_column(column, carry):
        own, other = own_ref[column], other_ref[column]
        both = jnp.concatenate([own, other], axis=0)
        query = (nn(own, w_in_ref[:, :128]) * (32 ** (-0.5) * log2e)).astype(bf16)
        keys = nn(both, w_in_ref[:, 128:256]).astype(bf16)
        values = nt(w_turned_ref[:128], both).astype(bf16)
        gate = jax.nn.sigmoid(nt(w_turned_ref[128:], own))
        attended = []
        for head in range(4):
            scores = nt(jnp.where(heads[head], keys, jnp.zeros_like(keys)), query) + bias_ref[head]
            weights = jnp.exp2(scores - jnp.max(scores, axis=0, keepdims=True)).astype(bf16)
            summed = nn(jnp.concatenate([values[head * 32 : head * 32 + 32], ones], axis=0), weights)
            attended.append(summed[:32] / summed[32:33])
        attended = (jnp.concatenate(attended, axis=0) * gate).astype(bf16)
        update = dot(attended, w_out_ref[...], ((0,), (0,)))
        out_ref[column] = (pair_ref[column].astype(f32) + update).astype(bf16)
        return carry

    lax.fori_loop(0, 8, one_column, 0)


def call(kernel, in_kinds, outs, scratch, flops):
    spaces = {"s": pltpu.SMEM, "v": pltpu.VMEM}
    return pl.pallas_call(
        kernel,
        out_shape=outs,
        in_specs=[pl.BlockSpec(memory_space=spaces[kind]) for kind in in_kinds],
        out_specs=jax.tree.map(lambda _: pl.BlockSpec(memory_space=pltpu.VMEM), outs),
        scratch_shapes=scratch,
        compiler_params=pltpu.CompilerParams(vmem_limit_bytes=40 * 2**20),
        cost_estimate=pl.CostEstimate(flops=flops, bytes_accessed=4 * 2**20, transcendentals=4 * 2**20),
    )


def body(pair, mask, tri_in, tri_out, start_in, start_bias, start_out, end_in, end_bias, end_out):
    q = lax.axis_index(("xl", "y"))
    core = lax.axis_index("core")
    c = lax.axis_index(("z", "xh"))
    maskf = mask.astype(f32)

    pieces = pair.reshape(4, 8, 2, 32, 128).transpose(2, 1, 0, 3, 4).reshape(16, 128, 128)
    pair_rows = swap(pieces, same_q).reshape(2, 8, 4, 2, 16, 128).transpose(0, 2, 3, 1, 4, 5).reshape(2048, 128)

    normed = layer_norm(pair.astype(f32)).astype(bf16).reshape(2048, 128)
    terms = dot(tri_in[:, :512], normed, ((0,), (1,)))
    row_mask = lax.dynamic_slice_in_dim(maskf, (2 * q + core) * 32, 32)
    col_mask = lax.dynamic_slice_in_dim(maskf, c * 64, 64)
    pair_mask = (row_mask[:, None] * col_mask[None, :]).reshape(1, 2048)
    left = (jax.nn.sigmoid(terms[:128]) * terms[128:256] * pair_mask).astype(bf16)
    right = (jax.nn.sigmoid(terms[256:384]) * terms[384:512] * pair_mask).astype(bf16)
    both = jnp.concatenate([left.reshape(128, 16, 128), right.reshape(128, 16, 128)], axis=1)
    both = swap(both, everyone).reshape(16, 8, 2, 32, 64).transpose(2, 0, 3, 1, 4).reshape(2, 512, 512)
    combined = dot(both[0], both[1], ((1,), (1,))).astype(bf16)
    pieces = combined.reshape(8, 2, 4, 8, 8, 2, 2, 16).transpose(0, 5, 3, 1, 2, 6, 4, 7).reshape(128, 16, 128)
    combined = swap(pieces, everyone).reshape(128, 2048).astype(f32)

    mixed = layer_norm(combined, 0).astype(bf16)
    update = dot(mixed, tri_out, ((0,), (0,)))
    normed_rows = layer_norm(pair_rows.astype(f32)).astype(bf16)
    gate = jax.nn.sigmoid(dot(normed_rows, tri_in[:, 512:], ((1,), (0,))))
    pair_one = (pair_rows.astype(f32) + gate * update).astype(bf16)

    normed = layer_norm(pair_one.astype(f32)).astype(bf16)
    other = lax.ppermute(normed, "core", [(0, 1), (1, 0)])
    halves = mask.reshape(8, 2, 2, 16).transpose(1, 2, 0, 3).reshape(2, 256)
    halves = jnp.concatenate([lax.dynamic_slice_in_dim(halves, place, 1) for place in (core, 1 - core)], axis=1)
    kept = halves.reshape(2, 1, 1, 256) > 0
    bias = dot(start_bias, jnp.stack([normed, other]), ((0,), (2,))).reshape(4, 2, 8, 256).transpose(1, 0, 2, 3)
    top = jnp.max(jnp.where(kept, bias, lowest), axis=(0, 3), keepdims=True)
    top = jnp.where(top > -1e38, top, jnp.max(bias, axis=(0, 3), keepdims=True))
    rest = (bias - top)[0].astype(bf16)
    rest = rest.reshape(4, 2, 4, 2, 128).transpose(1, 3, 2, 0, 4).reshape(1, 2, 1, 32, 128)
    pieces = jnp.broadcast_to(rest, (8, 2, 8, 32, 128)).reshape(128, 32, 128)
    rest = swap(pieces, everyone).reshape(8, 2, 8, 32, 128)
    own_rows = lax.dynamic_index_in_dim(mask.reshape(8, 2, 4, 8), c, 3, False)
    own_rows = lax.dynamic_index_in_dim(own_rows, q, 0, False).reshape(8)
    here = core.astype(jnp.int32).reshape(1)
    next_bias = jnp.pad(end_bias.T, ((0, 4), (0, 0)))
    pair_two, extra = call(
        start_kernel,
        "ssvvvvvvvv",
        (jax.ShapeDtypeStruct((8, 256, 128), bf16), jax.ShapeDtypeStruct((2, 40, 128), f32)),
        [pltpu.VMEM((4, 256, 512), f32), pltpu.VMEM((8, 8, 256), f32)],
        3 * 10**9,
    )(
        here,
        own_rows,
        normed.reshape(8, 256, 128),
        other.reshape(8, 256, 128),
        rest,
        (halves.astype(f32) - 1.0) * (1000000000.0 * log2e),
        start_in,
        start_out,
        pair_one.reshape(8, 256, 128),
        next_bias,
    )

    extra = jnp.broadcast_to(extra.astype(bf16)[None, :, None], (8, 2, 8, 40, 128)).reshape(128, 40, 128)
    pieces = pair_two.reshape(2, 2, 2, 2, 8, 2, 8, 128).transpose(6, 1, 4, 3, 5, 0, 2, 7).reshape(128, 16, 128)
    pieces = swap(jnp.concatenate([pieces, extra], axis=1), everyone)
    pair_two = pieces[:, :16].reshape(8, 2, 8, 4, 2, 2, 128).transpose(1, 3, 4, 0, 5, 2, 6).reshape(2048, 128)
    rest = pieces[:, 16:48].reshape(8, 2, 8, 32, 128)
    top = pieces[:, 48:].astype(f32).reshape(8, 2, 8, 8, 128)

    normed = layer_norm(pair_two.astype(f32)).astype(bf16)
    other = lax.ppermute(normed, "core", [(0, 1), (1, 0)])
    halves = mask.reshape(8, 2, 2, 16).transpose(2, 1, 0, 3).reshape(2, 256)
    halves = jnp.concatenate([lax.dynamic_slice_in_dim(halves, place, 1) for place in (core, 1 - core)], axis=1)
    result = call(
        end_kernel,
        "svvvvvvvvv",
        jax.ShapeDtypeStruct((8, 256, 128), bf16),
        [pltpu.VMEM((4, 512, 256), f32)],
        3 * 10**9,
    )(
        here,
        normed.reshape(8, 256, 128),
        other.reshape(8, 256, 128),
        rest,
        top,
        ((halves.astype(f32) - 1.0) * (1000000000.0 * log2e)).reshape(512, 1),
        end_in,
        end_in[:, 256:].T,
        end_out,
        pair_two.reshape(8, 256, 128),
    )

    pieces = result.reshape(8, 2, 8, 16, 128).transpose(2, 1, 3, 0, 4).reshape(16, 128, 128)
    pieces = swap(pieces, same_c).reshape(8, 2, 16, 8, 128).transpose(1, 2, 3, 0, 4)
    return pieces.reshape(32, 64, 128)


def solution(mesh):
    parts = Mesh(mesh.devices.reshape(2, 4, 2, 4, 2), everyone)
    placed = P(("xl", "y", "core"), ("z", "xh"), None)
    in_specs = (placed,) + (P(),) * 9
    return jax.shard_map(body, mesh=parts, in_specs=in_specs, out_specs=placed, check_vma=False)
```

time: 337 us -> 207 us (0.61); the launches traced: 332 us -> 206 us
  local copies, waits for them, and re-layouts: 126 us -> 36.1 us
  matrix products: 50.9 us -> 2.66 us
  Pallas kernels: 0 us -> 30.6 us
  other arithmetic: 33 us -> 11.3 us
  waiting for transfers between devices: 36.6 us -> 51 us
  blocking collectives: 51.3 us -> 44.4 us
  starting transfers between devices: 33.3 us -> 29.2 us
    reshape x18 -> x10, local copies, waits for them, and re-layouts: 50.8 us -> 16.6 us  [the longest x3 15.7 us: body(): combined.reshape(8, 2, 4, 8, 8, 2, 2, 16).transpose(0, 5, 3, 1, 2, 6, 4, 7)]
    pallas_call x0 -> x2, Pallas kernels: none -> 30.6 us  [the longest x1 17 us: body(): call(end_kernel, 'svvvvvvvvv', jax.ShapeDtypeStruct((8, 256, 128), bf16),...]
    transpose x8 -> x5, local copies, waits for them, and re-layouts: 23.9 us -> 0.69 us  [the longest x1 0.54 us: body(): pair_two.reshape(2, 2, 2, 2, 8, 2, 8, 128).transpose(6, 1, 4, 3, 5, 0, 2, 7)]
    convert_element_type x14 -> x2, local copies, waits for them, and re-layouts: 23.2 us -> 0.12 us  [the longest x1 0.11 us: body(): normed = layer_norm(pair_two.astype(f32)).astype(bf16)]
    sub x2 -> x0, matrix products: 21.1 us -> none  [the longest x1 10.6 us: body(): weights = jax.nn.softmax(scores, axis=2).astype(bf16)]
    dot_general x2 -> x0, matrix products: 14.6 us -> none  [the longest x1 8.03 us: body(): jnp.einsum('ihqk,ikhd->iqhd', weights, values, preferred_element_type=f32)]
    all_to_all x5 -> x4, waiting for transfers between devices: 36.6 us -> 50.1 us  [swap(): return lax.all_to_all(pieces, axes, 0, 0, tiled=True)]
    transpose x4 -> x0, other arithmetic: 12.7 us -> none  [the longest x1 7.4 us: body(): (rest + top).transpose(3, 0, 4, 5, 2, 6, 1, 7).reshape(4, 512, 256)]
  transfers between devices with their start and end apart: 5 -> 6, of which waited for: 5 -> 5; matrix products, arithmetic and copies ran while one was open for 8% -> 6% of each run, Pallas kernels for 0% -> 0%
where the time goes in v2:
time: 207 us; the launch traced here: 206 us
  waiting for transfers between devices  51 us (25%)
  blocking collectives  44.4 us (21%)
  local copies, waits for them, and re-layouts  36.1 us (17%)
  Pallas kernels  30.6 us (15%)
  starting transfers between devices  29.2 us (14%)
  other arithmetic  11.3 us (5%)
  matrix products  2.66 us (1%)
    all_to_all x4, waiting for transfers between devices, swap(): return lax.all_to_all(pieces, axes, 0, 0, tiled=True)  50.1 us
    all_to_all x2, blocking collectives, swap(): return lax.all_to_all(pieces, axes, 0, 0, tiled=True)  44.4 us
    all_to_all x4, starting transfers between devices, swap(): return lax.all_to_all(pieces, axes, 0, 0, tiled=True)  25.8 us
    pallas_call x1, Pallas kernels, body(): call(end_kernel, 'svvvvvvvvv', jax.ShapeDtypeStruct((8, 256, 128), bf16),...  17 us
    reshape x3, local copies, waits for them, and re-layouts, body(): combined.reshape(8, 2, 4, 8, 8, 2, 2, 16).transpose(0, 5, 3, 1, 2, 6, 4, 7)  15.7 us
    pallas_call x1, Pallas kernels, body(): call(start_kernel, 'ssvvvvvvvv', (jax.ShapeDtypeStruct((8, 256, 128), bf1...  13.6 us
    slice x3, local copies, waits for them, and re-layouts, body(): combined = dot(both[0], both[1], ((1,), (1,))).astype(bf16)  5.14 us
  transfers between devices with their start and end apart: 6, of which 5 were waited for; matrix products, arithmetic and copies ran while one was open for 6% of the time, Pallas kernels for 0%

profile of v2, /device:TPU:1, one launch (start us, length us, event | category | flops | bytes accessed | tf_op | source)
XLA Modules:
  0.0 205.9 jit_solution(7300962528823645814)
XLA Ops:
  0.0 2.0 copy.103
  2.0 9.3 %all-to-all-start = ((bf16[16,128,128]{2,1,0:T(8,128)(2,1)}), bf16[16,128,128]{2,1,0:T(8,128)(2,1)S(1)}, u32[]{:S(2)}, u32[]{:S(2)}) async-start(bf16[16,128,128]{2,1,0:T(8,128)(2,1)} %bitcast.3), calls=%async_computation | async-start | bytes 1048576 | tf_op jit(solution)/shard_map/all_to_all | solution.py:18
  12.0 0.6 fusion.11
  12.7 0.6 fusion.12
  13.3 0.7 convolution_bitcast_fusion
  14.0 0.6 fusion.21
  14.6 0.4 copy.108
  15.7 1.1 pad_maximum_fusion.1
  16.7 4.7 %all-to-all-done = bf16[16,128,128]{2,1,0:T(8,128)(2,1)S(1)} async-done(((bf16[16,128,128]{2,1,0:T(8,128)(2,1)}), bf16[16,128,128]{2,1,0:T(8,128)(2,1)S(1)}, u32[]{:S(2)}, u32[]{:S(2)}) %all-to-all-start) | async-done | bytes 524320 | tf_op jit(solution)/shard_map/all_to_all | solution.py:18
  21.5 7.2 %all-to-all-start.1 = ((bf16[128,32,128]{2,1,0:T(8,128)(2,1)}), bf16[128,32,128]{2,1,0:T(8,128)(2,1)S(1)}, u32[]{:S(2)}, u32[]{:S(2)}) async-start(bf16[128,32,128]{2,1,0:T(8,128)(2,1)} %pad_maximum_fusion.1), calls=%async_computation.1 | async-start | bytes 2097152 | tf_op jit(solution)/shard_map/all_to_all | solution.py:18
  28.7 0.4 fusion.32
  29.3 0.8 multiply_reduce_fusion.2
  30.4 16.1 %all-to-all-done.1 = bf16[128,32,128]{2,1,0:T(8,128)(2,1)S(1)} async-done(((bf16[128,32,128]{2,1,0:T(8,128)(2,1)}), bf16[128,32,128]{2,1,0:T(8,128)(2,1)S(1)}, u32[]{:S(2)}, u32[]{:S(2)}) %all-to-all-start.1) | async-done | bytes 1048608 | tf_op jit(solution)/shard_map/all_to_all | solution.py:18
  46.5 1.9 reshape.393
  48.4 3.0 %fusion.49 = (bf16[1,16,32,8,64]{4,2,0,3,1:T(8,128)(2,1)}, bf16[1,16,32,8,64]{4,2,0,3,1:T(8,128)(2,1)S(1)}) fusion(bf16[2,16,32,8,64]{4,2,0,3,1:T(8,128)(2,1)} %bitcast.141), kind=kLoop, calls=%fused_computation.99 | loop fusion | bytes 2097152 | tf_op jit(solution)/shard_map/slice | solution.py:180
  51.4 0.5 copy.110
  51.8 0.6 squeeze.11
  52.5 1.7 copy.111
  54.1 0.6 squeeze.12
  54.7 0.5 convolution_convert_fusion
  55.2 4.5 %reshape.394 = bf16[8,2,4,8,8,2,2,16]{7,6,5,4,3,2,1,0:T(2,128)(2,1)} reshape(bf16[512,512]{1,0:T(8,128)(2,1)S(1)} %convolution_convert_fusion) | data formatting | bytes 1048576 | tf_op jit(solution)/shard_map/reshape | solution.py:181
  59.7 5.4 %copy.152 = bf16[8,2,4,8,8,2,2,16]{7,4,6,2,1,3,5,0:T(8,128)(2,1)} copy(bf16[8,2,4,8,8,2,2,16]{7,6,5,4,3,2,1,0:T(2,128)(2,1)} %reshape.394) | data formatting | bytes 1048576 | tf_op jit(solution)/shard_map/reshape | solution.py:181
  65.2 5.8 %reshape.395 = bf16[128,16,128]{2,1,0:T(8,128)(2,1)} reshape(bf16[8,2,8,2,4,2,8,16]{7,6,5,4,3,2,1,0:T(8,128)(2,1)} %bitcast.132) | data formatting | bytes 1048576 | tf_op jit(solution)/shard_map/reshape | solution.py:181
  71.0 5.4 %all-to-all-start.2 = ((bf16[128,16,128]{2,1,0:T(8,128)(2,1)}), bf16[128,16,128]{2,1,0:T(8,128)(2,1)S(1)}, u32[]{:S(2)}, u32[]{:S(2)}) async-start(bf16[128,16,128]{2,1,0:T(8,128)(2,1)} %reshape.395), calls=%async_computation.2 | async-start | bytes 1048576 | tf_op jit(solution)/shard_map/all_to_all | solution.py:18
  76.4 0.6 fusion.31
  77.4 11.9 %all-to-all-done.2 = bf16[128,16,128]{2,1,0:T(8,128)(2,1)S(1)} async-done(((bf16[128,16,128]{2,1,0:T(8,128)(2,1)}), bf16[128,16,128]{2,1,0:T(8,128)(2,1)S(1)}, u32[]{:S(2)}, u32[]{:S(2)}) %all-to-all-start.2) | async-done | bytes 524320 | tf_op jit(solution)/shard_map/all_to_all | solution.py:18
  89.8 0.7 convert_reduce_fusion
  90.5 0.6 fusion.9
  91.2 0.6 fusion.10
  91.8 1.6 collective-permute-start
  93.4 0.6 fusion.55
  94.1 0.9 collective-permute-done
  95.6 1.2 broadcast_in_dim.21
  96.8 3.8 %all-to-all-start.3 = ((bf16[128,32,128]{2,1,0:T(8,128)(2,1)}), bf16[128,32,128]{2,1,0:T(8,128)(2,1)S(1)}, u32[]{:S(2)}, u32[]{:S(2)}) async-start(bf16[128,32,128]{2,1,0:T(8,128)(2,1)} %bitcast.145), calls=%async_computation.3 | async-start | bytes 2097152 | tf_op jit(solution)/shard_map/all_to_all | solution.py:18
  101.0 17.5 %all-to-all-done.3 = bf16[128,32,128]{2,1,0:T(8,128)(2,1)S(1)} async-done(((bf16[128,32,128]{2,1,0:T(8,128)(2,1)}), bf16[128,32,128]{2,1,0:T(8,128)(2,1)S(1)}, u32[]{:S(2)}, u32[]{:S(2)}) %all-to-all-start.3) | async-done | bytes 1048608 | tf_op jit(solution)/shard_map/all_to_all | solution.py:18
  118.5 13.6 %shard_map.100 = (bf16[8,256,128]{2,1,0:T(8,128)(2,1)S(1)}, f32[2,40,128]{2,1,0:T(8,128)S(1)}) custom-call(s32[1]{0:T(128)} %bitcast.core_ref, s32[8]{0:T(128)S(1)} %reshape.387.kept_ref, bf16[8,256,128]{2,1,0:T(8,128)(2,1)S(1)} %bitcast.125, bf16[8,256,128]{2,1,0:T(8,128)(2,1)S(1)} %bitcast.130, bf16[8,2,8,32,128]{4,3,2,1,0:T(8,128)(2,1)S(1)} %bitcast.123, ...), custom_call_target="tpu_custom_call" | custom-call | flops 3000000000 | bytes 4194304 | tf_op jit(solution)/shard_map/pallas_call | solution.py:206
  132.2 0.5 copy.115
  133.1 31.2 %all_to_all.30 = bf16[128,56,128]{2,1,0:T(8,128)(2,1)S(1)} all-to-all(bf16[128,56,128]{2,1,0:T(8,128)(2,1)S(1)} %pad_maximum_fusion), channel_id=1, replica_groups=mesh['xl'=2,'y'=4,'core'=2,'z'=4,'xh'=2] {'xl','y','core','z','xh'}, dimensions={0} | all-to-all | bytes 3670016 | tf_op jit(solution)/shard_map/all_to_all | solution.py:18
  164.3 1.3 copy-done.6
  165.7 0.4 convert_reduce_fusion.3
  166.5 0.8 multiply_reduce_fusion
  167.8 1.4 fusion.29
  169.2 1.8 collective-permute-start.1
  171.9 1.3 slice.63
  173.3 0.6 multiply_convert_fusion.own_ref
  173.9 17.0 %shard_map.101 = bf16[8,256,128]{2,1,0:T(8,128)(2,1)S(1)} custom-call(s32[1]{0:T(128)} %bitcast.core_ref, bf16[8,256,128]{2,1,0:T(8,128)(2,1)S(1)} %multiply_convert_fusion.own_ref, bf16[8,256,128]{2,1,0:T(8,128)(2,1)S(1)} %bitcast.131, bf16[8,2,8,32,128]{4,3,2,1,0:T(8,128)(2,1)S(1)} %bitcast.124, f32[8,2,8,8,128]{4,3,2,1,0:T(8,128)S(1)} %convert.13.top_ref, ...), custom_call_target="tpu_custom_call" | custom-call | flops 3000000000 | bytes 4194304 | tf_op jit(solution)/shard_map/pallas_call | solution.py:236
  191.3 13.2 %all_to_all.31 = bf16[16,128,128]{2,1,0:T(8,128)(2,1)S(1)} all-to-all(bf16[16,128,128]{2,1,0:T(8,128)(2,1)S(1)} %bitcast.150), channel_id=1, replica_groups=mesh['xl'=2,'y'=4,'core'=2,'z'=4,'xh'=2] {'xl','y','core'}, dimensions={0} | all-to-all | bytes 1048576 | tf_op jit(solution)/shard_map/all_to_all | solution.py:18
  204.5 1.4 copy.131
  (92 shorter events, 6.4 us)
Async XLA Ops:
  0.0 89.8 %copy-start = (bf16[128,128]{1,0:T(8,128)(2,1)S(1)}, bf16[128,128]{1,0:T(8,128)(2,1)}, u32[]{:S(2)}) copy-start(bf16[128,128]{1,0:T(8,128)(2,1)} %param.13) | copy-start | bytes 98308
  0.0 11.3 %copy-start.5 = (bf16[32,64,128]{2,1,0:T(8,128)(2,1)S(1)}, bf16[32,64,128]{2,1,0:T(8,128)(2,1)}, u32[]{:S(2)}) copy-start(bf16[32,64,128]{2,1,0:T(8,128)(2,1)} %param.10) | copy-start | bytes 1572868
  0.0 11.6 %copy-start.8 = (s32[512]{0:T(512)S(1)}, s32[512]{0:T(512)}, u32[]{:S(2)}) copy-start(s32[512]{0:T(512)} %param.11) | copy-start | bytes 6148
  0.0 13.3 %copy-start.7 = (bf16[128,640]{1,0:T(8,128)(2,1)S(1)}, bf16[128,640]{1,0:T(8,128)(2,1)}, u32[]{:S(2)}) copy-start(bf16[128,640]{1,0:T(8,128)(2,1)} %param.12) | copy-start | bytes 491524
  2.0 19.5 %all-to-all-start = ((bf16[16,128,128]{2,1,0:T(8,128)(2,1)}), bf16[16,128,128]{2,1,0:T(8,128)(2,1)S(1)}, u32[]{:S(2)}, u32[]{:S(2)}) async-start(bf16[16,128,128]{2,1,0:T(8,128)(2,1)} %bitcast.3), calls=%async_computation | async-start | bytes 1048576 | tf_op jit(solution)/shard_map/all_to_all | solution.py:18
  21.5 25.0 %all-to-all-start.1 = ((bf16[128,32,128]{2,1,0:T(8,128)(2,1)}), bf16[128,32,128]{2,1,0:T(8,128)(2,1)S(1)}, u32[]{:S(2)}, u32[]{:S(2)}) async-start(bf16[128,32,128]{2,1,0:T(8,128)(2,1)} %pad_maximum_fusion.1), calls=%async_computation.1 | async-start | bytes 2097152 | tf_op jit(solution)/shard_map/all_to_all | solution.py:18
  71.0 18.4 %all-to-all-start.2 = ((bf16[128,16,128]{2,1,0:T(8,128)(2,1)}), bf16[128,16,128]{2,1,0:T(8,128)(2,1)S(1)}, u32[]{:S(2)}, u32[]{:S(2)}) async-start(bf16[128,16,128]{2,1,0:T(8,128)(2,1)} %reshape.395), calls=%async_computation.2 | async-start | bytes 1048576 | tf_op jit(solution)/shard_map/all_to_all | solution.py:18
  90.5 4.4 %copy-start.10 = (bf16[128,4]{0,1:T(4,128)(2,1)S(1)}, bf16[128,4]{0,1:T(4,128)(2,1)}, u32[]{:S(2)}) copy-start(bf16[128,4]{0,1:T(4,128)(2,1)} %param.15) | copy-start | bytes 3076
  91.8 3.2 %collective-permute-start = (bf16[2048,128]{1,0:T(8,128)(2,1)S(1)}, bf16[2048,128]{1,0:T(8,128)(2,1)S(1)}, u32[]{:S(2)}, u32[]{:S(2)}) collective-permute-start(bf16[2048,128]{1,0:T(8,128)(2,1)S(1)} %fusion.10), channel_id=1, source_target_pairs={{0,8},{8,0},{1,9},{9,1},{2,10},{10,2},{3,11},{11,3},{4,12},{12,4},... | collective-permute-start | bytes 1572872 | tf_op jit(solution)/shard_map/ppermute | solution.py:191
  95.3 5.7 %copy-start.9 = (bf16[128,4]{0,1:T(4,128)(2,1)S(1)}, bf16[128,4]{0,1:T(4,128)(2,1)}, u32[]{:S(2)}) copy-start(bf16[128,4]{0,1:T(4,128)(2,1)} %param.18) | copy-start | bytes 3076
  95.3 23.2 %copy-start.2 = (bf16[128,512]{1,0:T(8,128)(2,1)S(1)}, bf16[128,512]{1,0:T(8,128)(2,1)}, u32[]{:S(2)}) copy-start(bf16[128,512]{1,0:T(8,128)(2,1)} %w_in_ref.2) | copy-start | bytes 393220
  95.3 23.2 %copy-start.3 = (bf16[128,128]{1,0:T(8,128)(2,1)S(1)}, bf16[128,128]{1,0:T(8,128)(2,1)}, u32[]{:S(2)}) copy-start(bf16[128,128]{1,0:T(8,128)(2,1)} %w_out_ref.2) | copy-start | bytes 98308
  96.8 21.7 %all-to-all-start.3 = ((bf16[128,32,128]{2,1,0:T(8,128)(2,1)}), bf16[128,32,128]{2,1,0:T(8,128)(2,1)S(1)}, u32[]{:S(2)}, u32[]{:S(2)}) async-start(bf16[128,32,128]{2,1,0:T(8,128)(2,1)} %bitcast.145), calls=%async_computation.3 | async-start | bytes 2097152 | tf_op jit(solution)/shard_map/all_to_all | solution.py:18
  164.3 1.3 copy-start.6
  166.3 4.9 %slice-start = ((bf16[128,512]{1,0:T(8,128)(2,1)}), bf16[128,256]{1,0:T(8,128)(2,1)S(1)}, s32[]{:S(2)}) async-start(bf16[128,512]{1,0:T(8,128)(2,1)} %w_in_ref.3), calls=%async_computation.6 | async-start | bytes 131072 | tf_op jit(solution)/shard_map/slice | solution.py:250
  167.8 4.1 %slice-start.1 = ((bf16[128,56,128]{2,1,0:T(8,128)(2,1)}), bf16[128,8,128]{2,1,0:T(8,128)(2,1)S(1)}, s32[]{:S(2)}) async-start(bf16[128,56,128]{2,1,0:T(8,128)(2,1)} %copy-done.6), calls=%async_computation.7 | async-start | bytes 524288 | tf_op jit(solution)/shard_map/slice | solution.py:230
  169.2 4.7 %collective-permute-start.1 = (bf16[2048,128]{1,0:T(8,128)(2,1)}, bf16[2048,128]{1,0:T(8,128)(2,1)S(1)}, u32[]{:S(2)}, u32[]{:S(2)}) collective-permute-start(bf16[2048,128]{1,0:T(8,128)(2,1)} %fusion.29), channel_id=1, source_target_pairs={{0,8},{8,0},{1,9},{9,1},{2,10},{10,2},{3,11},{11,3},{4,12},{12,4},... | collective-permute-start | bytes 1572872 | tf_op jit(solution)/shard_map/ppermute | solution.py:233
  171.9 2.0 copy-start.1
  171.9 2.0 copy-start.4

commit v3 on v2

--- a/solution.py
+++ b/solution.py
@@ -40,6 +40,34 @@
 def head_lanes(rows):
     lanes = lax.broadcasted_iota(jnp.int32, (rows, 128), 1)
     return [(lanes >= 32 * head) & (lanes < 32 * head + 32) for head in range(4)]
+
+
+def triangle_kernel(both_ref, out_ref, left_ref, right_ref):
+    at = lax.broadcasted_iota(jnp.int32, (256, 256), 0)
+    to = lax.broadcasted_iota(jnp.int32, (256, 256), 1)
+    lanes = (at == to // 64 % 2 * 128 + to // 128 * 64 + to % 64).astype(f32).astype(bf16)
+    for side, kept_ref in ((0, left_ref), (1, right_ref)):
+        for pair_at in range(4):
+            taken = [
+                both_ref[:, :, pair_at * 2 + odd, side * 16 : side * 16 + 16, :].reshape(256, 128) for odd in range(2)
+            ]
+            moved = nn(jnp.concatenate(taken, axis=1), lanes).astype(bf16)
+            for pi in range(2):
+                kept_ref[pi, :, pair_at * 128 : pair_at * 128 + 128] = moved[:, pi * 128 : pi * 128 + 128]
+    right = jnp.concatenate(
+        [right_ref[pi].reshape(8, 2, 16, 512)[:, half].reshape(128, 512) for half in range(2) for pi in range(2)], axis=0
+    )
+    place = to * 0 + at // 2 % 2 * 128 + at // 64 * 32 + at // 4 % 2 * 16 + at % 2 * 8 + at // 8 % 8
+    order = (to == place).astype(f32).astype(bf16)
+    for block in range(2):
+        taken = jnp.concatenate([left_ref[pi, block * 128 : block * 128 + 128, :] for pi in range(2)], axis=0)
+        left = nn(order, taken).astype(bf16)
+        combined = nt(left, right)
+        for q in range(4):
+            for half in range(2):
+                piece = combined[q * 64 : q * 64 + 64, half * 256 : half * 256 + 256].reshape(8, 8, 256)
+                piece = jnp.concatenate([piece[:, :, :128], piece[:, :, 128:]], axis=1)
+                out_ref[block * 4 + q, half] = piece.astype(bf16)
 
 
 def start_kernel(core_ref, kept_ref, own_ref, other_ref, rest_ref, mask_ref, w_in_ref, w_out_ref, pair_ref, next_ref,
@@ -67,7 +95,7 @@
     ones = jnp.ones((512, 128), bf16)
 
     def one_row(row, carry):
-        own, other = own_ref[row], other_ref[row]
+        own, other = own_ref[:, row].reshape(256, 128), other_ref[:, row].reshape(256, 128)
         projected = nn(own, w_in_ref[...])
         projected_other = nn(other, w_in_ref[:, 128:384])
         query = (projected[:, :128] * (32 ** (-0.5) * log2e)).astype(bf16)
@@ -82,8 +110,8 @@
             summed = nn(weights, values)
             attended = jnp.where(heads[head], summed[:, :128] / summed[:, 128:], attended)
         update = nn((attended * gate).astype(bf16), w_out_ref[...])
-        result = (pair_ref[row].astype(f32) + update).astype(bf16)
-        out_ref[row] = result
+        result = (pair_ref[:, row].reshape(256, 128).astype(f32) + update).astype(bf16)
+        out_ref[:, row] = result.reshape(2, 128, 128)
         normed = layer_norm(result.astype(f32)).astype(bf16)
         after_ref[row] = nt(next_ref[...], normed)
         return carry
@@ -166,20 +194,26 @@
     maskf = mask.astype(f32)
 
     pieces = pair.reshape(4, 8, 2, 32, 128).transpose(2, 1, 0, 3, 4).reshape(16, 128, 128)
-    pair_rows = swap(pieces, same_q).reshape(2, 8, 4, 2, 16, 128).transpose(0, 2, 3, 1, 4, 5).reshape(2048, 128)
-
-    normed = layer_norm(pair.astype(f32)).astype(bf16).reshape(2048, 128)
+    pair_rows = swap(pieces, same_q).reshape(2, 8, 4, 2, 16, 128).transpose(3, 0, 2, 1, 4, 5).reshape(2048, 128)
+
+    normed = layer_norm(pair.astype(f32)).astype(bf16)
+    normed = normed.reshape(2, 16, 64, 128).transpose(1, 0, 2, 3).reshape(2048, 128)
     terms = dot(tri_in[:, :512], normed, ((0,), (1,)))
     row_mask = lax.dynamic_slice_in_dim(maskf, (2 * q + core) * 32, 32)
     col_mask = lax.dynamic_slice_in_dim(maskf, c * 64, 64)
-    pair_mask = (row_mask[:, None] * col_mask[None, :]).reshape(1, 2048)
+    pair_mask = (row_mask.reshape(2, 16).T[:, :, None] * col_mask).reshape(1, 2048)
     left = (jax.nn.sigmoid(terms[:128]) * terms[128:256] * pair_mask).astype(bf16)
     right = (jax.nn.sigmoid(terms[256:384]) * terms[384:512] * pair_mask).astype(bf16)
     both = jnp.concatenate([left.reshape(128, 16, 128), right.reshape(128, 16, 128)], axis=1)
-    both = swap(both, everyone).reshape(16, 8, 2, 32, 64).transpose(2, 0, 3, 1, 4).reshape(2, 512, 512)
-    combined = dot(both[0], both[1], ((1,), (1,))).astype(bf16)
-    pieces = combined.reshape(8, 2, 4, 8, 8, 2, 2, 16).transpose(0, 5, 3, 1, 2, 6, 4, 7).reshape(128, 16, 128)
-    combined = swap(pieces, everyone).reshape(128, 2048).astype(f32)
+    both = swap(both, everyone).reshape(8, 2, 8, 32, 128)
+    pieces = call(
+        triangle_kernel,
+        "v",
+        jax.ShapeDtypeStruct((8, 2, 8, 16, 128), bf16),
+        [pltpu.VMEM((2, 256, 512), bf16)] * 2,
+        3 * 10**8,
+    )(both)
+    combined = swap(pieces.reshape(128, 16, 128), everyone).reshape(128, 2048).astype(f32)
 
     mixed = layer_norm(combined, 0).astype(bf16)
     update = dot(mixed, tri_out, ((0,), (0,)))
@@ -191,10 +225,10 @@
     other = lax.ppermute(normed, "core", [(0, 1), (1, 0)])
     halves = mask.reshape(8, 2, 2, 16).transpose(1, 2, 0, 3).reshape(2, 256)
     halves = jnp.concatenate([lax.dynamic_slice_in_dim(halves, place, 1) for place in (core, 1 - core)], axis=1)
-    kept = halves.reshape(2, 1, 1, 256) > 0
-    bias = dot(start_bias, jnp.stack([normed, other]), ((0,), (2,))).reshape(4, 2, 8, 256).transpose(1, 0, 2, 3)
-    top = jnp.max(jnp.where(kept, bias, lowest), axis=(0, 3), keepdims=True)
-    top = jnp.where(top > -1e38, top, jnp.max(bias, axis=(0, 3), keepdims=True))
+    kept = halves.reshape(2, 1, 1, 2, 128) > 0
+    bias = dot(start_bias, jnp.stack([normed, other]), ((0,), (2,))).reshape(4, 2, 2, 8, 128).transpose(1, 0, 3, 2, 4)
+    top = jnp.max(jnp.where(kept, bias, lowest), axis=(0, 3, 4), keepdims=True)
+    top = jnp.where(top > -1e38, top, jnp.max(bias, axis=(0, 3, 4), keepdims=True))
     rest = (bias - top)[0].astype(bf16)
     rest = rest.reshape(4, 2, 4, 2, 128).transpose(1, 3, 2, 0, 4).reshape(1, 2, 1, 32, 128)
     pieces = jnp.broadcast_to(rest, (8, 2, 8, 32, 128)).reshape(128, 32, 128)
@@ -206,24 +240,24 @@
     pair_two, extra = call(
         start_kernel,
         "ssvvvvvvvv",
-        (jax.ShapeDtypeStruct((8, 256, 128), bf16), jax.ShapeDtypeStruct((2, 40, 128), f32)),
+        (jax.ShapeDtypeStruct((2, 8, 128, 128), bf16), jax.ShapeDtypeStruct((2, 40, 128), f32)),
         [pltpu.VMEM((4, 256, 512), f32), pltpu.VMEM((8, 8, 256), f32)],
         3 * 10**9,
     )(
         here,
         own_rows,
-        normed.reshape(8, 256, 128),
-        other.reshape(8, 256, 128),
+        normed.reshape(2, 8, 128, 128),
+        other.reshape(2, 8, 128, 128),
         rest,
         (halves.astype(f32) - 1.0) * (1000000000.0 * log2e),
         start_in,
         start_out,
-        pair_one.reshape(8, 256, 128),
+        pair_one.reshape(2, 8, 128, 128),
         next_bias,
     )
 
     extra = jnp.broadcast_to(extra.astype(bf16)[None, :, None], (8, 2, 8, 40, 128)).reshape(128, 40, 128)
-    pieces = pair_two.reshape(2, 2, 2, 2, 8, 2, 8, 128).transpose(6, 1, 4, 3, 5, 0, 2, 7).reshape(128, 16, 128)
+    pieces = pair_two.reshape(2, 2, 2, 2, 8, 2, 8, 128).transpose(6, 2, 4, 0, 5, 1, 3, 7).reshape(128, 16, 128)
     pieces = swap(jnp.concatenate([pieces, extra], axis=1), everyone)
     pair_two = pieces[:, :16].reshape(8, 2, 8, 4, 2, 2, 128).transpose(1, 3, 4, 0, 5, 2, 6).reshape(2048, 128)
     rest = pieces[:, 16:48].reshape(8, 2, 8, 32, 128)

time: 207 us -> 184 us (0.89)
  local copies, waits for them, and re-layouts: 36.1 us -> 12.4 us
    reshape x4 -> x1, local copies, waits for them, and re-layouts: 17.6 us -> 0.08 us  [body(): row_mask.reshape(2, 16).T[:, :, None] * col_mask]
    slice x3 -> x0, local copies, waits for them, and re-layouts: 5.14 us -> none  [body(): combined = dot(both[0], both[1], ((1,), (1,))).astype(bf16)]
    pallas_call x1 -> x2, Pallas kernels: 13.6 us -> 15.5 us  [the longest x1 13.6 us: body(): call(start_kernel, 'ssvvvvvvvv', (jax.ShapeDtypeStruct((2, 8, 128, 128),...]
  transfers between devices with their start and end apart: 6 -> 6, of which waited for: 5 -> 5; matrix products, arithmetic and copies ran while one was open for 6% -> 7% of each run, Pallas kernels for 0% -> 0%
where the time goes in v3:
time: 184 us
  waiting for transfers between devices  50.8 us (28%)
  blocking collectives  44.4 us (24%)
  Pallas kernels  32.5 us (18%)
  starting transfers between devices  29.5 us (16%)
  local copies, waits for them, and re-layouts  12.4 us (7%)
  other arithmetic  11.3 us (6%)
  matrix products  2.18 us (1%)
    all_to_all x4, waiting for transfers between devices, swap(): return lax.all_to_all(pieces, axes, 0, 0, tiled=True)  49.9 us
    all_to_all x2, blocking collectives, swap(): return lax.all_to_all(pieces, axes, 0, 0, tiled=True)  44.4 us
    all_to_all x4, starting transfers between devices, swap(): return lax.all_to_all(pieces, axes, 0, 0, tiled=True)  26.1 us
    pallas_call x1, Pallas kernels, body(): call(end_kernel, 'svvvvvvvvv', jax.ShapeDtypeStruct((8, 256, 128), bf16),...  17 us
    pallas_call x1, Pallas kernels, body(): call(start_kernel, 'ssvvvvvvvv', (jax.ShapeDtypeStruct((2, 8, 128, 128),...  13.6 us
  transfers between devices with their start and end apart: 6, of which 5 were waited for; matrix products, arithmetic and copies ran while one was open for 7% of the time, Pallas kernels for 0%

profile of v3, /device:TPU:1, one launch (start us, length us, event | category | flops | bytes accessed | tf_op | source)
XLA Modules:
  0.0 183.6 jit_solution(10132832894834162204)
XLA Ops:
  0.0 2.0 %copy.101 = bf16[2,8,4,32,128]{4,3,2,1,0:T(8,128)(2,1)} copy(bf16[2,8,4,32,128]{4,3,0,1,2:T(8,128)(2,1)} %bitcast.135) | data formatting | bytes 1048576 | tf_op jit(solution)/shard_map/transpose | solution.py:196
  2.0 9.4 %all-to-all-start = ((bf16[16,128,128]{2,1,0:T(8,128)(2,1)}), bf16[16,128,128]{2,1,0:T(8,128)(2,1)S(1)}, u32[]{:S(2)}, u32[]{:S(2)}) async-start(bf16[16,128,128]{2,1,0:T(8,128)(2,1)} %bitcast.3), calls=%async_computation | async-start | bytes 1048576 | tf_op jit(solution)/shard_map/all_to_all | solution.py:18
  11.4 0.3 convert_reduce_fusion.1
  12.4 0.6 fusion.11
  13.0 0.6 fusion.12
  13.7 0.7 convolution_bitcast_fusion
  14.4 0.6 fusion.21
  15.0 0.4 copy.108
  15.4 0.4 copy.109
  16.0 1.1 pad_maximum_fusion.1
  17.1 4.5 %all-to-all-done = bf16[16,128,128]{2,1,0:T(8,128)(2,1)S(1)} async-done(((bf16[16,128,128]{2,1,0:T(8,128)(2,1)}), bf16[16,128,128]{2,1,0:T(8,128)(2,1)S(1)}, u32[]{:S(2)}, u32[]{:S(2)}) %all-to-all-start) | async-done | bytes 524320 | tf_op jit(solution)/shard_map/all_to_all | solution.py:18
  21.6 7.2 %all-to-all-start.1 = ((bf16[128,32,128]{2,1,0:T(8,128)(2,1)}), bf16[128,32,128]{2,1,0:T(8,128)(2,1)S(1)}, u32[]{:S(2)}, u32[]{:S(2)}) async-start(bf16[128,32,128]{2,1,0:T(8,128)(2,1)} %pad_maximum_fusion.1), calls=%async_computation.1 | async-start | bytes 2097152 | tf_op jit(solution)/shard_map/all_to_all | solution.py:18
  28.8 0.4 fusion.32
  29.4 0.8 multiply_reduce_fusion.2
  30.6 16.1 %all-to-all-done.1 = bf16[128,32,128]{2,1,0:T(8,128)(2,1)S(1)} async-done(((bf16[128,32,128]{2,1,0:T(8,128)(2,1)}), bf16[128,32,128]{2,1,0:T(8,128)(2,1)S(1)}, u32[]{:S(2)}, u32[]{:S(2)}) %all-to-all-start.1) | async-done | bytes 1048608 | tf_op jit(solution)/shard_map/all_to_all | solution.py:18
  46.6 1.9 %shard_map.100 = bf16[8,2,8,16,128]{4,3,2,1,0:T(8,128)(2,1)} custom-call(bf16[8,2,8,32,128]{4,3,2,1,0:T(8,128)(2,1)S(1)} %bitcast.118), custom_call_target="tpu_custom_call" | custom-call | flops 300000000 | bytes 4194304 | tf_op jit(solution)/shard_map/pallas_call | solution.py:209
  48.5 5.4 %all-to-all-start.2 = ((bf16[128,16,128]{2,1,0:T(8,128)(2,1)}), bf16[128,16,128]{2,1,0:T(8,128)(2,1)S(1)}, u32[]{:S(2)}, u32[]{:S(2)}) async-start(bf16[128,16,128]{2,1,0:T(8,128)(2,1)} %bitcast.16), calls=%async_computation.2 | async-start | bytes 1048576 | tf_op jit(solution)/shard_map/all_to_all | solution.py:18
  53.9 0.6 fusion.31
  54.5 0.4 fusion.3
  55.0 11.9 %all-to-all-done.2 = bf16[128,16,128]{2,1,0:T(8,128)(2,1)S(1)} async-done(((bf16[128,16,128]{2,1,0:T(8,128)(2,1)}), bf16[128,16,128]{2,1,0:T(8,128)(2,1)S(1)}, u32[]{:S(2)}, u32[]{:S(2)}) %all-to-all-start.2) | async-done | bytes 524320 | tf_op jit(solution)/shard_map/all_to_all | solution.py:18
  67.3 0.7 convert_reduce_fusion
  68.0 0.6 fusion.9
  68.7 0.6 fusion.10
  69.3 1.6 collective-permute-start
  71.0 0.6 fusion.52
  71.6 0.9 collective-permute-done
  72.5 0.4 convolution_bitcast_fusion.1
  73.1 1.2 broadcast_in_dim.21
  74.3 4.0 %all-to-all-start.3 = ((bf16[128,32,128]{2,1,0:T(8,128)(2,1)}), bf16[128,32,128]{2,1,0:T(8,128)(2,1)S(1)}, u32[]{:S(2)}, u32[]{:S(2)}) async-start(bf16[128,32,128]{2,1,0:T(8,128)(2,1)} %bitcast.138), calls=%async_computation.3 | async-start | bytes 2097152 | tf_op jit(solution)/shard_map/all_to_all | solution.py:18
  78.4 0.2 dynamic-slice_reduce_fusion
  78.7 17.5 %all-to-all-done.3 = bf16[128,32,128]{2,1,0:T(8,128)(2,1)S(1)} async-done(((bf16[128,32,128]{2,1,0:T(8,128)(2,1)}), bf16[128,32,128]{2,1,0:T(8,128)(2,1)S(1)}, u32[]{:S(2)}, u32[]{:S(2)}) %all-to-all-start.3) | async-done | bytes 1048608 | tf_op jit(solution)/shard_map/all_to_all | solution.py:18
  96.2 13.6 %shard_map.101 = (bf16[2,8,128,128]{3,2,1,0:T(8,128)(2,1)S(1)}, f32[2,40,128]{2,1,0:T(8,128)S(1)}) custom-call(s32[1]{0:T(128)} %bitcast.core_ref, s32[8]{0:T(128)S(1)} %reshape.385.kept_ref, bf16[2,8,128,128]{3,2,1,0:T(8,128)(2,1)S(1)} %bitcast.120, bf16[2,8,128,128]{3,2,1,0:T(8,128)(2,1)S(1)} %bitcast.125, bf16[8,2,8,32,128]{4,3,2,1,0:T(8,128)(2,1)S(1)} %bitcast.117, ...), custom_call_target="tpu_custom_call" | custom-call | flops 3000000000 | bytes 4194304 | tf_op jit(solution)/shard_map/pallas_call | solution.py:240
  109.8 0.5 copy.112
  110.4 0.2 broadcast_in_dim.22
  110.8 31.2 %all_to_all.30 = bf16[128,56,128]{2,1,0:T(8,128)(2,1)S(1)} all-to-all(bf16[128,56,128]{2,1,0:T(8,128)(2,1)S(1)} %pad_maximum_fusion), channel_id=1, replica_groups=mesh['xl'=2,'y'=4,'core'=2,'z'=4,'xh'=2] {'xl','y','core','z','xh'}, dimensions={0} | all-to-all | bytes 3670016 | tf_op jit(solution)/shard_map/all_to_all | solution.py:18
  142.0 1.3 copy-done.6
  143.4 0.4 convert_reduce_fusion.3
  144.2 0.8 multiply_reduce_fusion
  145.3 0.2 div.63
  145.5 1.4 fusion.29
  146.9 1.8 collective-permute-start.1
  149.4 0.2 div.61
  149.6 1.3 slice.51
  151.0 0.6 multiply_convert_fusion.own_ref
  151.6 17.0 %shard_map.102 = bf16[8,256,128]{2,1,0:T(8,128)(2,1)S(1)} custom-call(s32[1]{0:T(128)} %bitcast.core_ref, bf16[8,256,128]{2,1,0:T(8,128)(2,1)S(1)} %multiply_convert_fusion.own_ref, bf16[8,256,128]{2,1,0:T(8,128)(2,1)S(1)} %bitcast.126, bf16[8,2,8,32,128]{4,3,2,1,0:T(8,128)(2,1)S(1)} %bitcast.119, f32[8,2,8,8,128]{4,3,2,1,0:T(8,128)S(1)} %convert.13.top_ref, ...), custom_call_target="tpu_custom_call" | custom-call | flops 3000000000 | bytes 4194304 | tf_op jit(solution)/shard_map/pallas_call | solution.py:270
  168.6 0.3 copy.127
  169.0 13.2 %all_to_all.31 = bf16[16,128,128]{2,1,0:T(8,128)(2,1)S(1)} all-to-all(bf16[16,128,128]{2,1,0:T(8,128)(2,1)S(1)} %bitcast.144), channel_id=1, replica_groups=mesh['xl'=2,'y'=4,'core'=2,'z'=4,'xh'=2] {'xl','y','core'}, dimensions={0} | all-to-all | bytes 1048576 | tf_op jit(solution)/shard_map/all_to_all | solution.py:18
  182.2 1.4 copy.128
  (85 shorter events, 3.9 us)
Async XLA Ops:
  0.0 67.3 %copy-start = (bf16[128,128]{1,0:T(8,128)(2,1)S(1)}, bf16[128,128]{1,0:T(8,128)(2,1)}, u32[]{:S(2)}) copy-start(bf16[128,128]{1,0:T(8,128)(2,1)} %param.13) | copy-start | bytes 98308
  0.0 11.4 %copy-start.5 = (bf16[32,64,128]{2,1,0:T(8,128)(2,1)S(1)}, bf16[32,64,128]{2,1,0:T(8,128)(2,1)}, u32[]{:S(2)}) copy-start(bf16[32,64,128]{2,1,0:T(8,128)(2,1)} %param.10) | copy-start | bytes 1572868
  0.0 11.7 %copy-start.8 = (s32[512]{0:T(512)S(1)}, s32[512]{0:T(512)}, u32[]{:S(2)}) copy-start(s32[512]{0:T(512)} %param.11) | copy-start | bytes 6148
  2.0 11.7 %copy-start.7 = (bf16[128,640]{1,0:T(8,128)(2,1)S(1)}, bf16[128,640]{1,0:T(8,128)(2,1)}, u32[]{:S(2)}) copy-start(bf16[128,640]{1,0:T(8,128)(2,1)} %param.12) | copy-start | bytes 491524
  2.0 19.6 %all-to-all-start = ((bf16[16,128,128]{2,1,0:T(8,128)(2,1)}), bf16[16,128,128]{2,1,0:T(8,128)(2,1)S(1)}, u32[]{:S(2)}, u32[]{:S(2)}) async-start(bf16[16,128,128]{2,1,0:T(8,128)(2,1)} %bitcast.3), calls=%async_computation | async-start | bytes 1048576 | tf_op jit(solution)/shard_map/all_to_all | solution.py:18
  21.6 25.0 %all-to-all-start.1 = ((bf16[128,32,128]{2,1,0:T(8,128)(2,1)}), bf16[128,32,128]{2,1,0:T(8,128)(2,1)S(1)}, u32[]{:S(2)}, u32[]{:S(2)}) async-start(bf16[128,32,128]{2,1,0:T(8,128)(2,1)} %pad_maximum_fusion.1), calls=%async_computation.1 | async-start | bytes 2097152 | tf_op jit(solution)/shard_map/all_to_all | solution.py:18
  48.5 18.3 %all-to-all-start.2 = ((bf16[128,16,128]{2,1,0:T(8,128)(2,1)}), bf16[128,16,128]{2,1,0:T(8,128)(2,1)S(1)}, u32[]{:S(2)}, u32[]{:S(2)}) async-start(bf16[128,16,128]{2,1,0:T(8,128)(2,1)} %bitcast.16), calls=%async_computation.2 | async-start | bytes 1048576 | tf_op jit(solution)/shard_map/all_to_all | solution.py:18
  68.0 4.4 %copy-start.10 = (bf16[128,4]{0,1:T(4,128)(2,1)S(1)}, bf16[128,4]{0,1:T(4,128)(2,1)}, u32[]{:S(2)}) copy-start(bf16[128,4]{0,1:T(4,128)(2,1)} %param.15) | copy-start | bytes 3076
  69.3 3.2 %collective-permute-start = (bf16[2048,128]{1,0:T(8,128)(2,1)S(1)}, bf16[2048,128]{1,0:T(8,128)(2,1)S(1)}, u32[]{:S(2)}, u32[]{:S(2)}) collective-permute-start(bf16[2048,128]{1,0:T(8,128)(2,1)S(1)} %fusion.10), channel_id=1, source_target_pairs={{0,8},{8,0},{1,9},{9,1},{2,10},{10,2},{3,11},{11,3},{4,12},{12,4},... | collective-permute-start | bytes 1572872 | tf_op jit(solution)/shard_map/ppermute | solution.py:225
  72.8 5.8 %copy-start.9 = (bf16[128,4]{0,1:T(4,128)(2,1)S(1)}, bf16[128,4]{0,1:T(4,128)(2,1)}, u32[]{:S(2)}) copy-start(bf16[128,4]{0,1:T(4,128)(2,1)} %param.18) | copy-start | bytes 3076
  72.8 23.4 %copy-start.2 = (bf16[128,512]{1,0:T(8,128)(2,1)S(1)}, bf16[128,512]{1,0:T(8,128)(2,1)}, u32[]{:S(2)}) copy-start(bf16[128,512]{1,0:T(8,128)(2,1)} %w_in_ref.2) | copy-start | bytes 393220
  72.8 23.4 %copy-start.3 = (bf16[128,128]{1,0:T(8,128)(2,1)S(1)}, bf16[128,128]{1,0:T(8,128)(2,1)}, u32[]{:S(2)}) copy-start(bf16[128,128]{1,0:T(8,128)(2,1)} %w_out_ref.2) | copy-start | bytes 98308
  74.3 21.9 %all-to-all-start.3 = ((bf16[128,32,128]{2,1,0:T(8,128)(2,1)}), bf16[128,32,128]{2,1,0:T(8,128)(2,1)S(1)}, u32[]{:S(2)}, u32[]{:S(2)}) async-start(bf16[128,32,128]{2,1,0:T(8,128)(2,1)} %bitcast.138), calls=%async_computation.3 | async-start | bytes 2097152 | tf_op jit(solution)/shard_map/all_to_all | solution.py:18
  142.0 1.3 copy-start.6
  144.0 4.9 %slice-start = ((bf16[128,512]{1,0:T(8,128)(2,1)}), bf16[128,256]{1,0:T(8,128)(2,1)S(1)}, s32[]{:S(2)}) async-start(bf16[128,512]{1,0:T(8,128)(2,1)} %w_in_ref.3), calls=%async_computation.6 | async-start | bytes 131072 | tf_op jit(solution)/shard_map/slice | solution.py:284
  145.5 4.1 %slice-start.1 = ((bf16[128,56,128]{2,1,0:T(8,128)(2,1)}), bf16[128,8,128]{2,1,0:T(8,128)(2,1)S(1)}, s32[]{:S(2)}) async-start(bf16[128,56,128]{2,1,0:T(8,128)(2,1)} %copy-done.6), calls=%async_computation.7 | async-start | bytes 524288 | tf_op jit(solution)/shard_map/slice | solution.py:264
  146.9 4.7 %collective-permute-start.1 = (bf16[2048,128]{1,0:T(8,128)(2,1)}, bf16[2048,128]{1,0:T(8,128)(2,1)S(1)}, u32[]{:S(2)}, u32[]{:S(2)}) collective-permute-start(bf16[2048,128]{1,0:T(8,128)(2,1)} %fusion.29), channel_id=1, source_target_pairs={{0,8},{8,0},{1,9},{9,1},{2,10},{10,2},{3,11},{11,3},{4,12},{12,4},... | collective-permute-start | bytes 1572872 | tf_op jit(solution)/shard_map/ppermute | solution.py:267
  149.6 2.0 %copy-start.1 = (bf16[128,512]{1,0:T(8,128)(2,1)S(1)}, bf16[128,512]{1,0:T(8,128)(2,1)}, u32[]{:S(2)}) copy-start(bf16[128,512]{1,0:T(8,128)(2,1)} %w_in_ref.3) | copy-start | bytes 393220
  149.6 2.0 %copy-start.4 = (bf16[128,128]{1,0:T(8,128)(2,1)S(1)}, bf16[128,128]{1,0:T(8,128)(2,1)}, u32[]{:S(2)}) copy-start(bf16[128,128]{1,0:T(8,128)(2,1)} %w_out_ref.3) | copy-start | bytes 98308

commit v4 on v3

v4 whole, which is shorter than its diff:
```python
import jax
import jax.numpy as jnp
from jax import lax
from jax.experimental import pallas as pl
from jax.experimental.pallas import tpu as pltpu
from jax.sharding import Mesh, PartitionSpec as P

everyone = ("xl", "y", "core", "z", "xh")
by_row = ("z", "xh", "core")
same_c = ("xl", "y", "core")
epsilon = 1e-05
bf16, f32 = jnp.bfloat16, jnp.float32
log2e = 1.4426950408889634
lowest = -3e38


def swap(pieces, axes):
    return lax.all_to_all(pieces, axes, 0, 0, tiled=True)


def layer_norm(values_in, axis=-1):
    average = jnp.mean(values_in, axis=axis, keepdims=True)
    centred = values_in - average
    variance = jnp.mean(centred * centred, axis=axis, keepdims=True)
    return centred * lax.rsqrt(variance + epsilon)


def dot(a, b, dims):
    return lax.dot_general(a, b, (dims, ((), ())), preferred_element_type=f32)


def nn(a, b):
    return dot(a, b, ((1,), (0,)))


def nt(a, b):
    return dot(a, b, ((1,), (1,)))


def head_lanes(rows):
    lanes = lax.broadcasted_iota(jnp.int32, (rows, 128), 1)
    return [(lanes >= 32 * head) & (lanes < 32 * head + 32) for head in range(4)]


def terms_kernel(pair_ref, w_in_ref, mask_ref, left_ref, right_ref, held_ref):
    for step in range(8):
        rows = [(place % 8) * 4 + ah * 2 + place // 8 for place in (2 * step, 2 * step + 1) for ah in range(2)]
        tokens = jnp.concatenate([pair_ref[row] for row in rows], axis=0).astype(f32)
        terms = dot(w_in_ref[...], layer_norm(tokens).astype(bf16), ((0,), (1,)))
        for side in range(2):
            at = side * 256
            kept = jax.nn.sigmoid(terms[at : at + 128]) * terms[at + 128 : at + 256] * mask_ref[step : step + 1, :]
            for odd in range(2):
                held_ref[side, pl.ds(2 * step + odd, 128, stride=16), :] = kept[:, odd * 128 : odd * 128 + 128]
    left_ref[...] = held_ref[0].astype(bf16).reshape(128, 16, 128)
    right_ref[...] = held_ref[1].astype(bf16).reshape(128, 16, 128)


def triangle_kernel(both_ref, out_ref, left_ref, right_ref):
    at = lax.broadcasted_iota(jnp.int32, (256, 256), 0)
    to = lax.broadcasted_iota(jnp.int32, (256, 256), 1)
    lanes = (at == to // 64 % 2 * 128 + to // 128 * 64 + to % 64).astype(f32).astype(bf16)
    for side, kept_ref in ((0, left_ref), (1, right_ref)):
        for pair_at in range(4):
            taken = [
                both_ref[:, :, pair_at * 2 + odd, side * 16 : side * 16 + 16, :].reshape(256, 128) for odd in range(2)
            ]
            moved = nn(jnp.concatenate(taken, axis=1), lanes).astype(bf16)
            for pi in range(2):
                kept_ref[pi, :, pair_at * 128 : pair_at * 128 + 128] = moved[:, pi * 128 : pi * 128 + 128]
    place = to * 0 + at // 8 % 8 * 32 + at // 128 * 16 + at // 64 % 2 * 8 + at % 8
    order = (to == place).astype(f32).astype(bf16)
    right = [nn(order, right_ref[pi]).astype(bf16) for pi in range(2)]
    right = jnp.concatenate([right[pi][half * 128 : half * 128 + 128] for half in range(2) for pi in range(2)], axis=0)
    place = to * 0 + at // 2 % 2 * 128 + at // 64 * 32 + at // 4 % 2 * 16 + at % 2 * 8 + at // 8 % 8
    order = (to == place).astype(f32).astype(bf16)
    for block in range(2):
        taken = jnp.concatenate([left_ref[pi, block * 128 : block * 128 + 128, :] for pi in range(2)], axis=0)
        left = nn(order, taken).astype(bf16)
        combined = nt(left, right)
        for q in range(4):
            for half in range(2):
                piece = combined[q * 64 : q * 64 + 64, half * 256 : half * 256 + 256].reshape(8, 8, 256)
                piece = jnp.concatenate([piece[:, :, :128], piece[:, :, 128:]], axis=1)
                out_ref[block * 4 + q, half] = piece.astype(bf16)


def mix_kernel(combined_ref, pair_ref, gate_ref, w_ref, one_ref, normed_ref, held_ref):
    held_ref[...] = layer_norm(combined_ref[...].astype(f32), 0).reshape(2048, 128)
    for step in range(8):
        mixed = [held_ref[pl.ds(2 * step + odd, 128, stride=16), :] for odd in range(2)]
        update = dot(jnp.concatenate(mixed, axis=1).astype(bf16), w_ref[...], ((0,), (0,)))
        rows = slice(2 * step, 2 * step + 2)
        pair = pair_ref[rows].reshape(256, 128).astype(f32)
        one = (pair + gate_ref[rows].reshape(256, 128) * update).astype(bf16)
        one_ref[rows] = one.reshape(2, 128, 128)
        normed_ref[rows] = layer_norm(one.astype(f32)).astype(bf16).reshape(2, 128, 128)


def bias_kernel(own_ref, other_ref, w_ref, mask_ref, out_ref, held_ref):
    sides = [nt(w_ref[...], side[...].reshape(2048, 128)) for side in (own_ref, other_ref)]
    for row in range(8):
        parts = [side[:, ah * 1024 + row * 128 : ah * 1024 + row * 128 + 128] for side in sides for ah in range(2)]
        largest, top = parts[0], jnp.full((8, 128), lowest, f32)
        for place, part in enumerate(parts):
            largest = jnp.maximum(largest, part)
            top = jnp.maximum(top, jnp.where(mask_ref[:, place * 128 : place * 128 + 128] > 0, part, lowest))
        top = jnp.max(top, axis=1, keepdims=True)
        top = jnp.where(top > -1e38, top, jnp.max(largest, axis=1, keepdims=True))
        for ah in range(2):
            at = ah * 16 + row % 4 * 4
            held_ref[row // 4, at : at + 4, :] = (parts[ah] - top)[0:4]
    out_ref[...] = jnp.broadcast_to(held_ref[...].astype(bf16)[None, :, None], (8, 2, 8, 32, 128))


def start_kernel(core_ref, kept_ref, own_ref, other_ref, rest_ref, mask_ref, w_in_ref, w_out_ref, pair_ref, next_ref,
                 out_ref, extra_ref, bias_ref, after_ref):
    core = core_ref[0]
    to = lax.broadcasted_iota(jnp.int32, (256, 256), 0)
    place = (to // 8 % 2 * 8 + to % 8) * 16 + (to // 16 % 4) * 4 + to // 64
    order = (lax.broadcasted_iota(jnp.int32, (256, 256), 1) == place).astype(f32).astype(bf16)
    for half in range(2):
        source = core if half == 0 else 1 - core
        mask_bias = mask_ref[:, half * 256 : half * 256 + 256]
        for block in range(4):
            taken = [
                rest_ref[block * 2 : block * 2 + 2, source, :, part * 16 : part * 16 + 16, :].reshape(256, 128)
                for part in range(2)
            ]
            placed = nn(order, jnp.concatenate(taken, axis=1)) * log2e + mask_bias
            for head in range(4):
                for part in range(4):
                    at = head * 64 + part * 16
                    bias_ref[head, part * 64 + block * 16 : part * 64 + block * 16 + 16, half * 256 : half * 256 + 256] = (
                        placed[at : at + 16]
                    )
    heads = head_lanes(256)
    ones = jnp.ones((512, 128), bf16)

    def one_row(row, carry):
        own, other = own_ref[:, row].reshape(256, 128), other_ref[:, row].reshape(256, 128)
        projected = nn(own, w_in_ref[...])
        projected_other = nn(other, w_in_ref[:, 128:384])
        query = (projected[:, :128] * (32 ** (-0.5) * log2e)).astype(bf16)
        keys = jnp.concatenate([projected[:, 128:256].astype(bf16), projected_other[:, :128].astype(bf16)], axis=0)
        values = jnp.concatenate([projected[:, 256:384].astype(bf16), projected_other[:, 128:].astype(bf16)], axis=0)
        values = jnp.concatenate([values, ones], axis=1)
        gate = jax.nn.sigmoid(projected[:, 384:])
        queries = jnp.concatenate([jnp.where(lanes, query, jnp.zeros_like(query)) for lanes in heads], axis=0)
        scores = nt(queries, keys)
        attended = jnp.zeros((256, 128), f32)
        for head in range(4):
            part = scores[head * 256 : head * 256 + 256] + bias_ref[head]
            weights = jnp.exp2(part - jnp.max(part, axis=1, keepdims=True)).astype(bf16)
            summed = nn(weights, values)
            attended = jnp.where(heads[head], summed[:, :128] / summed[:, 128:], attended)
        update = nn((attended * gate).astype(bf16), w_out_ref[...])
        result = (pair_ref[:, row].reshape(256, 128).astype(f32) + update).astype(bf16)
        out_ref[:, row] = result.reshape(2, 128, 128)
        return carry

    lax.fori_loop(0, 8, one_row, 0, unroll=2)
    for row in range(8):
        normed = layer_norm(out_ref[:, row].reshape(256, 128).astype(f32)).astype(bf16)
        after_ref[row] = nt(next_ref[...], normed)
    largest, top = after_ref[0], jnp.full((8, 256), lowest, f32)
    for row in range(8):
        largest = jnp.maximum(largest, after_ref[row])
        top = jnp.maximum(top, jnp.where(kept_ref[row] > 0, after_ref[row], lowest))
    top = jnp.where(top > -1e38, top, largest).astype(bf16).astype(f32)
    for ah in range(2):
        extra_ref[ah, 32:40, :] = top[:, ah * 128 : ah * 128 + 128]
        for row in range(8):
            remains = after_ref[row] - top
            extra_ref[ah, row * 4 : row * 4 + 4, :] = remains[0:4, ah * 128 : ah * 128 + 128]


def end_kernel(core_ref, pieces_ref, other_ref, top_ref, mask_ref, w_in_ref, w_turned_ref, w_out_ref, out_ref, bias_ref,
               own_ref, both_ref):
    core = core_ref[0]
    to = lax.broadcasted_iota(jnp.int32, (256, 256), 0)
    key = to // 16 % 2 * 4 + to // 32 % 2 * 2 + to // 8 % 2
    place = to % 8 * 32 + key * 4 + to // 64
    order = (lax.broadcasted_iota(jnp.int32, (256, 256), 1) == place).astype(f32).astype(bf16)
    to = lax.broadcasted_iota(jnp.int32, (256, 64), 0)
    order_top = (lax.broadcasted_iota(jnp.int32, (256, 64), 1) == to % 8 * 8 + to // 64).astype(f32).astype(bf16)
    for block in range(8):
        rest = jnp.concatenate([pieces_ref[block, t, :, 16:48, :].reshape(256, 128) for t in range(2)], axis=1)
        top = jnp.concatenate([top_ref[block, t].reshape(64, 128).astype(bf16) for t in range(2)], axis=1)
        placed = (nn(order, rest) + nn(order_top, top)) * log2e
        for ah in range(2):
            half = core if ah == 0 else 1 - core
            for part in range(4):
                rows = pl.ds(pl.multiple_of(half * 256 + part * 64 + block * 8, 8), 8)
                mask_bias = mask_ref[rows, :]
                for head in range(4):
                    at = head * 64 + ah * 32 + part * 8
                    bias_ref[head, rows, :] = placed[at : at + 8] + mask_bias
    for block in range(8):
        for t in range(2):
            rows = slice(block * 128, block * 128 + 128)
            own_ref[t, rows, :] = pieces_ref[block, t, :, 0:16, :].astype(f32).reshape(128, 128)
            both_ref[t, rows, :] = other_ref[block, t].astype(f32).reshape(128, 128)
    heads = head_lanes(512)
    ones = jnp.ones((16, 512), bf16)

    def taken(from_ref, column):
        return jnp.concatenate(
            [from_ref[column // 4, pl.ds(column % 4 * 4 + part, 64, stride=16), :] for part in range(4)], axis=0
        )

    def one_column(column, carry):
        pair = taken(own_ref, column)
        own = layer_norm(pair).astype(bf16)
        other = layer_norm(taken(both_ref, column)).astype(bf16)
        both = jnp.concatenate([own, other], axis=0)
        query = (nn(own, w_in_ref[:, :128]) * (32 ** (-0.5) * log2e)).astype(bf16)
        keys = nn(both, w_in_ref[:, 128:256]).astype(bf16)
        values = nt(w_turned_ref[:128], both).astype(bf16)
        gate = jax.nn.sigmoid(nt(w_turned_ref[128:], own))
        stacked = jnp.concatenate([jnp.where(lanes, keys, jnp.zeros_like(keys)) for lanes in heads], axis=0)
        scores = nt(stacked, query)
        attended = []
        for head in range(4):
            part = scores[head * 512 : head * 512 + 512] + bias_ref[head]
            weights = jnp.exp2(part - jnp.max(part, axis=0, keepdims=True)).astype(bf16)
            summed = nn(jnp.concatenate([values[head * 32 : head * 32 + 32], ones], axis=0), weights)
            attended.append(summed[:32] / summed[32:33])
        attended = (jnp.concatenate(attended, axis=0) * gate).astype(bf16)
        update = dot(attended, w_out_ref[...], ((0,), (0,)))
        out_ref[column] = (pair + update).astype(bf16)
        return carry

    lax.fori_loop(0, 8, one_column, 0, unroll=2)


def call(kernel, in_kinds, outs, scratch, flops):
    spaces = {"s": pltpu.SMEM, "v": pltpu.VMEM}
    return pl.pallas_call(
        kernel,
        out_shape=outs,
        in_specs=[pl.BlockSpec(memory_space=spaces[kind]) for kind in in_kinds],
        out_specs=jax.tree.map(lambda _: pl.BlockSpec(memory_space=pltpu.VMEM), outs),
        scratch_shapes=scratch,
        compiler_params=pltpu.CompilerParams(vmem_limit_bytes=40 * 2**20),
        cost_estimate=pl.CostEstimate(flops=flops, bytes_accessed=4 * 2**20, transcendentals=4 * 2**20),
    )


def body(pair, mask, tri_in, tri_out, start_in, start_bias, start_out, end_in, end_bias, end_out):
    q = lax.axis_index(("xl", "y"))
    core = lax.axis_index("core")
    c = lax.axis_index(("z", "xh"))
    maskf = mask.astype(f32)

    rows = swap(pair.reshape(16, 128, 128), by_row).reshape(8, 2, 2, 2, 32, 128)

    row_mask = lax.dynamic_slice_in_dim(maskf, (2 * q + core) * 32, 32)
    col_mask = lax.dynamic_slice_in_dim(maskf, c * 64, 64)
    pair_mask = (row_mask.reshape(8, 2, 2).transpose(2, 0, 1).reshape(16, 2, 1) * col_mask).reshape(8, 256)
    both = call(
        terms_kernel,
        "vvv",
        (jax.ShapeDtypeStruct((128, 16, 128), bf16),) * 2,
        [pltpu.VMEM((2, 2048, 128), f32)],
        3 * 10**8,
    )(pair, tri_in[:, :512], pair_mask)
    both = jnp.concatenate(both, axis=1)
    both, rows = lax.optimization_barrier((both, rows))
    both = swap(both, everyone).reshape(8, 2, 8, 32, 128)
    kept = lax.dynamic_index_in_dim(rows, core, 3, False)
    given = lax.ppermute(lax.dynamic_index_in_dim(rows, 1 - core, 3, False), "core", [(0, 1), (1, 0)])
    rows = jnp.stack([jnp.where(core == 0, kept, given), jnp.where(core == 0, given, kept)])
    rows = rows.reshape(2, 8, 2, 2, 8, 2, 2, 128).transpose(5, 2, 0, 3, 6, 1, 4, 7)
    pair_rows = rows.reshape(2048, 128)
    pieces = call(
        triangle_kernel,
        "v",
        jax.ShapeDtypeStruct((8, 2, 8, 16, 128), bf16),
        [pltpu.VMEM((2, 256, 512), bf16)] * 2,
        3 * 10**8,
    )(both)
    combined = swap(pieces.reshape(128, 16, 128), everyone)

    normed_rows = layer_norm(pair_rows.astype(f32)).astype(bf16)
    gate = jax.nn.sigmoid(dot(normed_rows, tri_in[:, 512:], ((1,), (0,))))
    pair_one, normed = call(
        mix_kernel,
        "vvvv",
        (jax.ShapeDtypeStruct((16, 128, 128), bf16),) * 2,
        [pltpu.VMEM((2048, 128), f32)],
        2 * 10**8,
    )(combined, pair_rows.reshape(16, 128, 128), gate.reshape(16, 128, 128), tri_out)

    other = lax.ppermute(normed, "core", [(0, 1), (1, 0)])
    halves = mask.reshape(8, 2, 8, 2, 2).transpose(1, 3, 4, 0, 2).reshape(2, 256)
    halves = jnp.concatenate([lax.dynamic_slice_in_dim(halves, place, 1) for place in (core, 1 - core)], axis=1)
    pieces = call(
        bias_kernel,
        "vvvv",
        jax.ShapeDtypeStruct((8, 2, 8, 32, 128), bf16),
        [pltpu.VMEM((2, 32, 128), f32)],
        10**8,
    )(
        normed.reshape(2, 8, 128, 128),
        other.reshape(2, 8, 128, 128),
        jnp.pad(start_bias.T, ((0, 4), (0, 0))),
        halves.astype(f32),
    )
    rest = swap(pieces.reshape(128, 32, 128), everyone).reshape(8, 2, 8, 32, 128)
    own_rows = lax.dynamic_index_in_dim(mask.reshape(8, 2, 8, 4), c, 2, False)
    own_rows = lax.dynamic_index_in_dim(own_rows, q, 0, False).reshape(8)
    here = core.astype(jnp.int32).reshape(1)
    next_bias = jnp.pad(end_bias.T, ((0, 4), (0, 0)))
    pair_two, extra = call(
        start_kernel,
        "ssvvvvvvvv",
        (jax.ShapeDtypeStruct((2, 8, 128, 128), bf16), jax.ShapeDtypeStruct((2, 40, 128), f32)),
        [pltpu.VMEM((4, 256, 512), f32), pltpu.VMEM((8, 8, 256), f32)],
        3 * 10**9,
    )(
        here,
        own_rows,
        normed.reshape(2, 8, 128, 128),
        other.reshape(2, 8, 128, 128),
        rest,
        (halves.astype(f32) - 1.0) * (1000000000.0 * log2e),
        start_in,
        start_out,
        pair_one.reshape(2, 8, 128, 128),
        next_bias,
    )

    extra = jnp.broadcast_to(extra.astype(bf16)[None, :, None], (8, 2, 8, 40, 128)).reshape(128, 40, 128)
    pieces = pair_two.reshape(2, 2, 2, 2, 2, 8, 8, 128).transpose(6, 2, 5, 0, 4, 1, 3, 7).reshape(128, 16, 128)
    pieces = swap(jnp.concatenate([pieces, extra], axis=1), everyone)
    other = lax.ppermute(pieces[:, :16], "core", [(0, 1), (1, 0)])
    top = pieces[:, 48:].astype(f32).reshape(8, 2, 8, 8, 128)

    halves = mask.reshape(8, 2, 8, 2, 2).transpose(3, 1, 4, 0, 2).reshape(2, 256)
    halves = jnp.concatenate([lax.dynamic_slice_in_dim(halves, place, 1) for place in (core, 1 - core)], axis=1)
    result = call(
        end_kernel,
        "svvvvvvv",
        jax.ShapeDtypeStruct((8, 256, 128), bf16),
        [pltpu.VMEM((4, 512, 256), f32)] + [pltpu.VMEM((2, 1024, 128), f32)] * 2,
        3 * 10**9,
    )(
        here,
        pieces.reshape(8, 2, 8, 56, 128),
        other.reshape(8, 2, 8, 16, 128),
        top,
        ((halves.astype(f32) - 1.0) * (1000000000.0 * log2e)).reshape(512, 1),
        end_in,
        end_in[:, 256:].T,
        end_out,
    )

    pieces = result.reshape(8, 2, 2, 8, 8, 128).transpose(3, 1, 2, 4, 0, 5).reshape(16, 128, 128)
    pieces = swap(pieces, same_c).reshape(8, 2, 2, 8, 2, 4, 128).transpose(3, 1, 2, 4, 0, 5, 6)
    return pieces.reshape(32, 64, 128)


def solution(mesh):
    parts = Mesh(mesh.devices.reshape(2, 4, 2, 4, 2), everyone)
    placed = P(("xl", "y", "core"), ("z", "xh"), None)
    in_specs = (placed,) + (P(),) * 9
    return jax.shard_map(body, mesh=parts, in_specs=in_specs, out_specs=placed, check_vma=False)
```

time: 184 us -> 168 us (0.913)
  other arithmetic: 11.3 us -> 4.11 us
  local copies, waits for them, and re-layouts: 12.4 us -> 8.94 us
  Pallas kernels: 32.5 us -> 30.1 us
    convert_element_type x6 -> x0, other arithmetic: 3.93 us -> none  [the longest x2 2.01 us: body(): normed = layer_norm(pair_two.astype(f32)).astype(bf16)]
    ppermute x0 -> x2, starting transfers between devices: none -> 3.11 us  [the longest x1 1.86 us: body(): other = lax.ppermute(pieces[:, :16], 'core', [(0, 1), (1, 0)])]
    all_to_all x4, starting transfers between devices: 26.1 us -> 23.4 us  [swap(): return lax.all_to_all(pieces, axes, 0, 0, tiled=True)]
    pallas_call x1, Pallas kernels: 13.6 us -> 11.2 us  [body(): call(start_kernel, 'ssvvvvvvvv', (jax.ShapeDtypeStruct((2, 8, 128, 128),...]
    reduce_sum x5 -> x1, other arithmetic: 3.01 us -> 0.78 us  [layer_norm(): variance = jnp.mean(centred * centred, axis=axis, keepdims=True)]
    ppermute x2 -> x1, starting transfers between devices: 3.4 us -> 1.54 us  [body(): other = lax.ppermute(normed, 'core', [(0, 1), (1, 0)])]
    transpose x9 -> x5, local copies, waits for them, and re-layouts: 4.17 us -> 2.33 us  [the longest x1 1.07 us: body(): swap(pieces, same_c).reshape(8, 2, 2, 8, 2, 4, 128)]
    pallas_call x1 -> x4, Pallas kernels: 17 us -> 16.8 us  [the longest x1 12 us: body(): call(end_kernel, 'svvvvvvv', jax.ShapeDtypeStruct((8, 256, 128), bf16), [...]
  transfers between devices with their start and end apart: 6 -> 7, of which waited for: 5 -> 6; matrix products, arithmetic and copies ran while one was open for 7% -> 6% of each run, Pallas kernels for 0% -> 1%
where the time goes in v4:
time: 168 us
  waiting for transfers between devices  50.2 us (30%)
  blocking collectives  44.7 us (27%)
  Pallas kernels  30.1 us (18%)
  starting transfers between devices  28.1 us (17%)
  local copies, waits for them, and re-layouts  8.94 us (5%)
  other arithmetic  4.11 us (2%)
    all_to_all x4, waiting for transfers between devices, swap(): return lax.all_to_all(pieces, axes, 0, 0, tiled=True)  48.6 us
    all_to_all x2, blocking collectives, swap(): return lax.all_to_all(pieces, axes, 0, 0, tiled=True)  44.7 us
    all_to_all x4, starting transfers between devices, swap(): return lax.all_to_all(pieces, axes, 0, 0, tiled=True)  23.4 us
    pallas_call x1, Pallas kernels, body(): call(end_kernel, 'svvvvvvv', jax.ShapeDtypeStruct((8, 256, 128), bf16), [...  12 us
    pallas_call x1, Pallas kernels, body(): call(start_kernel, 'ssvvvvvvvv', (jax.ShapeDtypeStruct((2, 8, 128, 128),...  11.2 us
  transfers between devices with their start and end apart: 7, of which 6 were waited for; matrix products, arithmetic and copies ran while one was open for 6% of the time, Pallas kernels for 1%

profile of v4, /device:TPU:1, one launch (start us, length us, event | category | flops | bytes accessed | tf_op | source)
XLA Modules:
  0.0 167.7 jit_solution(533206335272198013)
XLA Ops:
  0.0 9.3 %all-to-all-start = ((bf16[16,128,128]{2,1,0:T(8,128)(2,1)}), bf16[16,128,128]{2,1,0:T(8,128)(2,1)S(1)}, u32[]{:S(2)}, u32[]{:S(2)}) async-start(bf16[16,128,128]{2,1,0:T(8,128)(2,1)} %bitcast.73), calls=%async_computation | async-start | bytes 1048576 | tf_op jit(solution)/shard_map/all_to_all | solution.py:18
  9.3 0.7 convert_element_type.39
  10.1 0.1 copy.86
  10.5 0.9 slice.15.w_in_ref
  11.5 1.0 copy-done
  12.5 1.8 %shard_map.100 = (bf16[128,16,128]{2,1,0:T(8,128)(2,1)S(1)}, bf16[128,16,128]{2,1,0:T(8,128)(2,1)S(1)}) custom-call(bf16[32,64,128]{2,1,0:T(8,128)(2,1)S(1)} %copy-done, bf16[128,512]{1,0:T(8,128)(2,1)S(1)} %slice.15.w_in_ref, f32[8,256]{1,0:T(8,128)S(1)} %mul.70.mask_ref), custom_call_target="tpu_custom_call" | custom-call | flops 300000000 | bytes 4194304 | tf_op jit(solution)/shard_map/pallas_call | solution.py:261
  14.3 1.1 pad_maximum_fusion.1
  15.4 5.2 %all-to-all-done = bf16[16,128,128]{2,1,0:T(8,128)(2,1)S(1)} async-done(((bf16[16,128,128]{2,1,0:T(8,128)(2,1)}), bf16[16,128,128]{2,1,0:T(8,128)(2,1)S(1)}, u32[]{:S(2)}, u32[]{:S(2)}) %all-to-all-start) | async-done | bytes 524320 | tf_op jit(solution)/shard_map/all_to_all | solution.py:18
  20.6 1.2 collective-permute-start
  21.9 4.8 %all-to-all-start.1 = ((bf16[128,32,128]{2,1,0:T(8,128)(2,1)}), bf16[128,32,128]{2,1,0:T(8,128)(2,1)S(1)}, u32[]{:S(2)}, u32[]{:S(2)}) async-start(bf16[128,32,128]{2,1,0:T(8,128)(2,1)} %pad_maximum_fusion.1), calls=%async_computation.1 | async-start | bytes 2097152 | tf_op jit(solution)/shard_map/all_to_all | solution.py:18
  26.7 0.2 copy.72
  26.9 0.2 copy.71
  27.1 0.4 convert_reduce_fusion
  27.5 0.1 copy.75
  27.7 0.1 copy.76
  27.9 0.8 multiply_reduce_fusion
  28.7 0.1 copy.77
  29.1 0.6 copy.74
  29.7 0.2 copy.73
  29.9 14.6 %all-to-all-done.1 = bf16[128,32,128]{2,1,0:T(8,128)(2,1)S(1)} async-done(((bf16[128,32,128]{2,1,0:T(8,128)(2,1)}), bf16[128,32,128]{2,1,0:T(8,128)(2,1)S(1)}, u32[]{:S(2)}, u32[]{:S(2)}) %all-to-all-start.1) | async-done | bytes 1048608 | tf_op jit(solution)/shard_map/all_to_all | solution.py:18
  44.4 2.0 %shard_map.101 = bf16[8,2,8,16,128]{4,3,2,1,0:T(8,128)(2,1)} custom-call(bf16[8,2,8,32,128]{4,3,2,1,0:T(8,128)(2,1)S(1)} %bitcast.71), custom_call_target="tpu_custom_call" | custom-call | flops 300000000 | bytes 4194304 | tf_op jit(solution)/shard_map/pallas_call | solution.py:276
  46.5 5.4 %all-to-all-start.2 = ((bf16[128,16,128]{2,1,0:T(8,128)(2,1)}), bf16[128,16,128]{2,1,0:T(8,128)(2,1)S(1)}, u32[]{:S(2)}, u32[]{:S(2)}) async-start(bf16[128,16,128]{2,1,0:T(8,128)(2,1)} %bitcast.6), calls=%async_computation.2 | async-start | bytes 1048576 | tf_op jit(solution)/shard_map/all_to_all | solution.py:18
  51.9 0.6 fusion.4
  52.5 1.2 fusion.2
  53.7 11.1 %all-to-all-done.2.combined_ref = bf16[128,16,128]{2,1,0:T(8,128)(2,1)S(1)} async-done(((bf16[128,16,128]{2,1,0:T(8,128)(2,1)}), bf16[128,16,128]{2,1,0:T(8,128)(2,1)S(1)}, u32[]{:S(2)}, u32[]{:S(2)}) %all-to-all-start.2) | async-done | bytes 524320 | tf_op jit(solution)/shard_map/all_to_all | solution.py:18
  64.8 1.5 shard_map.102
  66.4 0.8 copy-done.6
  67.2 1.5 collective-permute-start.1
  68.7 0.2 reshape.247
  68.9 0.3 copy.78
  69.3 0.3 copy.80
  69.7 0.5 collective-permute-done.1
  70.2 1.5 shard_map.103
  71.8 4.0 %all-to-all-start.3 = ((bf16[128,32,128]{2,1,0:T(8,128)(2,1)}), bf16[128,32,128]{2,1,0:T(8,128)(2,1)S(1)}, u32[]{:S(2)}, u32[]{:S(2)}) async-start(bf16[128,32,128]{2,1,0:T(8,128)(2,1)} %bitcast.19), calls=%async_computation.3 | async-start | bytes 2097152 | tf_op jit(solution)/shard_map/all_to_all | solution.py:18
  76.0 17.7 %all-to-all-done.3 = bf16[128,32,128]{2,1,0:T(8,128)(2,1)S(1)} async-done(((bf16[128,32,128]{2,1,0:T(8,128)(2,1)}), bf16[128,32,128]{2,1,0:T(8,128)(2,1)S(1)}, u32[]{:S(2)}, u32[]{:S(2)}) %all-to-all-start.3) | async-done | bytes 1048608 | tf_op jit(solution)/shard_map/all_to_all | solution.py:18
  93.7 11.2 %shard_map.104 = (bf16[2,8,128,128]{3,2,1,0:T(8,128)(2,1)S(1)}, f32[2,40,128]{2,1,0:T(8,128)S(1)}) custom-call(s32[1]{0:T(128)} %bitcast.core_ref, s32[8]{0:T(128)S(1)} %reshape.238.kept_ref, bf16[2,8,128,128]{3,2,1,0:T(8,128)(2,1)S(1)} %bitcast.79, bf16[2,8,128,128]{3,2,1,0:T(8,128)(2,1)S(1)} %bitcast.81, bf16[8,2,8,32,128]{4,3,2,1,0:T(8,128)(2,1)S(1)} %bitcast.72, ...), custom_call_target="tpu_custom_call" | custom-call | flops 3000000000 | bytes 4194304 | tf_op jit(solution)/shard_map/pallas_call | solution.py:315
  104.9 0.5 copy.79
  105.5 0.2 broadcast_in_dim.2
  105.7 0.1 pad_maximum_fusion
  105.9 31.2 %all_to_all.30 = bf16[128,56,128]{2,1,0:T(8,128)(2,1)S(1)} all-to-all(bf16[128,56,128]{2,1,0:T(8,128)(2,1)S(1)} %pad_maximum_fusion), channel_id=1, replica_groups=mesh['xl'=2,'y'=4,'core'=2,'z'=4,'xh'=2] {'xl','y','core','z','xh'}, dimensions={0} | all-to-all | bytes 3670016 | tf_op jit(solution)/shard_map/all_to_all | solution.py:18
  137.1 1.9 %collective-permute-start.2 = (bf16[128,16,128]{2,1,0:T(8,128)(2,1)S(1)}, bf16[128,16,128]{2,1,0:T(8,128)(2,1)S(1)}, u32[]{:S(2)}, u32[]{:S(2)}) collective-permute-start(bf16[128,16,128]{2,1,0:T(8,128)(2,1)S(1)} %slice.20), channel_id=1, source_target_pairs={{0,8},{8,0},{1,9},{9,1},{2,10},{10,2},{3,11},{11,3},{4,12},{12,4},... | collective-permute-start | bytes 1572872 | tf_op jit(solution)/shard_map/ppermute | solution.py:337
  139.0 0.1 copy.81
  139.2 0.1 copy.88
  139.4 1.1 collective-permute-done.2
  140.5 12.0 %shard_map.105 = bf16[8,256,128]{2,1,0:T(8,128)(2,1)S(1)} custom-call(s32[1]{0:T(128)} %bitcast.core_ref, bf16[8,2,8,56,128]{4,3,2,1,0:T(8,128)(2,1)S(1)} %bitcast.70, bf16[8,2,8,16,128]{4,3,2,1,0:T(8,128)(2,1)S(1)} %bitcast.82, f32[8,2,8,8,128]{4,3,2,1,0:T(8,128)S(1)} %convert.2.top_ref, f32[512,1]{1,0:T(8,128)S(1)} %broadcast_multiply_fusion.mask_ref, ...), custom_call_target="tpu_custom_call" | custom-call | flops 3000000000 | bytes 4194304 | tf_op jit(solution)/shard_map/pallas_call | solution.py:342
  152.5 0.6 copy.84
  153.1 13.5 %all_to_all.31 = bf16[16,128,128]{2,1,0:T(8,128)(2,1)S(1)} all-to-all(bf16[16,128,128]{2,1,0:T(8,128)(2,1)S(1)} %bitcast.95), channel_id=1, replica_groups=mesh['xl'=2,'y'=4,'core'=2,'z'=4,'xh'=2] {'xl','y','core'}, dimensions={0} | all-to-all | bytes 1048576 | tf_op jit(solution)/shard_map/all_to_all | solution.py:18
  166.6 1.1 copy.85
  (50 shorter events, 1.5 us)
Async XLA Ops:
  0.0 20.6 %all-to-all-start = ((bf16[16,128,128]{2,1,0:T(8,128)(2,1)}), bf16[16,128,128]{2,1,0:T(8,128)(2,1)S(1)}, u32[]{:S(2)}, u32[]{:S(2)}) async-start(bf16[16,128,128]{2,1,0:T(8,128)(2,1)} %bitcast.73), calls=%async_computation | async-start | bytes 1048576 | tf_op jit(solution)/shard_map/all_to_all | solution.py:18
  11.5 1.0 copy-start
  20.6 6.0 %collective-permute-start = (bf16[8,2,2,32,128]{4,3,2,1,0:T(8,128)(2,1)S(1)}, bf16[8,2,2,32,128]{4,3,2,1,0:T(8,128)(2,1)S(1)}, u32[]{:S(2)}, u32[]{:S(2)}) collective-permute-start(bf16[8,2,2,32,128]{4,3,2,1,0:T(8,128)(2,1)S(1)} %dynamic-slice_bitcast_fusion), channel_id=1, source_target_pairs={{0,8},{8,0},{1,9},{9,1},{2,10},{10,2},{3,11},{11,3},{4,12},{12,4},... | collective-permute-start | bytes 786440 | tf_op jit(solution)/shard_map/ppermute | solution.py:272
  21.9 22.6 %all-to-all-start.1 = ((bf16[128,32,128]{2,1,0:T(8,128)(2,1)}), bf16[128,32,128]{2,1,0:T(8,128)(2,1)S(1)}, u32[]{:S(2)}, u32[]{:S(2)}) async-start(bf16[128,32,128]{2,1,0:T(8,128)(2,1)} %pad_maximum_fusion.1), calls=%async_computation.1 | async-start | bytes 2097152 | tf_op jit(solution)/shard_map/all_to_all | solution.py:18
  46.5 18.3 %all-to-all-start.2 = ((bf16[128,16,128]{2,1,0:T(8,128)(2,1)}), bf16[128,16,128]{2,1,0:T(8,128)(2,1)S(1)}, u32[]{:S(2)}, u32[]{:S(2)}) async-start(bf16[128,16,128]{2,1,0:T(8,128)(2,1)} %bitcast.6), calls=%async_computation.2 | async-start | bytes 1048576 | tf_op jit(solution)/shard_map/all_to_all | solution.py:18
  52.5 12.3 %copy-start.3 = (bf16[128,128]{1,0:T(8,128)(2,1)S(1)}, bf16[128,128]{1,0:T(8,128)(2,1)}, u32[]{:S(2)}) copy-start(bf16[128,128]{1,0:T(8,128)(2,1)} %w_ref.1) | copy-start | bytes 98308
  64.8 3.9 %copy-start.8 = (s32[512]{0:T(512)S(1)}, s32[512]{0:T(512)}, u32[]{:S(2)}) copy-start(s32[512]{0:T(512)} %param.11) | copy-start | bytes 6148
  64.8 4.8 %copy-start.9 = (bf16[128,4]{0,1:T(4,128)(2,1)S(1)}, bf16[128,4]{0,1:T(4,128)(2,1)}, u32[]{:S(2)}) copy-start(bf16[128,4]{0,1:T(4,128)(2,1)} %param.15) | copy-start | bytes 3076
  66.4 0.8 copy-start.6
  67.2 3.1 %collective-permute-start.1 = (bf16[16,128,128]{2,1,0:T(8,128)(2,1)S(1)}, bf16[16,128,128]{2,1,0:T(8,128)(2,1)S(1)}, u32[]{:S(2)}, u32[]{:S(2)}) collective-permute-start(bf16[16,128,128]{2,1,0:T(8,128)(2,1)S(1)} %get-tuple-element.17), channel_id=1, source_target_pairs={{0,8},{8,0},{1,9},{9,1},{2,10},{10,2},{3,11},{11,3},{4,12},{12,4},... | collective-permute-start | bytes 1572872 | tf_op jit(solution)/shard_map/ppermute | solution.py:295
  71.8 4.2 %copy-start.10 = (bf16[128,4]{0,1:T(4,128)(2,1)S(1)}, bf16[128,4]{0,1:T(4,128)(2,1)}, u32[]{:S(2)}) copy-start(bf16[128,4]{0,1:T(4,128)(2,1)} %param.18) | copy-start | bytes 3076
  71.8 21.9 %copy-start.2 = (bf16[128,512]{1,0:T(8,128)(2,1)S(1)}, bf16[128,512]{1,0:T(8,128)(2,1)}, u32[]{:S(2)}) copy-start(bf16[128,512]{1,0:T(8,128)(2,1)} %w_in_ref.2) | copy-start | bytes 393220
  71.8 21.9 %copy-start.4 = (bf16[128,128]{1,0:T(8,128)(2,1)S(1)}, bf16[128,128]{1,0:T(8,128)(2,1)}, u32[]{:S(2)}) copy-start(bf16[128,128]{1,0:T(8,128)(2,1)} %w_out_ref.2) | copy-start | bytes 98308
  71.8 21.9 %copy-start.7 = (bf16[16,128,128]{2,1,0:T(8,128)(2,1)S(1)}, bf16[16,128,128]{2,1,0:T(8,128)(2,1)}, u32[]{:S(2)}) copy-start(bf16[16,128,128]{2,1,0:T(8,128)(2,1)} %copy-done.6) | copy-start | bytes 1572868
  71.8 21.9 %all-to-all-start.3 = ((bf16[128,32,128]{2,1,0:T(8,128)(2,1)}), bf16[128,32,128]{2,1,0:T(8,128)(2,1)S(1)}, u32[]{:S(2)}, u32[]{:S(2)}) async-start(bf16[128,32,128]{2,1,0:T(8,128)(2,1)} %bitcast.19), calls=%async_computation.3 | async-start | bytes 2097152 | tf_op jit(solution)/shard_map/all_to_all | solution.py:18
  105.9 33.3 %slice-start = ((bf16[128,512]{1,0:T(8,128)(2,1)}), bf16[128,256]{1,0:T(8,128)(2,1)S(1)}, s32[]{:S(2)}) async-start(bf16[128,512]{1,0:T(8,128)(2,1)} %w_in_ref.3), calls=%async_computation.6 | async-start | bytes 131072 | tf_op jit(solution)/shard_map/slice | solution.py:355
  137.1 3.4 %copy-start.1 = (bf16[128,512]{1,0:T(8,128)(2,1)S(1)}, bf16[128,512]{1,0:T(8,128)(2,1)}, u32[]{:S(2)}) copy-start(bf16[128,512]{1,0:T(8,128)(2,1)} %w_in_ref.3) | copy-start | bytes 393220
  137.1 3.4 %copy-start.5 = (bf16[128,128]{1,0:T(8,128)(2,1)S(1)}, bf16[128,128]{1,0:T(8,128)(2,1)}, u32[]{:S(2)}) copy-start(bf16[128,128]{1,0:T(8,128)(2,1)} %w_out_ref.3) | copy-start | bytes 98308
  137.1 3.4 %collective-permute-start.2 = (bf16[128,16,128]{2,1,0:T(8,128)(2,1)S(1)}, bf16[128,16,128]{2,1,0:T(8,128)(2,1)S(1)}, u32[]{:S(2)}, u32[]{:S(2)}) collective-permute-start(bf16[128,16,128]{2,1,0:T(8,128)(2,1)S(1)} %slice.20), channel_id=1, source_target_pairs={{0,8},{8,0},{1,9},{9,1},{2,10},{10,2},{3,11},{11,3},{4,12},{12,4},... | collective-permute-start | bytes 1572872 | tf_op jit(solution)/shard_map/ppermute | solution.py:337

commit v5 on v4

--- a/solution.py
+++ b/solution.py
@@ -137,29 +137,37 @@
     heads = head_lanes(256)
     ones = jnp.ones((512, 128), bf16)
 
-    def one_row(row, carry):
-        own, other = own_ref[:, row].reshape(256, 128), other_ref[:, row].reshape(256, 128)
-        projected = nn(own, w_in_ref[...])
-        projected_other = nn(other, w_in_ref[:, 128:384])
-        query = (projected[:, :128] * (32 ** (-0.5) * log2e)).astype(bf16)
-        keys = jnp.concatenate([projected[:, 128:256].astype(bf16), projected_other[:, :128].astype(bf16)], axis=0)
-        values = jnp.concatenate([projected[:, 256:384].astype(bf16), projected_other[:, 128:].astype(bf16)], axis=0)
-        values = jnp.concatenate([values, ones], axis=1)
-        gate = jax.nn.sigmoid(projected[:, 384:])
-        queries = jnp.concatenate([jnp.where(lanes, query, jnp.zeros_like(query)) for lanes in heads], axis=0)
-        scores = nt(queries, keys)
-        attended = jnp.zeros((256, 128), f32)
-        for head in range(4):
-            part = scores[head * 256 : head * 256 + 256] + bias_ref[head]
-            weights = jnp.exp2(part - jnp.max(part, axis=1, keepdims=True)).astype(bf16)
-            summed = nn(weights, values)
-            attended = jnp.where(heads[head], summed[:, :128] / summed[:, 128:], attended)
-        update = nn((attended * gate).astype(bf16), w_out_ref[...])
-        result = (pair_ref[:, row].reshape(256, 128).astype(f32) + update).astype(bf16)
-        out_ref[:, row] = result.reshape(2, 128, 128)
+    def two_rows(step, carry):
+        rows = pl.ds(step * 4, 4)
+        projected = nn(own_ref[:, rows].reshape(1024, 128), w_in_ref[...])
+        projected_other = nn(other_ref[:, rows].reshape(1024, 128), w_in_ref[:, 128:384])
+        gated = []
+        for row in range(4):
+            one, two = (
+                jnp.concatenate([whole[row * 128 : row * 128 + 128], whole[512 + row * 128 : 640 + row * 128]], axis=0)
+                for whole in (projected, projected_other)
+            )
+            query = (one[:, :128] * (32 ** (-0.5) * log2e)).astype(bf16)
+            keys = jnp.concatenate([one[:, 128:256], two[:, :128]], axis=0).astype(bf16)
+            values = jnp.concatenate([one[:, 256:384], two[:, 128:]], axis=0).astype(bf16)
+            values = jnp.concatenate([values, ones], axis=1)
+            queries = jnp.concatenate([jnp.where(lanes, query, jnp.zeros_like(query)) for lanes in heads], axis=0)
+            scores = nt(queries, keys)
+            attended = jnp.zeros((256, 128), f32)
+            for head in range(4):
+                part = scores[head * 256 : head * 256 + 256] + bias_ref[head]
+                weights = jnp.exp2(part - jnp.max(part, axis=1, keepdims=True)).astype(bf16)
+                summed = nn(weights, values)
+                attended = jnp.where(heads[head], summed[:, :128] / summed[:, 128:], attended)
+            gated.append((attended * jax.nn.sigmoid(one[:, 384:])).astype(bf16))
+        update = nn(jnp.concatenate(gated, axis=0), w_out_ref[...])
+        for row in range(4):
+            at = step * 4 + row
+            pair = pair_ref[:, at].reshape(256, 128).astype(f32)
+            out_ref[:, at] = (pair + update[row * 256 : row * 256 + 256]).astype(bf16).reshape(2, 128, 128)
         return carry
 
-    lax.fori_loop(0, 8, one_row, 0, unroll=2)
+    lax.fori_loop(0, 2, two_rows, 0)
     for row in range(8):
         normed = layer_norm(out_ref[:, row].reshape(256, 128).astype(f32)).astype(bf16)
         after_ref[row] = nt(next_ref[...], normed)
@@ -209,29 +217,36 @@
             [from_ref[column // 4, pl.ds(column % 4 * 4 + part, 64, stride=16), :] for part in range(4)], axis=0
         )
 
-    def one_column(column, carry):
-        pair = taken(own_ref, column)
-        own = layer_norm(pair).astype(bf16)
-        other = layer_norm(taken(both_ref, column)).astype(bf16)
-        both = jnp.concatenate([own, other], axis=0)
-        query = (nn(own, w_in_ref[:, :128]) * (32 ** (-0.5) * log2e)).astype(bf16)
-        keys = nn(both, w_in_ref[:, 128:256]).astype(bf16)
-        values = nt(w_turned_ref[:128], both).astype(bf16)
-        gate = jax.nn.sigmoid(nt(w_turned_ref[128:], own))
-        stacked = jnp.concatenate([jnp.where(lanes, keys, jnp.zeros_like(keys)) for lanes in heads], axis=0)
-        scores = nt(stacked, query)
-        attended = []
-        for head in range(4):
-            part = scores[head * 512 : head * 512 + 512] + bias_ref[head]
-            weights = jnp.exp2(part - jnp.max(part, axis=0, keepdims=True)).astype(bf16)
-            summed = nn(jnp.concatenate([values[head * 32 : head * 32 + 32], ones], axis=0), weights)
-            attended.append(summed[:32] / summed[32:33])
-        attended = (jnp.concatenate(attended, axis=0) * gate).astype(bf16)
-        update = dot(attended, w_out_ref[...], ((0,), (0,)))
-        out_ref[column] = (pair + update).astype(bf16)
+    def two_columns(step, carry):
+        pair = jnp.concatenate([taken(own_ref, step * 4 + place) for place in range(4)], axis=0)
+        other = jnp.concatenate([taken(both_ref, step * 4 + place) for place in range(4)], axis=0)
+        own, other = layer_norm(pair).astype(bf16), layer_norm(other).astype(bf16)
+        first = nn(own, w_in_ref[:, :256])
+        query = (first[:, :128] * (32 ** (-0.5) * log2e)).astype(bf16)
+        keys_own, keys_other = first[:, 128:].astype(bf16), nn(other, w_in_ref[:, 128:256]).astype(bf16)
+        turned = nt(w_turned_ref[...], own)
+        values_own, values_other = turned[:128].astype(bf16), nt(w_turned_ref[:128], other).astype(bf16)
+        gate = jax.nn.sigmoid(turned[128:])
+        gated = []
+        for place in range(4):
+            at = slice(place * 256, place * 256 + 256)
+            keys = jnp.concatenate([keys_own[at], keys_other[at]], axis=0)
+            values = jnp.concatenate([values_own[:, at], values_other[:, at]], axis=1)
+            stacked = jnp.concatenate([jnp.where(lanes, keys, jnp.zeros_like(keys)) for lanes in heads], axis=0)
+            scores = nt(stacked, query[at])
+            attended = []
+            for head in range(4):
+                part = scores[head * 512 : head * 512 + 512] + bias_ref[head]
+                weights = jnp.exp2(part - jnp.max(part, axis=0, keepdims=True)).astype(bf16)
+                summed = nn(jnp.concatenate([values[head * 32 : head * 32 + 32], ones], axis=0), weights)
+                attended.append(summed[:32] / summed[32:33])
+            gated.append(jnp.concatenate(attended, axis=0))
+        gated = (jnp.concatenate(gated, axis=1) * gate).astype(bf16)
+        result = (pair + dot(gated, w_out_ref[...], ((0,), (0,)))).astype(bf16)
+        out_ref[pl.ds(step * 4, 4)] = result.reshape(4, 256, 128)
         return carry
 
-    lax.fori_loop(0, 8, one_column, 0, unroll=2)
+    lax.fori_loop(0, 2, two_columns, 0)
 
 
 def call(kernel, in_kinds, outs, scratch, flops):

time: 168 us -> 164 us (0.976)
  Pallas kernels: 30.1 us -> 25.9 us
    pallas_call x1, Pallas kernels: 11.2 us -> 9.08 us  [body(): call(start_kernel, 'ssvvvvvvvv', (jax.ShapeDtypeStruct((2, 8, 128, 128),...]
    pallas_call x1, Pallas kernels: 12 us -> 9.96 us  [body(): call(end_kernel, 'svvvvvvv', jax.ShapeDtypeStruct((8, 256, 128), bf16), [...]
where the time goes in v5:
time: 164 us
  waiting for transfers between devices  50.2 us (31%)
  blocking collectives  44.7 us (27%)
  starting transfers between devices  28.3 us (17%)
  Pallas kernels  25.9 us (16%)
  local copies, waits for them, and re-layouts  8.94 us (5%)
  other arithmetic  4.11 us (3%)
    all_to_all x4, waiting for transfers between devices, swap(): return lax.all_to_all(pieces, axes, 0, 0, tiled=True)  48.6 us
    all_to_all x2, blocking collectives, swap(): return lax.all_to_all(pieces, axes, 0, 0, tiled=True)  44.7 us
    all_to_all x4, starting transfers between devices, swap(): return lax.all_to_all(pieces, axes, 0, 0, tiled=True)  23.4 us
    pallas_call x1, Pallas kernels, body(): call(end_kernel, 'svvvvvvv', jax.ShapeDtypeStruct((8, 256, 128), bf16), [...  9.96 us
    pallas_call x1, Pallas kernels, body(): call(start_kernel, 'ssvvvvvvvv', (jax.ShapeDtypeStruct((2, 8, 128, 128),...  9.08 us
  transfers between devices with their start and end apart: 7, of which 6 were waited for; matrix products, arithmetic and copies ran while one was open for 6% of the time, Pallas kernels for 1%

profile of v5, /device:TPU:1, one launch (start us, length us, event | category | flops | bytes accessed | tf_op | source)
XLA Modules:
  0.0 163.7 jit_solution(7739649296770003297)
XLA Ops:
  0.0 9.3 %all-to-all-start = ((bf16[16,128,128]{2,1,0:T(8,128)(2,1)}), bf16[16,128,128]{2,1,0:T(8,128)(2,1)S(1)}, u32[]{:S(2)}, u32[]{:S(2)}) async-start(bf16[16,128,128]{2,1,0:T(8,128)(2,1)} %bitcast.73), calls=%async_computation | async-start | bytes 1048576 | tf_op jit(solution)/shard_map/all_to_all | solution.py:18
  9.3 0.7 convert_element_type.39
  10.1 0.1 copy.86
  10.5 0.9 slice.15.w_in_ref
  11.5 1.0 copy-done
  12.5 1.8 %shard_map.100 = (bf16[128,16,128]{2,1,0:T(8,128)(2,1)S(1)}, bf16[128,16,128]{2,1,0:T(8,128)(2,1)S(1)}) custom-call(bf16[32,64,128]{2,1,0:T(8,128)(2,1)S(1)} %copy-done, bf16[128,512]{1,0:T(8,128)(2,1)S(1)} %slice.15.w_in_ref, f32[8,256]{1,0:T(8,128)S(1)} %mul.70.mask_ref), custom_call_target="tpu_custom_call" | custom-call | flops 300000000 | bytes 4194304 | tf_op jit(solution)/shard_map/pallas_call | solution.py:276
  14.3 1.1 pad_maximum_fusion.1
  15.4 5.2 %all-to-all-done = bf16[16,128,128]{2,1,0:T(8,128)(2,1)S(1)} async-done(((bf16[16,128,128]{2,1,0:T(8,128)(2,1)}), bf16[16,128,128]{2,1,0:T(8,128)(2,1)S(1)}, u32[]{:S(2)}, u32[]{:S(2)}) %all-to-all-start) | async-done | bytes 524320 | tf_op jit(solution)/shard_map/all_to_all | solution.py:18
  20.6 1.2 collective-permute-start
  21.9 4.8 %all-to-all-start.1 = ((bf16[128,32,128]{2,1,0:T(8,128)(2,1)}), bf16[128,32,128]{2,1,0:T(8,128)(2,1)S(1)}, u32[]{:S(2)}, u32[]{:S(2)}) async-start(bf16[128,32,128]{2,1,0:T(8,128)(2,1)} %pad_maximum_fusion.1), calls=%async_computation.1 | async-start | bytes 2097152 | tf_op jit(solution)/shard_map/all_to_all | solution.py:18
  26.7 0.2 copy.72
  26.9 0.2 copy.71
  27.1 0.4 convert_reduce_fusion
  27.5 0.1 copy.75
  27.7 0.1 copy.76
  27.9 0.8 multiply_reduce_fusion
  28.7 0.1 copy.77
  29.1 0.6 copy.74
  29.7 0.2 copy.73
  29.9 14.6 %all-to-all-done.1 = bf16[128,32,128]{2,1,0:T(8,128)(2,1)S(1)} async-done(((bf16[128,32,128]{2,1,0:T(8,128)(2,1)}), bf16[128,32,128]{2,1,0:T(8,128)(2,1)S(1)}, u32[]{:S(2)}, u32[]{:S(2)}) %all-to-all-start.1) | async-done | bytes 1048608 | tf_op jit(solution)/shard_map/all_to_all | solution.py:18
  44.4 2.0 %shard_map.101 = bf16[8,2,8,16,128]{4,3,2,1,0:T(8,128)(2,1)} custom-call(bf16[8,2,8,32,128]{4,3,2,1,0:T(8,128)(2,1)S(1)} %bitcast.71), custom_call_target="tpu_custom_call" | custom-call | flops 300000000 | bytes 4194304 | tf_op jit(solution)/shard_map/pallas_call | solution.py:291
  46.5 5.4 %all-to-all-start.2 = ((bf16[128,16,128]{2,1,0:T(8,128)(2,1)}), bf16[128,16,128]{2,1,0:T(8,128)(2,1)S(1)}, u32[]{:S(2)}, u32[]{:S(2)}) async-start(bf16[128,16,128]{2,1,0:T(8,128)(2,1)} %bitcast.6), calls=%async_computation.2 | async-start | bytes 1048576 | tf_op jit(solution)/shard_map/all_to_all | solution.py:18
  51.9 0.6 fusion.4
  52.5 1.2 fusion.2
  53.7 11.1 %all-to-all-done.2.combined_ref = bf16[128,16,128]{2,1,0:T(8,128)(2,1)S(1)} async-done(((bf16[128,16,128]{2,1,0:T(8,128)(2,1)}), bf16[128,16,128]{2,1,0:T(8,128)(2,1)S(1)}, u32[]{:S(2)}, u32[]{:S(2)}) %all-to-all-start.2) | async-done | bytes 524320 | tf_op jit(solution)/shard_map/all_to_all | solution.py:18
  64.8 1.5 shard_map.102
  66.4 0.8 copy-done.6
  67.2 1.5 collective-permute-start.1
  68.7 0.2 reshape.247
  68.9 0.3 copy.78
  69.3 0.3 copy.80
  69.7 0.5 collective-permute-done.1
  70.2 1.5 shard_map.103
  71.8 4.0 %all-to-all-start.3 = ((bf16[128,32,128]{2,1,0:T(8,128)(2,1)}), bf16[128,32,128]{2,1,0:T(8,128)(2,1)S(1)}, u32[]{:S(2)}, u32[]{:S(2)}) async-start(bf16[128,32,128]{2,1,0:T(8,128)(2,1)} %bitcast.19), calls=%async_computation.3 | async-start | bytes 2097152 | tf_op jit(solution)/shard_map/all_to_all | solution.py:18
  76.0 17.7 %all-to-all-done.3 = bf16[128,32,128]{2,1,0:T(8,128)(2,1)S(1)} async-done(((bf16[128,32,128]{2,1,0:T(8,128)(2,1)}), bf16[128,32,128]{2,1,0:T(8,128)(2,1)S(1)}, u32[]{:S(2)}, u32[]{:S(2)}) %all-to-all-start.3) | async-done | bytes 1048608 | tf_op jit(solution)/shard_map/all_to_all | solution.py:18
  93.7 9.1 %shard_map.104 = (bf16[2,8,128,128]{3,2,1,0:T(8,128)(2,1)S(1)}, f32[2,40,128]{2,1,0:T(8,128)S(1)}) custom-call(s32[1]{0:T(128)} %bitcast.core_ref, s32[8]{0:T(128)S(1)} %reshape.238.kept_ref, bf16[2,8,128,128]{3,2,1,0:T(8,128)(2,1)S(1)} %bitcast.79, bf16[2,8,128,128]{3,2,1,0:T(8,128)(2,1)S(1)} %bitcast.81, bf16[8,2,8,32,128]{4,3,2,1,0:T(8,128)(2,1)S(1)} %bitcast.72, ...), custom_call_target="tpu_custom_call" | custom-call | flops 3000000000 | bytes 4194304 | tf_op jit(solution)/shard_map/pallas_call | solution.py:330
  102.8 0.5 copy.79
  103.3 0.2 broadcast_in_dim.2
  103.5 0.1 pad_maximum_fusion
  103.7 31.2 %all_to_all.30 = bf16[128,56,128]{2,1,0:T(8,128)(2,1)S(1)} all-to-all(bf16[128,56,128]{2,1,0:T(8,128)(2,1)S(1)} %pad_maximum_fusion), channel_id=1, replica_groups=mesh['xl'=2,'y'=4,'core'=2,'z'=4,'xh'=2] {'xl','y','core','z','xh'}, dimensions={0} | all-to-all | bytes 3670016 | tf_op jit(solution)/shard_map/all_to_all | solution.py:18
  135.0 2.1 %collective-permute-start.2 = (bf16[128,16,128]{2,1,0:T(8,128)(2,1)S(1)}, bf16[128,16,128]{2,1,0:T(8,128)(2,1)S(1)}, u32[]{:S(2)}, u32[]{:S(2)}) collective-permute-start(bf16[128,16,128]{2,1,0:T(8,128)(2,1)S(1)} %slice.20), channel_id=1, source_target_pairs={{0,8},{8,0},{1,9},{9,1},{2,10},{10,2},{3,11},{11,3},{4,12},{12,4},... | collective-permute-start | bytes 1572872 | tf_op jit(solution)/shard_map/ppermute | solution.py:352
  137.1 0.1 copy.81
  137.2 0.1 copy.88
  137.5 1.1 collective-permute-done.2
  138.6 10.0 %shard_map.105 = bf16[8,256,128]{2,1,0:T(8,128)(2,1)S(1)} custom-call(s32[1]{0:T(128)} %bitcast.core_ref, bf16[8,2,8,56,128]{4,3,2,1,0:T(8,128)(2,1)S(1)} %bitcast.70, bf16[8,2,8,16,128]{4,3,2,1,0:T(8,128)(2,1)S(1)} %bitcast.82, f32[8,2,8,8,128]{4,3,2,1,0:T(8,128)S(1)} %convert.2.top_ref, f32[512,1]{1,0:T(8,128)S(1)} %broadcast_multiply_fusion.mask_ref, ...), custom_call_target="tpu_custom_call" | custom-call | flops 3000000000 | bytes 4194304 | tf_op jit(solution)/shard_map/pallas_call | solution.py:357
  148.6 0.6 copy.84
  149.2 13.5 %all_to_all.31 = bf16[16,128,128]{2,1,0:T(8,128)(2,1)S(1)} all-to-all(bf16[16,128,128]{2,1,0:T(8,128)(2,1)S(1)} %bitcast.95), channel_id=1, replica_groups=mesh['xl'=2,'y'=4,'core'=2,'z'=4,'xh'=2] {'xl','y','core'}, dimensions={0} | all-to-all | bytes 1048576 | tf_op jit(solution)/shard_map/all_to_all | solution.py:18
  162.6 1.1 copy.85
  (50 shorter events, 1.5 us)
Async XLA Ops:
  0.0 20.6 %all-to-all-start = ((bf16[16,128,128]{2,1,0:T(8,128)(2,1)}), bf16[16,128,128]{2,1,0:T(8,128)(2,1)S(1)}, u32[]{:S(2)}, u32[]{:S(2)}) async-start(bf16[16,128,128]{2,1,0:T(8,128)(2,1)} %bitcast.73), calls=%async_computation | async-start | bytes 1048576 | tf_op jit(solution)/shard_map/all_to_all | solution.py:18
  11.5 1.0 copy-start
  20.6 6.0 %collective-permute-start = (bf16[8,2,2,32,128]{4,3,2,1,0:T(8,128)(2,1)S(1)}, bf16[8,2,2,32,128]{4,3,2,1,0:T(8,128)(2,1)S(1)}, u32[]{:S(2)}, u32[]{:S(2)}) collective-permute-start(bf16[8,2,2,32,128]{4,3,2,1,0:T(8,128)(2,1)S(1)} %dynamic-slice_bitcast_fusion), channel_id=1, source_target_pairs={{0,8},{8,0},{1,9},{9,1},{2,10},{10,2},{3,11},{11,3},{4,12},{12,4},... | collective-permute-start | bytes 786440 | tf_op jit(solution)/shard_map/ppermute | solution.py:287
  21.9 22.6 %all-to-all-start.1 = ((bf16[128,32,128]{2,1,0:T(8,128)(2,1)}), bf16[128,32,128]{2,1,0:T(8,128)(2,1)S(1)}, u32[]{:S(2)}, u32[]{:S(2)}) async-start(bf16[128,32,128]{2,1,0:T(8,128)(2,1)} %pad_maximum_fusion.1), calls=%async_computation.1 | async-start | bytes 2097152 | tf_op jit(solution)/shard_map/all_to_all | solution.py:18
  46.5 18.3 %all-to-all-start.2 = ((bf16[128,16,128]{2,1,0:T(8,128)(2,1)}), bf16[128,16,128]{2,1,0:T(8,128)(2,1)S(1)}, u32[]{:S(2)}, u32[]{:S(2)}) async-start(bf16[128,16,128]{2,1,0:T(8,128)(2,1)} %bitcast.6), calls=%async_computation.2 | async-start | bytes 1048576 | tf_op jit(solution)/shard_map/all_to_all | solution.py:18
  52.5 12.3 %copy-start.3 = (bf16[128,128]{1,0:T(8,128)(2,1)S(1)}, bf16[128,128]{1,0:T(8,128)(2,1)}, u32[]{:S(2)}) copy-start(bf16[128,128]{1,0:T(8,128)(2,1)} %w_ref.1) | copy-start | bytes 98308
  64.8 3.9 %copy-start.8 = (s32[512]{0:T(512)S(1)}, s32[512]{0:T(512)}, u32[]{:S(2)}) copy-start(s32[512]{0:T(512)} %param.11) | copy-start | bytes 6148
  64.8 4.8 %copy-start.9 = (bf16[128,4]{0,1:T(4,128)(2,1)S(1)}, bf16[128,4]{0,1:T(4,128)(2,1)}, u32[]{:S(2)}) copy-start(bf16[128,4]{0,1:T(4,128)(2,1)} %param.15) | copy-start | bytes 3076
  66.4 0.8 copy-start.6
  67.2 3.1 %collective-permute-start.1 = (bf16[16,128,128]{2,1,0:T(8,128)(2,1)S(1)}, bf16[16,128,128]{2,1,0:T(8,128)(2,1)S(1)}, u32[]{:S(2)}, u32[]{:S(2)}) collective-permute-start(bf16[16,128,128]{2,1,0:T(8,128)(2,1)S(1)} %get-tuple-element.17), channel_id=1, source_target_pairs={{0,8},{8,0},{1,9},{9,1},{2,10},{10,2},{3,11},{11,3},{4,12},{12,4},... | collective-permute-start | bytes 1572872 | tf_op jit(solution)/shard_map/ppermute | solution.py:310
  71.8 4.2 %copy-start.10 = (bf16[128,4]{0,1:T(4,128)(2,1)S(1)}, bf16[128,4]{0,1:T(4,128)(2,1)}, u32[]{:S(2)}) copy-start(bf16[128,4]{0,1:T(4,128)(2,1)} %param.18) | copy-start | bytes 3076
  71.8 21.9 %copy-start.2 = (bf16[128,512]{1,0:T(8,128)(2,1)S(1)}, bf16[128,512]{1,0:T(8,128)(2,1)}, u32[]{:S(2)}) copy-start(bf16[128,512]{1,0:T(8,128)(2,1)} %w_in_ref.2) | copy-start | bytes 393220
  71.8 21.9 %copy-start.4 = (bf16[128,128]{1,0:T(8,128)(2,1)S(1)}, bf16[128,128]{1,0:T(8,128)(2,1)}, u32[]{:S(2)}) copy-start(bf16[128,128]{1,0:T(8,128)(2,1)} %w_out_ref.2) | copy-start | bytes 98308
  71.8 21.9 %copy-start.7 = (bf16[16,128,128]{2,1,0:T(8,128)(2,1)S(1)}, bf16[16,128,128]{2,1,0:T(8,128)(2,1)}, u32[]{:S(2)}) copy-start(bf16[16,128,128]{2,1,0:T(8,128)(2,1)} %copy-done.6) | copy-start | bytes 1572868
  71.8 21.9 %all-to-all-start.3 = ((bf16[128,32,128]{2,1,0:T(8,128)(2,1)}), bf16[128,32,128]{2,1,0:T(8,128)(2,1)S(1)}, u32[]{:S(2)}, u32[]{:S(2)}) async-start(bf16[128,32,128]{2,1,0:T(8,128)(2,1)} %bitcast.19), calls=%async_computation.3 | async-start | bytes 2097152 | tf_op jit(solution)/shard_map/all_to_all | solution.py:18
  103.7 33.5 %slice-start = ((bf16[128,512]{1,0:T(8,128)(2,1)}), bf16[128,256]{1,0:T(8,128)(2,1)S(1)}, s32[]{:S(2)}) async-start(bf16[128,512]{1,0:T(8,128)(2,1)} %w_in_ref.3), calls=%async_computation.6 | async-start | bytes 131072 | tf_op jit(solution)/shard_map/slice | solution.py:370
  134.9 3.7 %copy-start.1 = (bf16[128,512]{1,0:T(8,128)(2,1)S(1)}, bf16[128,512]{1,0:T(8,128)(2,1)}, u32[]{:S(2)}) copy-start(bf16[128,512]{1,0:T(8,128)(2,1)} %w_in_ref.3) | copy-start | bytes 393220
  134.9 3.7 %copy-start.5 = (bf16[128,128]{1,0:T(8,128)(2,1)S(1)}, bf16[128,128]{1,0:T(8,128)(2,1)}, u32[]{:S(2)}) copy-start(bf16[128,128]{1,0:T(8,128)(2,1)} %w_out_ref.3) | copy-start | bytes 98308
  135.0 3.6 %collective-permute-start.2 = (bf16[128,16,128]{2,1,0:T(8,128)(2,1)S(1)}, bf16[128,16,128]{2,1,0:T(8,128)(2,1)S(1)}, u32[]{:S(2)}, u32[]{:S(2)}) collective-permute-start(bf16[128,16,128]{2,1,0:T(8,128)(2,1)S(1)} %slice.20), channel_id=1, source_target_pairs={{0,8},{8,0},{1,9},{9,1},{2,10},{10,2},{3,11},{11,3},{4,12},{12,4},... | collective-permute-start | bytes 1572872 | tf_op jit(solution)/shard_map/ppermute | solution.py:352

commit v6 on v5

--- a/solution.py
+++ b/solution.py
@@ -138,13 +138,13 @@
     ones = jnp.ones((512, 128), bf16)
 
     def two_rows(step, carry):
-        rows = pl.ds(step * 4, 4)
-        projected = nn(own_ref[:, rows].reshape(1024, 128), w_in_ref[...])
-        projected_other = nn(other_ref[:, rows].reshape(1024, 128), w_in_ref[:, 128:384])
+        rows = pl.ds(step * 8, 8)
+        projected = nn(own_ref[:, rows].reshape(2048, 128), w_in_ref[...])
+        projected_other = nn(other_ref[:, rows].reshape(2048, 128), w_in_ref[:, 128:384])
         gated = []
-        for row in range(4):
+        for row in range(8):
             one, two = (
-                jnp.concatenate([whole[row * 128 : row * 128 + 128], whole[512 + row * 128 : 640 + row * 128]], axis=0)
+                jnp.concatenate([whole[row * 128 : row * 128 + 128], whole[1024 + row * 128 : 1152 + row * 128]], axis=0)
                 for whole in (projected, projected_other)
             )
             query = (one[:, :128] * (32 ** (-0.5) * log2e)).astype(bf16)
@@ -161,13 +161,13 @@
                 attended = jnp.where(heads[head], summed[:, :128] / summed[:, 128:], attended)
             gated.append((attended * jax.nn.sigmoid(one[:, 384:])).astype(bf16))
         update = nn(jnp.concatenate(gated, axis=0), w_out_ref[...])
-        for row in range(4):
-            at = step * 4 + row
+        for row in range(8):
+            at = step * 8 + row
             pair = pair_ref[:, at].reshape(256, 128).astype(f32)
             out_ref[:, at] = (pair + update[row * 256 : row * 256 + 256]).astype(bf16).reshape(2, 128, 128)
         return carry
 
-    lax.fori_loop(0, 2, two_rows, 0)
+    lax.fori_loop(0, 1, two_rows, 0)
     for row in range(8):
         normed = layer_norm(out_ref[:, row].reshape(256, 128).astype(f32)).astype(bf16)
         after_ref[row] = nt(next_ref[...], normed)
@@ -218,8 +218,8 @@
         )
 
     def two_columns(step, carry):
-        pair = jnp.concatenate([taken(own_ref, step * 4 + place) for place in range(4)], axis=0)
-        other = jnp.concatenate([taken(both_ref, step * 4 + place) for place in range(4)], axis=0)
+        pair = jnp.concatenate([taken(own_ref, step * 8 + place) for place in range(8)], axis=0)
+        other = jnp.concatenate([taken(both_ref, step * 8 + place) for place in range(8)], axis=0)
         own, other = layer_norm(pair).astype(bf16), layer_norm(other).astype(bf16)
         first = nn(own, w_in_ref[:, :256])
         query = (first[:, :128] * (32 ** (-0.5) * log2e)).astype(bf16)
@@ -228,7 +228,7 @@
         values_own, values_other = turned[:128].astype(bf16), nt(w_turned_ref[:128], other).astype(bf16)
         gate = jax.nn.sigmoid(turned[128:])
         gated = []
-        for place in range(4):
+        for place in range(8):
             at = slice(place * 256, place * 256 + 256)
             keys = jnp.concatenate([keys_own[at], keys_other[at]], axis=0)
             values = jnp.concatenate([values_own[:, at], values_other[:, at]], axis=1)
@@ -243,10 +243,10 @@
             gated.append(jnp.concatenate(attended, axis=0))
         gated = (jnp.concatenate(gated, axis=1) * gate).astype(bf16)
         result = (pair + dot(gated, w_out_ref[...], ((0,), (0,)))).astype(bf16)
-        out_ref[pl.ds(step * 4, 4)] = result.reshape(4, 256, 128)
+        out_ref[pl.ds(step * 8, 8)] = result.reshape(8, 256, 128)
         return carry
 
-    lax.fori_loop(0, 2, two_columns, 0)
+    lax.fori_loop(0, 1, two_columns, 0)
 
 
 def call(kernel, in_kinds, outs, scratch, flops):

time: 164 us -> 163 us (level)
  Pallas kernels: 25.9 us -> 24.2 us
where the time goes in v6:
time: 163 us; the launch traced here: 162 us
  waiting for transfers between devices  50.2 us (31%)
  blocking collectives  44.7 us (27%)
  starting transfers between devices  28.3 us (17%)
  Pallas kernels  24.2 us (15%)
  local copies, waits for them, and re-layouts  8.94 us (5%)
  other arithmetic  4.11 us (3%)
    all_to_all x4, waiting for transfers between devices, swap(): return lax.all_to_all(pieces, axes, 0, 0, tiled=True)  48.6 us
    all_to_all x2, blocking collectives, swap(): return lax.all_to_all(pieces, axes, 0, 0, tiled=True)  44.7 us
    all_to_all x4, starting transfers between devices, swap(): return lax.all_to_all(pieces, axes, 0, 0, tiled=True)  23.4 us
    pallas_call x1, Pallas kernels, body(): call(end_kernel, 'svvvvvvv', jax.ShapeDtypeStruct((8, 256, 128), bf16), [...  9.23 us
    pallas_call x1, Pallas kernels, body(): call(start_kernel, 'ssvvvvvvvv', (jax.ShapeDtypeStruct((2, 8, 128, 128),...  8.12 us
  transfers between devices with their start and end apart: 7, of which 6 were waited for; matrix products, arithmetic and copies ran while one was open for 6% of the time, Pallas kernels for 1%

profile of v6, /device:TPU:1, one launch (start us, length us, event | category | flops | bytes accessed | tf_op | source)
XLA Modules:
  0.0 162.0 jit_solution(1855825012426925263)
XLA Ops:
  0.0 9.3 %all-to-all-start = ((bf16[16,128,128]{2,1,0:T(8,128)(2,1)}), bf16[16,128,128]{2,1,0:T(8,128)(2,1)S(1)}, u32[]{:S(2)}, u32[]{:S(2)}) async-start(bf16[16,128,128]{2,1,0:T(8,128)(2,1)} %bitcast.73), calls=%async_computation | async-start | bytes 1048576 | tf_op jit(solution)/shard_map/all_to_all | solution.py:18
  9.3 0.7 convert_element_type.39
  10.1 0.1 copy.86
  10.5 0.9 slice.15.w_in_ref
  11.5 1.0 copy-done
  12.5 1.8 %shard_map.100 = (bf16[128,16,128]{2,1,0:T(8,128)(2,1)S(1)}, bf16[128,16,128]{2,1,0:T(8,128)(2,1)S(1)}) custom-call(bf16[32,64,128]{2,1,0:T(8,128)(2,1)S(1)} %copy-done, bf16[128,512]{1,0:T(8,128)(2,1)S(1)} %slice.15.w_in_ref, f32[8,256]{1,0:T(8,128)S(1)} %mul.70.mask_ref), custom_call_target="tpu_custom_call" | custom-call | flops 300000000 | bytes 4194304 | tf_op jit(solution)/shard_map/pallas_call | solution.py:276
  14.3 1.1 pad_maximum_fusion.1
  15.4 5.2 %all-to-all-done = bf16[16,128,128]{2,1,0:T(8,128)(2,1)S(1)} async-done(((bf16[16,128,128]{2,1,0:T(8,128)(2,1)}), bf16[16,128,128]{2,1,0:T(8,128)(2,1)S(1)}, u32[]{:S(2)}, u32[]{:S(2)}) %all-to-all-start) | async-done | bytes 524320 | tf_op jit(solution)/shard_map/all_to_all | solution.py:18
  20.6 1.2 collective-permute-start
  21.9 4.8 %all-to-all-start.1 = ((bf16[128,32,128]{2,1,0:T(8,128)(2,1)}), bf16[128,32,128]{2,1,0:T(8,128)(2,1)S(1)}, u32[]{:S(2)}, u32[]{:S(2)}) async-start(bf16[128,32,128]{2,1,0:T(8,128)(2,1)} %pad_maximum_fusion.1), calls=%async_computation.1 | async-start | bytes 2097152 | tf_op jit(solution)/shard_map/all_to_all | solution.py:18
  26.7 0.2 copy.72
  26.9 0.2 copy.71
  27.1 0.4 convert_reduce_fusion
  27.5 0.1 copy.75
  27.7 0.1 copy.76
  27.9 0.8 multiply_reduce_fusion
  28.7 0.1 copy.77
  29.1 0.6 copy.74
  29.7 0.2 copy.73
  29.9 14.6 %all-to-all-done.1 = bf16[128,32,128]{2,1,0:T(8,128)(2,1)S(1)} async-done(((bf16[128,32,128]{2,1,0:T(8,128)(2,1)}), bf16[128,32,128]{2,1,0:T(8,128)(2,1)S(1)}, u32[]{:S(2)}, u32[]{:S(2)}) %all-to-all-start.1) | async-done | bytes 1048608 | tf_op jit(solution)/shard_map/all_to_all | solution.py:18
  44.4 2.0 %shard_map.101 = bf16[8,2,8,16,128]{4,3,2,1,0:T(8,128)(2,1)} custom-call(bf16[8,2,8,32,128]{4,3,2,1,0:T(8,128)(2,1)S(1)} %bitcast.71), custom_call_target="tpu_custom_call" | custom-call | flops 300000000 | bytes 4194304 | tf_op jit(solution)/shard_map/pallas_call | solution.py:291
  46.5 5.4 %all-to-all-start.2 = ((bf16[128,16,128]{2,1,0:T(8,128)(2,1)}), bf16[128,16,128]{2,1,0:T(8,128)(2,1)S(1)}, u32[]{:S(2)}, u32[]{:S(2)}) async-start(bf16[128,16,128]{2,1,0:T(8,128)(2,1)} %bitcast.6), calls=%async_computation.2 | async-start | bytes 1048576 | tf_op jit(solution)/shard_map/all_to_all | solution.py:18
  51.9 0.6 fusion.4
  52.5 1.2 fusion.2
  53.7 11.1 %all-to-all-done.2.combined_ref = bf16[128,16,128]{2,1,0:T(8,128)(2,1)S(1)} async-done(((bf16[128,16,128]{2,1,0:T(8,128)(2,1)}), bf16[128,16,128]{2,1,0:T(8,128)(2,1)S(1)}, u32[]{:S(2)}, u32[]{:S(2)}) %all-to-all-start.2) | async-done | bytes 524320 | tf_op jit(solution)/shard_map/all_to_all | solution.py:18
  64.8 1.5 shard_map.102
  66.4 0.8 copy-done.6
  67.2 1.5 collective-permute-start.1
  68.7 0.2 reshape.247
  68.9 0.3 copy.78
  69.3 0.3 copy.80
  69.7 0.5 collective-permute-done.1
  70.2 1.5 shard_map.103
  71.8 4.0 %all-to-all-start.3 = ((bf16[128,32,128]{2,1,0:T(8,128)(2,1)}), bf16[128,32,128]{2,1,0:T(8,128)(2,1)S(1)}, u32[]{:S(2)}, u32[]{:S(2)}) async-start(bf16[128,32,128]{2,1,0:T(8,128)(2,1)} %bitcast.19), calls=%async_computation.3 | async-start | bytes 2097152 | tf_op jit(solution)/shard_map/all_to_all | solution.py:18
  76.0 17.7 %all-to-all-done.3 = bf16[128,32,128]{2,1,0:T(8,128)(2,1)S(1)} async-done(((bf16[128,32,128]{2,1,0:T(8,128)(2,1)}), bf16[128,32,128]{2,1,0:T(8,128)(2,1)S(1)}, u32[]{:S(2)}, u32[]{:S(2)}) %all-to-all-start.3) | async-done | bytes 1048608 | tf_op jit(solution)/shard_map/all_to_all | solution.py:18
  93.7 8.1 %shard_map.104 = (bf16[2,8,128,128]{3,2,1,0:T(8,128)(2,1)S(1)}, f32[2,40,128]{2,1,0:T(8,128)S(1)}) custom-call(s32[1]{0:T(128)} %bitcast.core_ref, s32[8]{0:T(128)S(1)} %reshape.238.kept_ref, bf16[2,8,128,128]{3,2,1,0:T(8,128)(2,1)S(1)} %bitcast.79, bf16[2,8,128,128]{3,2,1,0:T(8,128)(2,1)S(1)} %bitcast.81, bf16[8,2,8,32,128]{4,3,2,1,0:T(8,128)(2,1)S(1)} %bitcast.72, ...), custom_call_target="tpu_custom_call" | custom-call | flops 3000000000 | bytes 4194304 | tf_op jit(solution)/shard_map/pallas_call | solution.py:330
  101.8 0.5 copy.79
  102.4 0.2 broadcast_in_dim.2
  102.6 0.1 pad_maximum_fusion
  102.8 31.2 %all_to_all.30 = bf16[128,56,128]{2,1,0:T(8,128)(2,1)S(1)} all-to-all(bf16[128,56,128]{2,1,0:T(8,128)(2,1)S(1)} %pad_maximum_fusion), channel_id=1, replica_groups=mesh['xl'=2,'y'=4,'core'=2,'z'=4,'xh'=2] {'xl','y','core','z','xh'}, dimensions={0} | all-to-all | bytes 3670016 | tf_op jit(solution)/shard_map/all_to_all | solution.py:18
  134.0 2.1 %collective-permute-start.2 = (bf16[128,16,128]{2,1,0:T(8,128)(2,1)S(1)}, bf16[128,16,128]{2,1,0:T(8,128)(2,1)S(1)}, u32[]{:S(2)}, u32[]{:S(2)}) collective-permute-start(bf16[128,16,128]{2,1,0:T(8,128)(2,1)S(1)} %slice.20), channel_id=1, source_target_pairs={{0,8},{8,0},{1,9},{9,1},{2,10},{10,2},{3,11},{11,3},{4,12},{12,4},... | collective-permute-start | bytes 1572872 | tf_op jit(solution)/shard_map/ppermute | solution.py:352
  136.1 0.1 copy.81
  136.3 0.1 copy.88
  136.5 1.1 collective-permute-done.2
  137.6 9.2 %shard_map.105 = bf16[8,256,128]{2,1,0:T(8,128)(2,1)S(1)} custom-call(s32[1]{0:T(128)} %bitcast.core_ref, bf16[8,2,8,56,128]{4,3,2,1,0:T(8,128)(2,1)S(1)} %bitcast.70, bf16[8,2,8,16,128]{4,3,2,1,0:T(8,128)(2,1)S(1)} %bitcast.82, f32[8,2,8,8,128]{4,3,2,1,0:T(8,128)S(1)} %convert.2.top_ref, f32[512,1]{1,0:T(8,128)S(1)} %broadcast_multiply_fusion.mask_ref, ...), custom_call_target="tpu_custom_call" | custom-call | flops 3000000000 | bytes 4194304 | tf_op jit(solution)/shard_map/pallas_call | solution.py:357
  146.9 0.6 copy.84
  147.5 13.5 %all_to_all.31 = bf16[16,128,128]{2,1,0:T(8,128)(2,1)S(1)} all-to-all(bf16[16,128,128]{2,1,0:T(8,128)(2,1)S(1)} %bitcast.95), channel_id=1, replica_groups=mesh['xl'=2,'y'=4,'core'=2,'z'=4,'xh'=2] {'xl','y','core'}, dimensions={0} | all-to-all | bytes 1048576 | tf_op jit(solution)/shard_map/all_to_all | solution.py:18
  160.9 1.1 copy.85
  (50 shorter events, 1.5 us)
Async XLA Ops:
  0.0 20.6 %all-to-all-start = ((bf16[16,128,128]{2,1,0:T(8,128)(2,1)}), bf16[16,128,128]{2,1,0:T(8,128)(2,1)S(1)}, u32[]{:S(2)}, u32[]{:S(2)}) async-start(bf16[16,128,128]{2,1,0:T(8,128)(2,1)} %bitcast.73), calls=%async_computation | async-start | bytes 1048576 | tf_op jit(solution)/shard_map/all_to_all | solution.py:18
  11.5 1.0 copy-start
  20.6 6.0 %collective-permute-start = (bf16[8,2,2,32,128]{4,3,2,1,0:T(8,128)(2,1)S(1)}, bf16[8,2,2,32,128]{4,3,2,1,0:T(8,128)(2,1)S(1)}, u32[]{:S(2)}, u32[]{:S(2)}) collective-permute-start(bf16[8,2,2,32,128]{4,3,2,1,0:T(8,128)(2,1)S(1)} %dynamic-slice_bitcast_fusion), channel_id=1, source_target_pairs={{0,8},{8,0},{1,9},{9,1},{2,10},{10,2},{3,11},{11,3},{4,12},{12,4},... | collective-permute-start | bytes 786440 | tf_op jit(solution)/shard_map/ppermute | solution.py:287
  21.9 22.6 %all-to-all-start.1 = ((bf16[128,32,128]{2,1,0:T(8,128)(2,1)}), bf16[128,32,128]{2,1,0:T(8,128)(2,1)S(1)}, u32[]{:S(2)}, u32[]{:S(2)}) async-start(bf16[128,32,128]{2,1,0:T(8,128)(2,1)} %pad_maximum_fusion.1), calls=%async_computation.1 | async-start | bytes 2097152 | tf_op jit(solution)/shard_map/all_to_all | solution.py:18
  46.5 18.3 %all-to-all-start.2 = ((bf16[128,16,128]{2,1,0:T(8,128)(2,1)}), bf16[128,16,128]{2,1,0:T(8,128)(2,1)S(1)}, u32[]{:S(2)}, u32[]{:S(2)}) async-start(bf16[128,16,128]{2,1,0:T(8,128)(2,1)} %bitcast.6), calls=%async_computation.2 | async-start | bytes 1048576 | tf_op jit(solution)/shard_map/all_to_all | solution.py:18
  52.5 12.3 %copy-start.3 = (bf16[128,128]{1,0:T(8,128)(2,1)S(1)}, bf16[128,128]{1,0:T(8,128)(2,1)}, u32[]{:S(2)}) copy-start(bf16[128,128]{1,0:T(8,128)(2,1)} %w_ref.1) | copy-start | bytes 98308
  64.8 3.9 %copy-start.8 = (s32[512]{0:T(512)S(1)}, s32[512]{0:T(512)}, u32[]{:S(2)}) copy-start(s32[512]{0:T(512)} %param.11) | copy-start | bytes 6148
  64.8 4.8 %copy-start.9 = (bf16[128,4]{0,1:T(4,128)(2,1)S(1)}, bf16[128,4]{0,1:T(4,128)(2,1)}, u32[]{:S(2)}) copy-start(bf16[128,4]{0,1:T(4,128)(2,1)} %param.15) | copy-start | bytes 3076
  66.4 0.8 copy-start.6
  67.2 3.1 %collective-permute-start.1 = (bf16[16,128,128]{2,1,0:T(8,128)(2,1)S(1)}, bf16[16,128,128]{2,1,0:T(8,128)(2,1)S(1)}, u32[]{:S(2)}, u32[]{:S(2)}) collective-permute-start(bf16[16,128,128]{2,1,0:T(8,128)(2,1)S(1)} %get-tuple-element.17), channel_id=1, source_target_pairs={{0,8},{8,0},{1,9},{9,1},{2,10},{10,2},{3,11},{11,3},{4,12},{12,4},... | collective-permute-start | bytes 1572872 | tf_op jit(solution)/shard_map/ppermute | solution.py:310
  71.8 4.2 %copy-start.10 = (bf16[128,4]{0,1:T(4,128)(2,1)S(1)}, bf16[128,4]{0,1:T(4,128)(2,1)}, u32[]{:S(2)}) copy-start(bf16[128,4]{0,1:T(4,128)(2,1)} %param.18) | copy-start | bytes 3076
  71.8 21.9 %copy-start.2 = (bf16[128,512]{1,0:T(8,128)(2,1)S(1)}, bf16[128,512]{1,0:T(8,128)(2,1)}, u32[]{:S(2)}) copy-start(bf16[128,512]{1,0:T(8,128)(2,1)} %w_in_ref.2) | copy-start | bytes 393220
  71.8 21.9 %copy-start.4 = (bf16[128,128]{1,0:T(8,128)(2,1)S(1)}, bf16[128,128]{1,0:T(8,128)(2,1)}, u32[]{:S(2)}) copy-start(bf16[128,128]{1,0:T(8,128)(2,1)} %w_out_ref.2) | copy-start | bytes 98308
  71.8 21.9 %copy-start.7 = (bf16[16,128,128]{2,1,0:T(8,128)(2,1)S(1)}, bf16[16,128,128]{2,1,0:T(8,128)(2,1)}, u32[]{:S(2)}) copy-start(bf16[16,128,128]{2,1,0:T(8,128)(2,1)} %copy-done.6) | copy-start | bytes 1572868
  71.8 21.9 %all-to-all-start.3 = ((bf16[128,32,128]{2,1,0:T(8,128)(2,1)}), bf16[128,32,128]{2,1,0:T(8,128)(2,1)S(1)}, u32[]{:S(2)}, u32[]{:S(2)}) async-start(bf16[128,32,128]{2,1,0:T(8,128)(2,1)} %bitcast.19), calls=%async_computation.3 | async-start | bytes 2097152 | tf_op jit(solution)/shard_map/all_to_all | solution.py:18
  102.7 33.5 %slice-start = ((bf16[128,512]{1,0:T(8,128)(2,1)}), bf16[128,256]{1,0:T(8,128)(2,1)S(1)}, s32[]{:S(2)}) async-start(bf16[128,512]{1,0:T(8,128)(2,1)} %w_in_ref.3), calls=%async_computation.6 | async-start | bytes 131072 | tf_op jit(solution)/shard_map/slice | solution.py:370
  134.0 3.7 %copy-start.1 = (bf16[128,512]{1,0:T(8,128)(2,1)S(1)}, bf16[128,512]{1,0:T(8,128)(2,1)}, u32[]{:S(2)}) copy-start(bf16[128,512]{1,0:T(8,128)(2,1)} %w_in_ref.3) | copy-start | bytes 393220
  134.0 3.7 %copy-start.5 = (bf16[128,128]{1,0:T(8,128)(2,1)S(1)}, bf16[128,128]{1,0:T(8,128)(2,1)}, u32[]{:S(2)}) copy-start(bf16[128,128]{1,0:T(8,128)(2,1)} %w_out_ref.3) | copy-start | bytes 98308
  134.0 3.6 %collective-permute-start.2 = (bf16[128,16,128]{2,1,0:T(8,128)(2,1)S(1)}, bf16[128,16,128]{2,1,0:T(8,128)(2,1)S(1)}, u32[]{:S(2)}, u32[]{:S(2)}) collective-permute-start(bf16[128,16,128]{2,1,0:T(8,128)(2,1)S(1)} %slice.20), channel_id=1, source_target_pairs={{0,8},{8,0},{1,9},{9,1},{2,10},{10,2},{3,11},{11,3},{4,12},{12,4},... | collective-permute-start | bytes 1572872 | tf_op jit(solution)/shard_map/ppermute | solution.py:352

commit v7 on v6

--- a/solution.py
+++ b/solution.py
@@ -156,7 +156,7 @@
             attended = jnp.zeros((256, 128), f32)
             for head in range(4):
                 part = scores[head * 256 : head * 256 + 256] + bias_ref[head]
-                weights = jnp.exp2(part - jnp.max(part, axis=1, keepdims=True)).astype(bf16)
+                weights = jnp.exp2((part - jnp.max(part, axis=1, keepdims=True)).astype(bf16))
                 summed = nn(weights, values)
                 attended = jnp.where(heads[head], summed[:, :128] / summed[:, 128:], attended)
             gated.append((attended * jax.nn.sigmoid(one[:, 384:])).astype(bf16))
@@ -237,7 +237,7 @@
             attended = []
             for head in range(4):
                 part = scores[head * 512 : head * 512 + 512] + bias_ref[head]
-                weights = jnp.exp2(part - jnp.max(part, axis=0, keepdims=True)).astype(bf16)
+                weights = jnp.exp2((part - jnp.max(part, axis=0, keepdims=True)).astype(bf16))
                 summed = nn(jnp.concatenate([values[head * 32 : head * 32 + 32], ones], axis=0), weights)
                 attended.append(summed[:32] / summed[32:33])
             gated.append(jnp.concatenate(attended, axis=0))

time: 163 us -> 162 us (level)
  no operation moved by 1% of the time
where the time goes in v7:
time: 162 us
  waiting for transfers between devices  50.2 us (31%)
  blocking collectives  44.7 us (28%)
  starting transfers between devices  28.3 us (17%)
  Pallas kernels  23.8 us (15%)
  local copies, waits for them, and re-layouts  8.94 us (6%)
  other arithmetic  4.11 us (3%)
    all_to_all x4, waiting for transfers between devices, swap(): return lax.all_to_all(pieces, axes, 0, 0, tiled=True)  48.6 us
    all_to_all x2, blocking collectives, swap(): return lax.all_to_all(pieces, axes, 0, 0, tiled=True)  44.7 us
    all_to_all x4, starting transfers between devices, swap(): return lax.all_to_all(pieces, axes, 0, 0, tiled=True)  23.4 us
    pallas_call x1, Pallas kernels, body(): call(end_kernel, 'svvvvvvv', jax.ShapeDtypeStruct((8, 256, 128), bf16), [...  8.96 us
    pallas_call x1, Pallas kernels, body(): call(start_kernel, 'ssvvvvvvvv', (jax.ShapeDtypeStruct((2, 8, 128, 128),...  7.94 us
  transfers between devices with their start and end apart: 7, of which 6 were waited for; matrix products, arithmetic and copies ran while one was open for 6% of the time, Pallas kernels for 1%

profile of v7, /device:TPU:1, one launch (start us, length us, event | category | flops | bytes accessed | tf_op | source)
XLA Modules:
  0.0 161.6 jit_solution(8061140873909053669)
XLA Ops:
  0.0 9.3 %all-to-all-start = ((bf16[16,128,128]{2,1,0:T(8,128)(2,1)}), bf16[16,128,128]{2,1,0:T(8,128)(2,1)S(1)}, u32[]{:S(2)}, u32[]{:S(2)}) async-start(bf16[16,128,128]{2,1,0:T(8,128)(2,1)} %bitcast.73), calls=%async_computation | async-start | bytes 1048576 | tf_op jit(solution)/shard_map/all_to_all | solution.py:18
  9.3 0.7 convert_element_type.39
  10.1 0.1 copy.86
  10.5 0.9 slice.15.w_in_ref
  11.5 1.0 copy-done
  12.5 1.8 %shard_map.100 = (bf16[128,16,128]{2,1,0:T(8,128)(2,1)S(1)}, bf16[128,16,128]{2,1,0:T(8,128)(2,1)S(1)}) custom-call(bf16[32,64,128]{2,1,0:T(8,128)(2,1)S(1)} %copy-done, bf16[128,512]{1,0:T(8,128)(2,1)S(1)} %slice.15.w_in_ref, f32[8,256]{1,0:T(8,128)S(1)} %mul.70.mask_ref), custom_call_target="tpu_custom_call" | custom-call | flops 300000000 | bytes 4194304 | tf_op jit(solution)/shard_map/pallas_call | solution.py:276
  14.3 1.1 pad_maximum_fusion.1
  15.4 5.2 %all-to-all-done = bf16[16,128,128]{2,1,0:T(8,128)(2,1)S(1)} async-done(((bf16[16,128,128]{2,1,0:T(8,128)(2,1)}), bf16[16,128,128]{2,1,0:T(8,128)(2,1)S(1)}, u32[]{:S(2)}, u32[]{:S(2)}) %all-to-all-start) | async-done | bytes 524320 | tf_op jit(solution)/shard_map/all_to_all | solution.py:18
  20.6 1.2 collective-permute-start
  21.9 4.8 %all-to-all-start.1 = ((bf16[128,32,128]{2,1,0:T(8,128)(2,1)}), bf16[128,32,128]{2,1,0:T(8,128)(2,1)S(1)}, u32[]{:S(2)}, u32[]{:S(2)}) async-start(bf16[128,32,128]{2,1,0:T(8,128)(2,1)} %pad_maximum_fusion.1), calls=%async_computation.1 | async-start | bytes 2097152 | tf_op jit(solution)/shard_map/all_to_all | solution.py:18
  26.7 0.2 copy.72
  26.9 0.2 copy.71
  27.1 0.4 convert_reduce_fusion
  27.5 0.1 copy.75
  27.7 0.1 copy.76
  27.9 0.8 multiply_reduce_fusion
  28.7 0.1 copy.77
  29.1 0.6 copy.74
  29.7 0.2 copy.73
  29.9 14.6 %all-to-all-done.1 = bf16[128,32,128]{2,1,0:T(8,128)(2,1)S(1)} async-done(((bf16[128,32,128]{2,1,0:T(8,128)(2,1)}), bf16[128,32,128]{2,1,0:T(8,128)(2,1)S(1)}, u32[]{:S(2)}, u32[]{:S(2)}) %all-to-all-start.1) | async-done | bytes 1048608 | tf_op jit(solution)/shard_map/all_to_all | solution.py:18
  44.4 2.0 %shard_map.101 = bf16[8,2,8,16,128]{4,3,2,1,0:T(8,128)(2,1)} custom-call(bf16[8,2,8,32,128]{4,3,2,1,0:T(8,128)(2,1)S(1)} %bitcast.71), custom_call_target="tpu_custom_call" | custom-call | flops 300000000 | bytes 4194304 | tf_op jit(solution)/shard_map/pallas_call | solution.py:291
  46.5 5.4 %all-to-all-start.2 = ((bf16[128,16,128]{2,1,0:T(8,128)(2,1)}), bf16[128,16,128]{2,1,0:T(8,128)(2,1)S(1)}, u32[]{:S(2)}, u32[]{:S(2)}) async-start(bf16[128,16,128]{2,1,0:T(8,128)(2,1)} %bitcast.6), calls=%async_computation.2 | async-start | bytes 1048576 | tf_op jit(solution)/shard_map/all_to_all | solution.py:18
  51.9 0.6 fusion.4
  52.5 1.2 fusion.2
  53.7 11.1 %all-to-all-done.2.combined_ref = bf16[128,16,128]{2,1,0:T(8,128)(2,1)S(1)} async-done(((bf16[128,16,128]{2,1,0:T(8,128)(2,1)}), bf16[128,16,128]{2,1,0:T(8,128)(2,1)S(1)}, u32[]{:S(2)}, u32[]{:S(2)}) %all-to-all-start.2) | async-done | bytes 524320 | tf_op jit(solution)/shard_map/all_to_all | solution.py:18
  64.8 1.5 shard_map.102
  66.4 0.8 copy-done.6
  67.2 1.5 collective-permute-start.1
  68.7 0.2 reshape.247
  68.9 0.3 copy.78
  69.3 0.3 copy.80
  69.7 0.5 collective-permute-done.1
  70.2 1.5 shard_map.103
  71.8 4.0 %all-to-all-start.3 = ((bf16[128,32,128]{2,1,0:T(8,128)(2,1)}), bf16[128,32,128]{2,1,0:T(8,128)(2,1)S(1)}, u32[]{:S(2)}, u32[]{:S(2)}) async-start(bf16[128,32,128]{2,1,0:T(8,128)(2,1)} %bitcast.19), calls=%async_computation.3 | async-start | bytes 2097152 | tf_op jit(solution)/shard_map/all_to_all | solution.py:18
  76.0 17.7 %all-to-all-done.3 = bf16[128,32,128]{2,1,0:T(8,128)(2,1)S(1)} async-done(((bf16[128,32,128]{2,1,0:T(8,128)(2,1)}), bf16[128,32,128]{2,1,0:T(8,128)(2,1)S(1)}, u32[]{:S(2)}, u32[]{:S(2)}) %all-to-all-start.3) | async-done | bytes 1048608 | tf_op jit(solution)/shard_map/all_to_all | solution.py:18
  93.7 7.9 %shard_map.104 = (bf16[2,8,128,128]{3,2,1,0:T(8,128)(2,1)S(1)}, f32[2,40,128]{2,1,0:T(8,128)S(1)}) custom-call(s32[1]{0:T(128)} %bitcast.core_ref, s32[8]{0:T(128)S(1)} %reshape.238.kept_ref, bf16[2,8,128,128]{3,2,1,0:T(8,128)(2,1)S(1)} %bitcast.79, bf16[2,8,128,128]{3,2,1,0:T(8,128)(2,1)S(1)} %bitcast.81, bf16[8,2,8,32,128]{4,3,2,1,0:T(8,128)(2,1)S(1)} %bitcast.72, ...), custom_call_target="tpu_custom_call" | custom-call | flops 3000000000 | bytes 4194304 | tf_op jit(solution)/shard_map/pallas_call | solution.py:330
  101.6 0.5 copy.79
  102.2 0.2 broadcast_in_dim.2
  102.4 0.1 pad_maximum_fusion
  102.6 31.2 %all_to_all.30 = bf16[128,56,128]{2,1,0:T(8,128)(2,1)S(1)} all-to-all(bf16[128,56,128]{2,1,0:T(8,128)(2,1)S(1)} %pad_maximum_fusion), channel_id=1, replica_groups=mesh['xl'=2,'y'=4,'core'=2,'z'=4,'xh'=2] {'xl','y','core','z','xh'}, dimensions={0} | all-to-all | bytes 3670016 | tf_op jit(solution)/shard_map/all_to_all | solution.py:18
  133.8 2.1 %collective-permute-start.2 = (bf16[128,16,128]{2,1,0:T(8,128)(2,1)S(1)}, bf16[128,16,128]{2,1,0:T(8,128)(2,1)S(1)}, u32[]{:S(2)}, u32[]{:S(2)}) collective-permute-start(bf16[128,16,128]{2,1,0:T(8,128)(2,1)S(1)} %slice.20), channel_id=1, source_target_pairs={{0,8},{8,0},{1,9},{9,1},{2,10},{10,2},{3,11},{11,3},{4,12},{12,4},... | collective-permute-start | bytes 1572872 | tf_op jit(solution)/shard_map/ppermute | solution.py:352
  135.9 0.1 copy.81
  136.1 0.1 copy.88
  136.3 1.1 collective-permute-done.2
  137.5 9.0 %shard_map.105 = bf16[8,256,128]{2,1,0:T(8,128)(2,1)S(1)} custom-call(s32[1]{0:T(128)} %bitcast.core_ref, bf16[8,2,8,56,128]{4,3,2,1,0:T(8,128)(2,1)S(1)} %bitcast.70, bf16[8,2,8,16,128]{4,3,2,1,0:T(8,128)(2,1)S(1)} %bitcast.82, f32[8,2,8,8,128]{4,3,2,1,0:T(8,128)S(1)} %convert.2.top_ref, f32[512,1]{1,0:T(8,128)S(1)} %broadcast_multiply_fusion.mask_ref, ...), custom_call_target="tpu_custom_call" | custom-call | flops 3000000000 | bytes 4194304 | tf_op jit(solution)/shard_map/pallas_call | solution.py:357
  146.4 0.6 copy.84
  147.1 13.5 %all_to_all.31 = bf16[16,128,128]{2,1,0:T(8,128)(2,1)S(1)} all-to-all(bf16[16,128,128]{2,1,0:T(8,128)(2,1)S(1)} %bitcast.95), channel_id=1, replica_groups=mesh['xl'=2,'y'=4,'core'=2,'z'=4,'xh'=2] {'xl','y','core'}, dimensions={0} | all-to-all | bytes 1048576 | tf_op jit(solution)/shard_map/all_to_all | solution.py:18
  160.5 1.1 copy.85
  (50 shorter events, 1.5 us)
Async XLA Ops:
  0.0 20.6 %all-to-all-start = ((bf16[16,128,128]{2,1,0:T(8,128)(2,1)}), bf16[16,128,128]{2,1,0:T(8,128)(2,1)S(1)}, u32[]{:S(2)}, u32[]{:S(2)}) async-start(bf16[16,128,128]{2,1,0:T(8,128)(2,1)} %bitcast.73), calls=%async_computation | async-start | bytes 1048576 | tf_op jit(solution)/shard_map/all_to_all | solution.py:18
  11.5 1.0 copy-start
  20.6 6.0 %collective-permute-start = (bf16[8,2,2,32,128]{4,3,2,1,0:T(8,128)(2,1)S(1)}, bf16[8,2,2,32,128]{4,3,2,1,0:T(8,128)(2,1)S(1)}, u32[]{:S(2)}, u32[]{:S(2)}) collective-permute-start(bf16[8,2,2,32,128]{4,3,2,1,0:T(8,128)(2,1)S(1)} %dynamic-slice_bitcast_fusion), channel_id=1, source_target_pairs={{0,8},{8,0},{1,9},{9,1},{2,10},{10,2},{3,11},{11,3},{4,12},{12,4},... | collective-permute-start | bytes 786440 | tf_op jit(solution)/shard_map/ppermute | solution.py:287
  21.9 22.6 %all-to-all-start.1 = ((bf16[128,32,128]{2,1,0:T(8,128)(2,1)}), bf16[128,32,128]{2,1,0:T(8,128)(2,1)S(1)}, u32[]{:S(2)}, u32[]{:S(2)}) async-start(bf16[128,32,128]{2,1,0:T(8,128)(2,1)} %pad_maximum_fusion.1), calls=%async_computation.1 | async-start | bytes 2097152 | tf_op jit(solution)/shard_map/all_to_all | solution.py:18
  46.5 18.3 %all-to-all-start.2 = ((bf16[128,16,128]{2,1,0:T(8,128)(2,1)}), bf16[128,16,128]{2,1,0:T(8,128)(2,1)S(1)}, u32[]{:S(2)}, u32[]{:S(2)}) async-start(bf16[128,16,128]{2,1,0:T(8,128)(2,1)} %bitcast.6), calls=%async_computation.2 | async-start | bytes 1048576 | tf_op jit(solution)/shard_map/all_to_all | solution.py:18
  52.5 12.3 %copy-start.3 = (bf16[128,128]{1,0:T(8,128)(2,1)S(1)}, bf16[128,128]{1,0:T(8,128)(2,1)}, u32[]{:S(2)}) copy-start(bf16[128,128]{1,0:T(8,128)(2,1)} %w_ref.1) | copy-start | bytes 98308
  64.8 3.9 %copy-start.8 = (s32[512]{0:T(512)S(1)}, s32[512]{0:T(512)}, u32[]{:S(2)}) copy-start(s32[512]{0:T(512)} %param.11) | copy-start | bytes 6148
  64.8 4.8 %copy-start.9 = (bf16[128,4]{0,1:T(4,128)(2,1)S(1)}, bf16[128,4]{0,1:T(4,128)(2,1)}, u32[]{:S(2)}) copy-start(bf16[128,4]{0,1:T(4,128)(2,1)} %param.15) | copy-start | bytes 3076
  66.4 0.8 copy-start.6
  67.2 3.1 %collective-permute-start.1 = (bf16[16,128,128]{2,1,0:T(8,128)(2,1)S(1)}, bf16[16,128,128]{2,1,0:T(8,128)(2,1)S(1)}, u32[]{:S(2)}, u32[]{:S(2)}) collective-permute-start(bf16[16,128,128]{2,1,0:T(8,128)(2,1)S(1)} %get-tuple-element.17), channel_id=1, source_target_pairs={{0,8},{8,0},{1,9},{9,1},{2,10},{10,2},{3,11},{11,3},{4,12},{12,4},... | collective-permute-start | bytes 1572872 | tf_op jit(solution)/shard_map/ppermute | solution.py:310
  71.8 4.2 %copy-start.10 = (bf16[128,4]{0,1:T(4,128)(2,1)S(1)}, bf16[128,4]{0,1:T(4,128)(2,1)}, u32[]{:S(2)}) copy-start(bf16[128,4]{0,1:T(4,128)(2,1)} %param.18) | copy-start | bytes 3076
  71.8 21.9 %copy-start.2 = (bf16[128,512]{1,0:T(8,128)(2,1)S(1)}, bf16[128,512]{1,0:T(8,128)(2,1)}, u32[]{:S(2)}) copy-start(bf16[128,512]{1,0:T(8,128)(2,1)} %w_in_ref.2) | copy-start | bytes 393220
  71.8 21.9 %copy-start.4 = (bf16[128,128]{1,0:T(8,128)(2,1)S(1)}, bf16[128,128]{1,0:T(8,128)(2,1)}, u32[]{:S(2)}) copy-start(bf16[128,128]{1,0:T(8,128)(2,1)} %w_out_ref.2) | copy-start | bytes 98308
  71.8 21.9 %copy-start.7 = (bf16[16,128,128]{2,1,0:T(8,128)(2,1)S(1)}, bf16[16,128,128]{2,1,0:T(8,128)(2,1)}, u32[]{:S(2)}) copy-start(bf16[16,128,128]{2,1,0:T(8,128)(2,1)} %copy-done.6) | copy-start | bytes 1572868
  71.8 21.9 %all-to-all-start.3 = ((bf16[128,32,128]{2,1,0:T(8,128)(2,1)}), bf16[128,32,128]{2,1,0:T(8,128)(2,1)S(1)}, u32[]{:S(2)}, u32[]{:S(2)}) async-start(bf16[128,32,128]{2,1,0:T(8,128)(2,1)} %bitcast.19), calls=%async_computation.3 | async-start | bytes 2097152 | tf_op jit(solution)/shard_map/all_to_all | solution.py:18
  102.6 33.5 %slice-start = ((bf16[128,512]{1,0:T(8,128)(2,1)}), bf16[128,256]{1,0:T(8,128)(2,1)S(1)}, s32[]{:S(2)}) async-start(bf16[128,512]{1,0:T(8,128)(2,1)} %w_in_ref.3), calls=%async_computation.6 | async-start | bytes 131072 | tf_op jit(solution)/shard_map/slice | solution.py:370
  133.8 3.7 %copy-start.1 = (bf16[128,512]{1,0:T(8,128)(2,1)S(1)}, bf16[128,512]{1,0:T(8,128)(2,1)}, u32[]{:S(2)}) copy-start(bf16[128,512]{1,0:T(8,128)(2,1)} %w_in_ref.3) | copy-start | bytes 393220
  133.8 3.7 %copy-start.5 = (bf16[128,128]{1,0:T(8,128)(2,1)S(1)}, bf16[128,128]{1,0:T(8,128)(2,1)}, u32[]{:S(2)}) copy-start(bf16[128,128]{1,0:T(8,128)(2,1)} %w_out_ref.3) | copy-start | bytes 98308
  133.8 3.6 %collective-permute-start.2 = (bf16[128,16,128]{2,1,0:T(8,128)(2,1)S(1)}, bf16[128,16,128]{2,1,0:T(8,128)(2,1)S(1)}, u32[]{:S(2)}, u32[]{:S(2)}) collective-permute-start(bf16[128,16,128]{2,1,0:T(8,128)(2,1)S(1)} %slice.20), channel_id=1, source_target_pairs={{0,8},{8,0},{1,9},{9,1},{2,10},{10,2},{3,11},{11,3},{4,12},{12,4},... | collective-permute-start | bytes 1572872 | tf_op jit(solution)/shard_map/ppermute | solution.py:352
